TPU v7x, 128 devices: a whole 4x4x4 slice. The times are simulated.
128 devices in a mesh: set: 2 (over z_lo), tx: 16 (over x, y), ty: 4 (over z_hi, core).
Axes of the slice: x: 4, y: 4, z: 4 (z_hi: 2, z_lo: 2; z = z_hi * 2 + z_lo), core: 2. Of those that a mesh axis runs over, the one named last changes fastest.
Arguments:
- tracers: float32 [32, 16, 64, 4096], P('set', None, 'ty', 'tx'), may hold values from 0 to 2
- thickness: float32 [16, 64, 4096], P('set', 'ty', 'tx'), may hold values from 0.6 to 1.4
- velocity: float32 [2, 16, 64, 4096], P(None, 'set', 'ty', 'tx'), may hold values from -0.5 to 0.5
- diffusivity: float32 [16, 64, 4096], P(None, 'ty', 'tx'), may hold values from 0.05 to 5
- reaction: float32 [4, 8, 8], P('set'), may hold values from -2 to 2
- land_mask: int32 [64, 4096], P('ty', 'tx'), may hold values 0 or 1
- level_count: int32 [64, 4096], P('ty', 'tx'), may hold values from 1 to 16
Outputs:
- tracers_out: float32 [32, 16, 64, 4096], P('set', None, 'ty', 'tx')
- thickness_out: float32 [16, 64, 4096], P('set', 'ty', 'tx')
- velocity_out: float32 [2, 16, 64, 4096], P(None, 'set', 'ty', 'tx')
All inputs are finite; a program needn't handle non-finite values. No bound on the sum of `land_mask` on one device may be relied on, other than what follows from the above.
Results may differ from a plain program's by a relative error of at most 0.00025.
Values sent between devices are 32-bit elements; how exact they have to be, the bound alone decides.
No kernel may reach another device: no remote copies, remote signals or barrier semaphores. Data moves between devices by JAX's collectives and lax.ppermute only.
A program may use at most 128 MiB of HBM per device.

v0:
```python
import jax
import jax.numpy as jnp
from jax import lax
from jax.sharding import PartitionSpec as P

ITERS = 4


TIME_STEP = 0.2
GRAVITY = 1.0
ROTATION = 0.5


def extended(shard, sides, width, wrap):
    for axis, dim in sides:
        count, length = (lax.axis_size(axis), shard.shape[dim])
        up = [(i, (i + 1) % count) for i in range(count if wrap else count - 1)]
        down = [(j, i) for i, j in up]
        last = lax.slice_in_dim(shard, length - width, length, axis=dim)
        first = lax.slice_in_dim(shard, 0, width, axis=dim)
        before = lax.ppermute(last, axis, up)
        after = lax.ppermute(first, axis, down)
        shard = jnp.concatenate([before, shard, after], axis=dim)
    return shard


def with_rims(field):
    zonal = extended(field, (("tx", 3),), 1, True)
    return extended(zonal, (("ty", 2),), 1, False)


def tracer_rims(field):
    zonal = extended(field, (("tx", 3),), 1, True)
    return extended(zonal, (("ty", 2),), 1, False)


def divergence(flux_pad):
    zonal = flux_pad[0, :, 1:-1, 1:-1] - flux_pad[0, :, 1:-1, :-2]
    meridional = flux_pad[1, :, 1:-1, 1:-1] - flux_pad[1, :, :-2, 1:-1]
    return zonal + meridional


def momentum_fluxes(thick_pad, velocity, mask_pad, coriolis):
    center = thick_pad[:, 1:-1, 1:-1]
    east_side = thick_pad[:, 1:-1, 2:]
    north_side = thick_pad[:, 2:, 1:-1]
    wet_here = mask_pad[:, 1:-1, 1:-1]
    east_wet = wet_here * mask_pad[:, 1:-1, 2:]
    north_wet = wet_here * mask_pad[:, 2:, 1:-1]
    eastward = east_wet * (
        velocity[0] + TIME_STEP * (coriolis * velocity[1] - GRAVITY * (east_side - center))
    )
    northward = north_wet * (
        velocity[1] - TIME_STEP * (coriolis * velocity[0] + GRAVITY * (north_side - center))
    )
    fluxes = jnp.stack(
        [eastward * 0.5 * (center + east_side), northward * 0.5 * (center + north_side)]
    )
    return (jnp.stack([eastward, northward]), fluxes)


def column_mix(content, thick_new, link):
    levels = content.shape[1]
    upper_link = jnp.zeros_like(link[0])
    prev_ratio = jnp.zeros_like(link[0])
    prev_solved = jnp.zeros_like(content[:, 0])
    ratios = []
    solved = []
    for level in range(levels):
        below = link[level]
        recip = 1.0 / (thick_new[level] + upper_link + below - upper_link * prev_ratio)
        prev_ratio = below * recip
        prev_solved = (content[:, level] + upper_link * prev_solved) * recip
        ratios.append(prev_ratio)
        solved.append(prev_solved)
        upper_link = below
    result = [None] * levels
    result[levels - 1] = solved[levels - 1]
    for level in range(levels - 2, -1, -1):
        result[level] = solved[level] + ratios[level] * result[level + 1]
    return jnp.stack(result, axis=1)


def tracer_update(conc_pad, flux_pad, thickness, mask_pad, diffusivity, reaction):
    east_flux = flux_pad[0, :, 1:-1, 1:-1]
    west_flux = flux_pad[0, :, 1:-1, :-2]
    north_flux = flux_pad[1, :, 1:-1, 1:-1]
    south_flux = flux_pad[1, :, :-2, 1:-1]
    center = conc_pad[..., 1:-1, 1:-1]
    east_conc = conc_pad[..., 1:-1, 2:]
    west_conc = conc_pad[..., 1:-1, :-2]
    north_conc = conc_pad[..., 2:, 1:-1]
    south_conc = conc_pad[..., :-2, 1:-1]
    flux_east = jnp.maximum(east_flux, 0.0) * center + jnp.minimum(east_flux, 0.0) * east_conc
    flux_west = jnp.maximum(west_flux, 0.0) * west_conc + jnp.minimum(west_flux, 0.0) * center
    flux_north = jnp.maximum(north_flux, 0.0) * center + jnp.minimum(north_flux, 0.0) * north_conc
    flux_south = jnp.maximum(south_flux, 0.0) * south_conc + jnp.minimum(south_flux, 0.0) * center
    thick_new = thickness - TIME_STEP * divergence(flux_pad)
    content = thickness * center - TIME_STEP * (flux_east - flux_west + (flux_north - flux_south))
    wet_here = mask_pad[:, 1:-1, 1:-1]
    wet_below = jnp.concatenate([wet_here[1:], jnp.zeros_like(wet_here[:1])], axis=0)
    link = TIME_STEP * diffusivity * wet_here * wet_below
    mixed = column_mix(content, thick_new, link)
    groups = reaction.shape[0]
    per_group = reaction.shape[1]
    shaped = mixed.reshape((groups, per_group) + mixed.shape[1:])
    reacted = shaped + TIME_STEP * jnp.einsum(
        "sab,sbzyx->sazyx", reaction, shaped, precision=lax.Precision.HIGHEST
    )
    return reacted.reshape(mixed.shape) * wet_here


def body(tracers, thickness, velocity, diffusivity, reaction, land_mask, level_count):
    levels_all = diffusivity.shape[0]
    own_levels = thickness.shape[0]
    rows_local = thickness.shape[1]
    offset = lax.axis_index("set") * own_levels
    level_index = jnp.arange(levels_all, dtype=jnp.int32)[:, None, None]
    wet_cells = ((level_index < level_count[None]) & (land_mask[None] == 1)).astype(jnp.float32)
    row_start = lax.axis_index("ty") * rows_local
    rows_total = rows_local * lax.axis_size("ty")
    mask_pad = with_rims(wet_cells[None])[0]
    row_index = row_start + jnp.arange(rows_local, dtype=jnp.int32)
    coriolis = (ROTATION * (2.0 * (row_index.astype(jnp.float32) + 0.5) / rows_total - 1.0))[
        :, None
    ]
    concentration = tracers
    own_mask = lax.dynamic_slice_in_dim(mask_pad, offset, own_levels, 0)
    thick_now = thickness
    veloc_now = velocity
    for iteration in range(ITERS):
        thick_pad = with_rims(thick_now[None])[0]
        veloc_next, fluxes = momentum_fluxes(thick_pad, veloc_now, own_mask, coriolis)
        veloc_next, flux_pad = (veloc_next, with_rims(fluxes))
        flux_all, thick_all = (
            lax.all_gather(flux_pad, "set", axis=1, tiled=True),
            lax.all_gather(thick_now, "set", axis=0, tiled=True),
        )
        concentration = tracer_update(
            tracer_rims(concentration), flux_all, thick_all, mask_pad, diffusivity, reaction
        )
        thick_now = thick_now - TIME_STEP * divergence(flux_pad)
        veloc_now = veloc_next
    return (concentration, thick_now, veloc_now)


def solution(mesh):
    placed = (
        P("set", None, "ty", "tx"),
        P("set", "ty", "tx"),
        P(None, "set", "ty", "tx"),
        P(None, "ty", "tx"),
        P("set", None, None),
        P("ty", "tx"),
        P("ty", "tx"),
    )
    return jax.shard_map(
        body,
        mesh=mesh,
        in_specs=placed,
        out_specs=(P("set", None, "ty", "tx"), P("set", "ty", "tx"), P(None, "set", "ty", "tx")),
        check_vma=False,
    )
```

profile of v0, /device:TPU:1, one launch (start us, length us, event | category | flops | bytes accessed | tf_op | source)
XLA Modules:
  0.0 505.8 jit_solution(16782649315254134235)
XLA Ops:
  2.2 5.8 %collective-permute-start.1 = (f32[1,16,16,1]{3,2,1,0:T(8,128)S(1)}, f32[1,16,16,1]{3,2,1,0:T(8,128)S(1)}, u32[]{:S(2)}, u32[]{:S(2)}) collective-permute-start(f32[1,16,16,1]{3,2,1,0:T(8,128)S(1)} %get-tuple-element.378), channel_id=1, source_target_pairs={{4,0},{8,4},{12,8},{16,12},{20,16},{24,20},{28,24},{32,28},{36,32}... | collective-permute-start | bytes 3080 | tf_op jit(solution)/shard_map/ppermute | solution.py:22
  8.1 4.3 fusion.447
  12.4 3.8 copy.199
  16.2 4.7 collective-permute-start.26
  23.1 4.8 copy.93
  27.9 4.6 all_gather.27
  35.0 5.0 collective-permute-start.7
  40.0 5.4 %collective-permute-start.6 = (f32[1,8,1,258]{3,2,1,0:T(1,128)S(1)}, f32[1,8,1,258]{3,2,1,0:T(1,128)S(1)}, u32[]{:S(2)}, u32[]{:S(2)}) collective-permute-start(f32[1,8,1,258]{3,2,1,0:T(1,128)S(1)} %get-tuple-element.379), channel_id=1, source_target_pairs={{0,1},{1,2},{2,3},{4,5},{5,6},{6,7},{8,9},{9,10},{10,11},{12,13},{... | collective-permute-start | bytes 24776 | tf_op jit(solution)/shard_map/ppermute | solution.py:21
  47.6 5.1 %collective-permute-start.2 = (f32[1,16,1,258]{3,2,1,0:T(1,128)S(1)}, f32[1,16,1,258]{3,2,1,0:T(1,128)S(1)}, u32[]{:S(2)}, u32[]{:S(2)}) collective-permute-start(f32[1,16,1,258]{3,2,1,0:T(1,128)S(1)} %get-tuple-element.312), channel_id=1, source_target_pairs={{0,1},{1,2},{2,3},{4,5},{5,6},{6,7},{8,9},{9,10},{10,11},{12,13},{... | collective-permute-start | bytes 49544 | tf_op jit(solution)/shard_map/ppermute | solution.py:21
  55.4 3.8 copy.99
  61.0 5.1 %collective-permute-start.9 = (f32[2,8,16,1]{3,2,1,0:T(8,128)S(1)}, f32[2,8,16,1]{3,2,1,0:T(8,128)S(1)}, u32[]{:S(2)}, u32[]{:S(2)}) collective-permute-start(f32[2,8,16,1]{3,2,1,0:T(8,128)S(1)} %get-tuple-element.376), channel_id=1, source_target_pairs={{4,0},{8,4},{12,8},{16,12},{20,16},{24,20},{28,24},{32,28},{36,32}... | collective-permute-start | bytes 3080 | tf_op jit(solution)/shard_map/ppermute | solution.py:22
  66.1 3.8 pad_maximum_fusion.48
  74.7 4.9 collective-permute-start.10
  82.0 5.5 %collective-permute-start.12 = (f32[1,8,16,1]{3,2,1,0:T(8,128)S(1)}, f32[1,8,16,1]{3,2,1,0:T(8,128)S(1)}, u32[]{:S(2)}, u32[]{:S(2)}) collective-permute-start(f32[1,8,16,1]{3,2,1,0:T(8,128)S(1)} %get-tuple-element.386), channel_id=1, source_target_pairs={{4,0},{8,4},{12,8},{16,12},{20,16},{24,20},{28,24},{32,28},{36,32}... | collective-permute-start | bytes 1544 | tf_op jit(solution)/shard_map/ppermute | solution.py:22
  87.9 13.1 %all_gather.28 = f32[2,16,18,258]{3,2,1,0:T(8,128)S(1)} all-gather(f32[2,8,18,258]{3,2,1,0:T(8,128)S(1)} %pad_maximum_fusion.33), channel_id=1, replica_groups=mesh['set'=2,'tx'=16,'ty'=4] {'set'}, dimensions={1}, use_global_device_ids=true | all-gather | bytes 891648 | tf_op jit(solution)/shard_map/all_gather | solution.py:136
  103.1 5.2 %collective-permute-start.13 = (f32[1,8,1,258]{3,2,1,0:T(1,128)S(1)}, f32[1,8,1,258]{3,2,1,0:T(1,128)S(1)}, u32[]{:S(2)}, u32[]{:S(2)}) collective-permute-start(f32[1,8,1,258]{3,2,1,0:T(1,128)S(1)} %get-tuple-element.373), channel_id=1, source_target_pairs={{0,1},{1,2},{2,3},{4,5},{5,6},{6,7},{8,9},{9,10},{10,11},{12,13},{... | collective-permute-start | bytes 24776 | tf_op jit(solution)/shard_map/ppermute | solution.py:21
  110.4 5.1 %collective-permute-start.16 = (f32[2,8,16,1]{3,2,1,0:T(8,128)S(1)}, f32[2,8,16,1]{3,2,1,0:T(8,128)S(1)}, u32[]{:S(2)}, u32[]{:S(2)}) collective-permute-start(f32[2,8,16,1]{3,2,1,0:T(8,128)S(1)} %get-tuple-element.372), channel_id=1, source_target_pairs={{4,0},{8,4},{12,8},{16,12},{20,16},{24,20},{28,24},{32,28},{36,32}... | collective-permute-start | bytes 3080 | tf_op jit(solution)/shard_map/ppermute | solution.py:22
  117.4 5.2 %collective-permute-done.15 = f32[2,8,16,1]{3,2,1,0:T(8,128)S(1)} collective-permute-done((f32[2,8,16,1]{3,2,1,0:T(8,128)S(1)}, f32[2,8,16,1]{3,2,1,0:T(8,128)S(1)}, u32[]{:S(2)}, u32[]{:S(2)}) %collective-permute-start.15) | collective-permute-done | bytes 1056 | tf_op jit(solution)/shard_map/ppermute | solution.py:21
  122.8 6.3 %collective-permute-start.17 = (f32[2,8,1,258]{3,2,1,0:T(1,128)S(1)}, f32[2,8,1,258]{3,2,1,0:T(1,128)S(1)}, u32[]{:S(2)}, u32[]{:S(2)}) collective-permute-start(f32[2,8,1,258]{3,2,1,0:T(1,128)S(1)} %get-tuple-element.305), channel_id=1, source_target_pairs={{0,1},{1,2},{2,3},{4,5},{5,6},{6,7},{8,9},{9,10},{10,11},{12,13},{... | collective-permute-start | bytes 49544 | tf_op jit(solution)/shard_map/ppermute | solution.py:21
  129.1 4.5 all_gather.26
  144.5 6.3 %collective-permute-start.20 = (f32[1,8,1,258]{3,2,1,0:T(1,128)S(1)}, f32[1,8,1,258]{3,2,1,0:T(1,128)S(1)}, u32[]{:S(2)}, u32[]{:S(2)}) collective-permute-start(f32[1,8,1,258]{3,2,1,0:T(1,128)S(1)} %get-tuple-element.363), channel_id=1, source_target_pairs={{0,1},{1,2},{2,3},{4,5},{5,6},{6,7},{8,9},{9,10},{10,11},{12,13},{... | collective-permute-start | bytes 24776 | tf_op jit(solution)/shard_map/ppermute | solution.py:21
  150.8 12.4 %all_gather.29 = f32[2,16,18,258]{3,2,1,0:T(8,128)S(1)} all-gather(f32[2,8,18,258]{3,2,1,0:T(8,128)S(1)} %pad_maximum_fusion.34), channel_id=1, replica_groups=mesh['set'=2,'tx'=16,'ty'=4] {'set'}, dimensions={1}, use_global_device_ids=true | all-gather | bytes 891648 | tf_op jit(solution)/shard_map/all_gather | solution.py:136
  171.2 6.4 %collective-permute-start.24 = (f32[2,8,1,258]{3,2,1,0:T(1,128)S(1)}, f32[2,8,1,258]{3,2,1,0:T(1,128)S(1)}, u32[]{:S(2)}, u32[]{:S(2)}) collective-permute-start(f32[2,8,1,258]{3,2,1,0:T(1,128)S(1)} %get-tuple-element.300), channel_id=1, source_target_pairs={{0,1},{1,2},{2,3},{4,5},{5,6},{6,7},{8,9},{9,10},{10,11},{12,13},{... | collective-permute-start | bytes 49544 | tf_op jit(solution)/shard_map/ppermute | solution.py:21
  177.6 4.5 all_gather.25
  193.0 6.3 %collective-permute-start.42 = (f32[1,8,1,258]{3,2,1,0:T(1,128)S(1)}, f32[1,8,1,258]{3,2,1,0:T(1,128)S(1)}, u32[]{:S(2)}, u32[]{:S(2)}) collective-permute-start(f32[1,8,1,258]{3,2,1,0:T(1,128)S(1)} %get-tuple-element.347), channel_id=1, source_target_pairs={{0,1},{1,2},{2,3},{4,5},{5,6},{6,7},{8,9},{9,10},{10,11},{12,13},{... | collective-permute-start | bytes 24776 | tf_op jit(solution)/shard_map/ppermute | solution.py:21
  199.3 12.4 %all_gather.30 = f32[2,16,18,258]{3,2,1,0:T(8,128)S(1)} all-gather(f32[2,8,18,258]{3,2,1,0:T(8,128)S(1)} %pad_maximum_fusion.35), channel_id=1, replica_groups=mesh['set'=2,'tx'=16,'ty'=4] {'set'}, dimensions={1}, use_global_device_ids=true | all-gather | bytes 891648 | tf_op jit(solution)/shard_map/all_gather | solution.py:136
  222.5 6.4 %collective-permute-start.46 = (f32[2,8,1,258]{3,2,1,0:T(1,128)S(1)}, f32[2,8,1,258]{3,2,1,0:T(1,128)S(1)}, u32[]{:S(2)}, u32[]{:S(2)}) collective-permute-start(f32[2,8,1,258]{3,2,1,0:T(1,128)S(1)} %get-tuple-element.295), channel_id=1, source_target_pairs={{0,1},{1,2},{2,3},{4,5},{5,6},{6,7},{8,9},{9,10},{10,11},{12,13},{... | collective-permute-start | bytes 49544 | tf_op jit(solution)/shard_map/ppermute | solution.py:21
  228.9 4.5 all_gather.24
  233.7 13.5 %all_gather.31 = f32[2,16,18,258]{3,2,1,0:T(8,128)S(1)} all-gather(f32[2,8,18,258]{3,2,1,0:T(8,128)S(1)} %pad_maximum_fusion.36), channel_id=1, replica_groups=mesh['set'=2,'tx'=16,'ty'=4] {'set'}, dimensions={1}, use_global_device_ids=true | all-gather | bytes 891648 | tf_op jit(solution)/shard_map/all_gather | solution.py:136
  275.6 17.6 %fusion.44 = f32[16,16,16,256]{3,2,0,1:T(8,128)S(1)} fusion(f32[16,16,1,258]{3,2,0,1:T(1,128)} %copy-done.71, f32[16,16,16,1]{3,2,0,1:T(8,128)S(1)} %copy.97, f32[16,16,16,256]{3,2,0,1:T(8,128)} %copy.93, f32[16,16,16,1]{3,2,0,1:T(8,128)} %copy.99, f32[16,16,1,258]{3,2,0,1:T(1,128)} %copy-done.72, f32[16,16,256]{2,1,0:T(8,128)} %get-tuple-element.275, ...), kind=kLoop, calls=%fused_computation.69 | loop fusion | flops 27262976 | bytes 11309056 | tf_op jit(solution)/shard_map/sub | solution.py:99
  298.8 4.4 bitcast_add_fusion.3
  308.2 3.8 copy.125
  322.4 3.8 copy.128
  326.2 5.2 %pad_maximum_fusion.45 = (f32[16,16,1,258]{3,2,0,1:T(1,128)S(1)}, f32[16,16,1,258]{3,2,0,1:T(1,128)S(1)}) fusion(f32[16,16,16,1]{3,2,0,1:T(8,128)S(1)} %copy.126, f32[16,16,16,256]{3,2,0,1:T(8,128)} %copy-done.5, f32[16,16,16,1]{3,2,0,1:T(8,128)} %copy.128), kind=kLoop, calls=%fused_computation.105 | loop fusion | flops 264192 | bytes 4755456 | tf_op jit(solution)/shard_map/slice | solution.py:20
  331.4 5.3 %collective-permute-start.34 = (f32[16,16,1,258]{3,2,0,1:T(1,128)S(1)}, f32[16,16,1,258]{3,2,0,1:T(1,128)S(1)}, u32[]{:S(2)}, u32[]{:S(2)}) collective-permute-start(f32[16,16,1,258]{3,2,0,1:T(1,128)S(1)} %get-tuple-element.236), channel_id=1, source_target_pairs={{0,1},{1,2},{2,3},{4,5},{5,6},{6,7},{8,9},{9,10},{10,11},{12,13},{... | collective-permute-start | bytes 792584 | tf_op jit(solution)/shard_map/ppermute | solution.py:21
  341.3 5.9 %collective-permute-done.33 = f32[16,16,1,258]{3,2,0,1:T(1,128)S(1)} collective-permute-done((f32[16,16,1,258]{3,2,0,1:T(1,128)S(1)}, f32[16,16,1,258]{3,2,0,1:T(1,128)S(1)}, u32[]{:S(2)}, u32[]{:S(2)}) %collective-permute-start.33) | collective-permute-done | bytes 264224 | tf_op jit(solution)/shard_map/ppermute | solution.py:22
  348.0 11.2 %fusion.31 = f32[16,16,16,256]{3,2,0,1:T(8,128)} fusion(f32[16,16,1,258]{3,2,0,1:T(1,128)} %copy-done.74, f32[16,16,16,1]{3,2,0,1:T(8,128)S(1)} %copy.126, f32[16,16,16,256]{3,2,0,1:T(8,128)S(1)} %copy-done.6, f32[16,16,16,1]{3,2,0,1:T(8,128)} %copy.128, f32[16,16,1,258]{3,2,0,1:T(1,128)} %copy-done.77, f32[16,16,256]{2,1,0:T(8,128)} %get-tuple-element.267, ...), kind=kLoop, calls=%fused_computation.48 | loop fusion | flops 27262976 | bytes 11309056 | tf_op jit(solution)/shard_map/sub | solution.py:99
  366.2 4.4 bitcast_add_fusion.2
  375.8 3.8 copy.149
  393.0 5.2 %pad_maximum_fusion.42 = (f32[16,16,1,258]{3,2,0,1:T(1,128)S(1)}, f32[16,16,1,258]{3,2,0,1:T(1,128)S(1)}) fusion(f32[16,16,16,1]{3,2,0,1:T(8,128)S(1)} %copy.150, f32[16,16,16,256]{3,2,0,1:T(8,128)} %copy-done.3, f32[16,16,16,1]{3,2,0,1:T(8,128)} %copy.152), kind=kLoop, calls=%fused_computation.102 | loop fusion | flops 264192 | bytes 4755456 | tf_op jit(solution)/shard_map/slice | solution.py:20
  406.0 5.9 %collective-permute-done.38 = f32[16,16,1,258]{3,2,0,1:T(1,128)S(1)} collective-permute-done((f32[16,16,1,258]{3,2,0,1:T(1,128)S(1)}, f32[16,16,1,258]{3,2,0,1:T(1,128)S(1)}, u32[]{:S(2)}, u32[]{:S(2)}) %collective-permute-start.38) | collective-permute-done | bytes 264224 | tf_op jit(solution)/shard_map/ppermute | solution.py:22
  412.7 10.9 %fusion.18 = f32[16,16,16,256]{3,2,0,1:T(8,128)} fusion(f32[16,16,1,258]{3,2,0,1:T(1,128)} %copy-done.73, f32[16,16,16,1]{3,2,0,1:T(8,128)S(1)} %copy.150, f32[16,16,16,256]{3,2,0,1:T(8,128)S(1)} %copy-done.4, f32[16,16,16,1]{3,2,0,1:T(8,128)} %copy.152, f32[16,16,1,258]{3,2,0,1:T(1,128)} %copy-done.76, f32[16,16,256]{2,1,0:T(8,128)} %get-tuple-element.259, ...), kind=kLoop, calls=%fused_computation.27 | loop fusion | flops 27262976 | bytes 11309056 | tf_op jit(solution)/shard_map/sub | solution.py:99
  430.7 4.4 bitcast_add_fusion.1
  440.5 3.8 copy.173
  457.7 5.2 %pad_maximum_fusion.39 = (f32[16,16,1,258]{3,2,0,1:T(1,128)S(1)}, f32[16,16,1,258]{3,2,0,1:T(1,128)S(1)}) fusion(f32[16,16,16,1]{3,2,0,1:T(8,128)S(1)} %copy.174, f32[16,16,16,256]{3,2,0,1:T(8,128)} %copy-done.1, f32[16,16,16,1]{3,2,0,1:T(8,128)} %copy.176), kind=kLoop, calls=%fused_computation.99 | loop fusion | flops 264192 | bytes 4755456 | tf_op jit(solution)/shard_map/slice | solution.py:20
  470.7 5.9 %collective-permute-done.50 = f32[16,16,1,258]{3,2,0,1:T(1,128)S(1)} collective-permute-done((f32[16,16,1,258]{3,2,0,1:T(1,128)S(1)}, f32[16,16,1,258]{3,2,0,1:T(1,128)S(1)}, u32[]{:S(2)}, u32[]{:S(2)}) %collective-permute-start.50) | collective-permute-done | bytes 264224 | tf_op jit(solution)/shard_map/ppermute | solution.py:22
  477.7 10.9 %fusion.5 = f32[16,16,16,256]{3,2,0,1:T(8,128)} fusion(f32[16,16,1,258]{3,2,0,1:T(1,128)} %copy-done.75, f32[16,16,16,1]{3,2,0,1:T(8,128)S(1)} %copy.174, f32[16,16,16,256]{3,2,0,1:T(8,128)S(1)} %copy-done.2, f32[16,16,16,1]{3,2,0,1:T(8,128)} %copy.176, f32[16,16,1,258]{3,2,0,1:T(1,128)} %copy-done.78, f32[16,16,256]{2,1,0:T(8,128)} %get-tuple-element.251, ...), kind=kLoop, calls=%fused_computation.6 | loop fusion | flops 27262976 | bytes 11309056 | tf_op jit(solution)/shard_map/sub | solution.py:99
  496.3 4.4 bitcast_add_fusion
  (737 shorter events, 200.4 us)
Async XLA Ops:
  2.2 37.7 %collective-permute-start.1 = (f32[1,16,16,1]{3,2,1,0:T(8,128)S(1)}, f32[1,16,16,1]{3,2,1,0:T(8,128)S(1)}, u32[]{:S(2)}, u32[]{:S(2)}) collective-permute-start(f32[1,16,16,1]{3,2,1,0:T(8,128)S(1)} %get-tuple-element.378), channel_id=1, source_target_pairs={{4,0},{8,4},{12,8},{16,12},{20,16},{24,20},{28,24},{32,28},{36,32}... | collective-permute-start | bytes 3080 | tf_op jit(solution)/shard_map/ppermute | solution.py:22
  8.1 37.3 %collective-permute-start = (f32[1,16,16,1]{3,2,1,0:T(8,128)S(1)}, f32[1,16,16,1]{3,2,1,0:T(8,128)S(1)}, u32[]{:S(2)}, u32[]{:S(2)}) collective-permute-start(f32[1,16,16,1]{3,2,1,0:T(8,128)S(1)} %get-tuple-element.377), channel_id=1, source_target_pairs={{0,4},{4,8},{8,12},{12,16},{16,20},{20,24},{24,28},{28,32},{32,36}... | collective-permute-start | bytes 3080 | tf_op jit(solution)/shard_map/ppermute | solution.py:21
  16.2 36.7 %collective-permute-start.26 = (f32[16,16,16,1]{2,1,3,0:T(8,128)}, f32[16,16,16,1]{2,1,3,0:T(8,128)}, u32[]{:S(2)}, u32[]{:S(2)}) collective-permute-start(f32[16,16,16,1]{2,1,3,0:T(8,128)} %copy.199), channel_id=1, source_target_pairs={{4,0},{8,4},{12,8},{16,12},{20,16},{24,20},{28,24},{32,28},{36,32}... | collective-permute-start | bytes 49160 | tf_op jit(solution)/shard_map/ppermute | solution.py:22
  21.6 13.2 %collective-permute-start.5 = (f32[1,8,16,1]{3,2,1,0:T(8,128)}, f32[1,8,16,1]{3,2,1,0:T(8,128)S(1)}, u32[]{:S(2)}, u32[]{:S(2)}) collective-permute-start(f32[1,8,16,1]{3,2,1,0:T(8,128)} %get-tuple-element.388), channel_id=1, source_target_pairs={{4,0},{8,4},{12,8},{16,12},{20,16},{24,20},{28,24},{32,28},{36,32}... | collective-permute-start | bytes 1544 | tf_op jit(solution)/shard_map/ppermute | solution.py:22
  21.6 13.3 %collective-permute-start.4 = (f32[1,8,16,1]{3,2,1,0:T(8,128)S(1)}, f32[1,8,16,1]{3,2,1,0:T(8,128)S(1)}, u32[]{:S(2)}, u32[]{:S(2)}) collective-permute-start(f32[1,8,16,1]{3,2,1,0:T(8,128)S(1)} %get-tuple-element.387), channel_id=1, source_target_pairs={{0,4},{4,8},{8,12},{12,16},{16,20},{20,24},{24,28},{28,32},{32,36}... | collective-permute-start | bytes 1544 | tf_op jit(solution)/shard_map/ppermute | solution.py:21
  34.8 20.6 %collective-permute-start.27 = (f32[16,16,16,1]{2,1,3,0:T(8,128)}, f32[16,16,16,1]{2,1,3,0:T(8,128)}, u32[]{:S(2)}, u32[]{:S(2)}) collective-permute-start(f32[16,16,16,1]{2,1,3,0:T(8,128)} %copy.200), channel_id=1, source_target_pairs={{0,4},{4,8},{8,12},{12,16},{16,20},{20,24},{24,28},{28,32},{32,36}... | collective-permute-start | bytes 49160 | tf_op jit(solution)/shard_map/ppermute | solution.py:21
  35.0 12.6 %collective-permute-start.7 = (f32[1,8,1,258]{3,2,1,0:T(1,128)S(1)}, f32[1,8,1,258]{3,2,1,0:T(1,128)S(1)}, u32[]{:S(2)}, u32[]{:S(2)}) collective-permute-start(f32[1,8,1,258]{3,2,1,0:T(1,128)S(1)} %get-tuple-element.380), channel_id=1, source_target_pairs={{1,0},{2,1},{3,2},{5,4},{6,5},{7,6},{9,8},{10,9},{11,10},{13,12},{... | collective-permute-start | bytes 24776 | tf_op jit(solution)/shard_map/ppermute | solution.py:22
  40.0 12.7 %collective-permute-start.6 = (f32[1,8,1,258]{3,2,1,0:T(1,128)S(1)}, f32[1,8,1,258]{3,2,1,0:T(1,128)S(1)}, u32[]{:S(2)}, u32[]{:S(2)}) collective-permute-start(f32[1,8,1,258]{3,2,1,0:T(1,128)S(1)} %get-tuple-element.379), channel_id=1, source_target_pairs={{0,1},{1,2},{2,3},{4,5},{5,6},{6,7},{8,9},{9,10},{10,11},{12,13},{... | collective-permute-start | bytes 24776 | tf_op jit(solution)/shard_map/ppermute | solution.py:21
  45.6 13.5 %collective-permute-start.3 = (f32[1,16,1,258]{3,2,1,0:T(1,128)S(1)}, f32[1,16,1,258]{3,2,1,0:T(1,128)S(1)}, u32[]{:S(2)}, u32[]{:S(2)}) collective-permute-start(f32[1,16,1,258]{3,2,1,0:T(1,128)S(1)} %get-tuple-element.313), channel_id=1, source_target_pairs={{1,0},{2,1},{3,2},{5,4},{6,5},{7,6},{9,8},{10,9},{11,10},{13,12},{... | collective-permute-start | bytes 49544 | tf_op jit(solution)/shard_map/ppermute | solution.py:22
  47.6 11.6 %collective-permute-start.2 = (f32[1,16,1,258]{3,2,1,0:T(1,128)S(1)}, f32[1,16,1,258]{3,2,1,0:T(1,128)S(1)}, u32[]{:S(2)}, u32[]{:S(2)}) collective-permute-start(f32[1,16,1,258]{3,2,1,0:T(1,128)S(1)} %get-tuple-element.312), channel_id=1, source_target_pairs={{0,1},{1,2},{2,3},{4,5},{5,6},{6,7},{8,9},{9,10},{10,11},{12,13},{... | collective-permute-start | bytes 49544 | tf_op jit(solution)/shard_map/ppermute | solution.py:21
  61.0 13.5 %collective-permute-start.9 = (f32[2,8,16,1]{3,2,1,0:T(8,128)S(1)}, f32[2,8,16,1]{3,2,1,0:T(8,128)S(1)}, u32[]{:S(2)}, u32[]{:S(2)}) collective-permute-start(f32[2,8,16,1]{3,2,1,0:T(8,128)S(1)} %get-tuple-element.376), channel_id=1, source_target_pairs={{4,0},{8,4},{12,8},{16,12},{20,16},{24,20},{28,24},{32,28},{36,32}... | collective-permute-start | bytes 3080 | tf_op jit(solution)/shard_map/ppermute | solution.py:22
  66.1 8.4 %collective-permute-start.8 = (f32[2,8,16,1]{3,2,1,0:T(8,128)S(1)}, f32[2,8,16,1]{3,2,1,0:T(8,128)S(1)}, u32[]{:S(2)}, u32[]{:S(2)}) collective-permute-start(f32[2,8,16,1]{3,2,1,0:T(8,128)S(1)} %get-tuple-element.375), channel_id=1, source_target_pairs={{0,4},{4,8},{8,12},{12,16},{16,20},{20,24},{24,28},{28,32},{32,36}... | collective-permute-start | bytes 3080 | tf_op jit(solution)/shard_map/ppermute | solution.py:21
  70.0 204.8 %collective-permute-start.29 = (f32[16,16,1,258]{3,2,0,1:T(1,128)S(1)}, f32[16,16,1,258]{3,2,0,1:T(1,128)S(1)}, u32[]{:S(2)}, u32[]{:S(2)}) collective-permute-start(f32[16,16,1,258]{3,2,0,1:T(1,128)S(1)} %get-tuple-element.238), channel_id=1, source_target_pairs={{0,1},{1,2},{2,3},{4,5},{5,6},{6,7},{8,9},{9,10},{10,11},{12,13},{... | collective-permute-start | bytes 792584 | tf_op jit(solution)/shard_map/ppermute | solution.py:21
  72.2 202.6 %collective-permute-start.28 = (f32[16,16,1,258]{3,2,0,1:T(1,128)S(1)}, f32[16,16,1,258]{3,2,0,1:T(1,128)S(1)}, u32[]{:S(2)}, u32[]{:S(2)}) collective-permute-start(f32[16,16,1,258]{3,2,0,1:T(1,128)S(1)} %get-tuple-element.237), channel_id=1, source_target_pairs={{1,0},{2,1},{3,2},{5,4},{6,5},{7,6},{9,8},{10,9},{11,10},{13,12},{... | collective-permute-start | bytes 792584 | tf_op jit(solution)/shard_map/ppermute | solution.py:22
  74.7 7.0 %collective-permute-start.10 = (f32[2,8,1,258]{3,2,1,0:T(1,128)S(1)}, f32[2,8,1,258]{3,2,1,0:T(1,128)S(1)}, u32[]{:S(2)}, u32[]{:S(2)}) collective-permute-start(f32[2,8,1,258]{3,2,1,0:T(1,128)S(1)} %get-tuple-element.310), channel_id=1, source_target_pairs={{0,1},{1,2},{2,3},{4,5},{5,6},{6,7},{8,9},{9,10},{10,11},{12,13},{... | collective-permute-start | bytes 49544 | tf_op jit(solution)/shard_map/ppermute | solution.py:21
  79.8 7.8 %collective-permute-start.25 = (f32[2,8,1,258]{3,2,1,0:T(1,128)S(1)}, f32[2,8,1,258]{3,2,1,0:T(1,128)S(1)}, u32[]{:S(2)}, u32[]{:S(2)}) collective-permute-start(f32[2,8,1,258]{3,2,1,0:T(1,128)S(1)} %get-tuple-element.311), channel_id=1, source_target_pairs={{1,0},{2,1},{3,2},{5,4},{6,5},{7,6},{9,8},{10,9},{11,10},{13,12},{... | collective-permute-start | bytes 49544 | tf_op jit(solution)/shard_map/ppermute | solution.py:22
  82.0 18.9 %collective-permute-start.12 = (f32[1,8,16,1]{3,2,1,0:T(8,128)S(1)}, f32[1,8,16,1]{3,2,1,0:T(8,128)S(1)}, u32[]{:S(2)}, u32[]{:S(2)}) collective-permute-start(f32[1,8,16,1]{3,2,1,0:T(8,128)S(1)} %get-tuple-element.386), channel_id=1, source_target_pairs={{4,0},{8,4},{12,8},{16,12},{20,16},{24,20},{28,24},{32,28},{36,32}... | collective-permute-start | bytes 1544 | tf_op jit(solution)/shard_map/ppermute | solution.py:22
  87.6 13.4 %collective-permute-start.11 = (f32[1,8,16,1]{3,2,1,0:T(8,128)S(1)}, f32[1,8,16,1]{3,2,1,0:T(8,128)S(1)}, u32[]{:S(2)}, u32[]{:S(2)}) collective-permute-start(f32[1,8,16,1]{3,2,1,0:T(8,128)S(1)} %get-tuple-element.385), channel_id=1, source_target_pairs={{0,4},{4,8},{8,12},{12,16},{16,20},{20,24},{24,28},{28,32},{32,36}... | collective-permute-start | bytes 1544 | tf_op jit(solution)/shard_map/ppermute | solution.py:21
  101.1 8.8 %collective-permute-start.14 = (f32[1,8,1,258]{3,2,1,0:T(1,128)S(1)}, f32[1,8,1,258]{3,2,1,0:T(1,128)S(1)}, u32[]{:S(2)}, u32[]{:S(2)}) collective-permute-start(f32[1,8,1,258]{3,2,1,0:T(1,128)S(1)} %get-tuple-element.374), channel_id=1, source_target_pairs={{1,0},{2,1},{3,2},{5,4},{6,5},{7,6},{9,8},{10,9},{11,10},{13,12},{... | collective-permute-start | bytes 24776 | tf_op jit(solution)/shard_map/ppermute | solution.py:22
  103.1 6.8 %collective-permute-start.13 = (f32[1,8,1,258]{3,2,1,0:T(1,128)S(1)}, f32[1,8,1,258]{3,2,1,0:T(1,128)S(1)}, u32[]{:S(2)}, u32[]{:S(2)}) collective-permute-start(f32[1,8,1,258]{3,2,1,0:T(1,128)S(1)} %get-tuple-element.373), channel_id=1, source_target_pairs={{0,1},{1,2},{2,3},{4,5},{5,6},{6,7},{8,9},{9,10},{10,11},{12,13},{... | collective-permute-start | bytes 24776 | tf_op jit(solution)/shard_map/ppermute | solution.py:21
  110.4 7.0 %collective-permute-start.16 = (f32[2,8,16,1]{3,2,1,0:T(8,128)S(1)}, f32[2,8,16,1]{3,2,1,0:T(8,128)S(1)}, u32[]{:S(2)}, u32[]{:S(2)}) collective-permute-start(f32[2,8,16,1]{3,2,1,0:T(8,128)S(1)} %get-tuple-element.372), channel_id=1, source_target_pairs={{4,0},{8,4},{12,8},{16,12},{20,16},{24,20},{28,24},{32,28},{36,32}... | collective-permute-start | bytes 3080 | tf_op jit(solution)/shard_map/ppermute | solution.py:22
  115.4 7.1 %collective-permute-start.15 = (f32[2,8,16,1]{3,2,1,0:T(8,128)S(1)}, f32[2,8,16,1]{3,2,1,0:T(8,128)S(1)}, u32[]{:S(2)}, u32[]{:S(2)}) collective-permute-start(f32[2,8,16,1]{3,2,1,0:T(8,128)S(1)} %get-tuple-element.371), channel_id=1, source_target_pairs={{0,4},{4,8},{8,12},{12,16},{16,20},{20,24},{24,28},{28,32},{32,36}... | collective-permute-start | bytes 3080 | tf_op jit(solution)/shard_map/ppermute | solution.py:21
  122.8 12.7 %collective-permute-start.17 = (f32[2,8,1,258]{3,2,1,0:T(1,128)S(1)}, f32[2,8,1,258]{3,2,1,0:T(1,128)S(1)}, u32[]{:S(2)}, u32[]{:S(2)}) collective-permute-start(f32[2,8,1,258]{3,2,1,0:T(1,128)S(1)} %get-tuple-element.305), channel_id=1, source_target_pairs={{0,1},{1,2},{2,3},{4,5},{5,6},{6,7},{8,9},{9,10},{10,11},{12,13},{... | collective-permute-start | bytes 49544 | tf_op jit(solution)/shard_map/ppermute | solution.py:21
  133.6 6.6 %collective-permute-start.30 = (f32[2,8,1,258]{3,2,1,0:T(1,128)S(1)}, f32[2,8,1,258]{3,2,1,0:T(1,128)S(1)}, u32[]{:S(2)}, u32[]{:S(2)}) collective-permute-start(f32[2,8,1,258]{3,2,1,0:T(1,128)S(1)} %get-tuple-element.306), channel_id=1, source_target_pairs={{1,0},{2,1},{3,2},{5,4},{6,5},{7,6},{9,8},{10,9},{11,10},{13,12},{... | collective-permute-start | bytes 49544 | tf_op jit(solution)/shard_map/ppermute | solution.py:22
  135.9 4.7 collective-permute-start.19
  135.9 6.5 %collective-permute-start.18 = (f32[1,8,16,1]{3,2,1,0:T(8,128)S(1)}, f32[1,8,16,1]{3,2,1,0:T(8,128)S(1)}, u32[]{:S(2)}, u32[]{:S(2)}) collective-permute-start(f32[1,8,16,1]{3,2,1,0:T(8,128)S(1)} %get-tuple-element.383), channel_id=1, source_target_pairs={{0,4},{4,8},{8,12},{12,16},{16,20},{20,24},{24,28},{28,32},{32,36}... | collective-permute-start | bytes 1544 | tf_op jit(solution)/shard_map/ppermute | solution.py:21
  142.6 20.7 %collective-permute-start.21 = (f32[1,8,1,258]{3,2,1,0:T(1,128)S(1)}, f32[1,8,1,258]{3,2,1,0:T(1,128)S(1)}, u32[]{:S(2)}, u32[]{:S(2)}) collective-permute-start(f32[1,8,1,258]{3,2,1,0:T(1,128)S(1)} %get-tuple-element.364), channel_id=1, source_target_pairs={{1,0},{2,1},{3,2},{5,4},{6,5},{7,6},{9,8},{10,9},{11,10},{13,12},{... | collective-permute-start | bytes 24776 | tf_op jit(solution)/shard_map/ppermute | solution.py:22
  144.5 18.8 %collective-permute-start.20 = (f32[1,8,1,258]{3,2,1,0:T(1,128)S(1)}, f32[1,8,1,258]{3,2,1,0:T(1,128)S(1)}, u32[]{:S(2)}, u32[]{:S(2)}) collective-permute-start(f32[1,8,1,258]{3,2,1,0:T(1,128)S(1)} %get-tuple-element.363), channel_id=1, source_target_pairs={{0,1},{1,2},{2,3},{4,5},{5,6},{6,7},{8,9},{9,10},{10,11},{12,13},{... | collective-permute-start | bytes 24776 | tf_op jit(solution)/shard_map/ppermute | solution.py:21
  163.8 7.2 %collective-permute-start.22 = (f32[2,8,16,1]{3,2,1,0:T(8,128)S(1)}, f32[2,8,16,1]{3,2,1,0:T(8,128)S(1)}, u32[]{:S(2)}, u32[]{:S(2)}) collective-permute-start(f32[2,8,16,1]{3,2,1,0:T(8,128)S(1)} %get-tuple-element.361), channel_id=1, source_target_pairs={{0,4},{4,8},{8,12},{12,16},{16,20},{20,24},{24,28},{28,32},{32,36}... | collective-permute-start | bytes 3080 | tf_op jit(solution)/shard_map/ppermute | solution.py:21
  171.2 12.8 %collective-permute-start.24 = (f32[2,8,1,258]{3,2,1,0:T(1,128)S(1)}, f32[2,8,1,258]{3,2,1,0:T(1,128)S(1)}, u32[]{:S(2)}, u32[]{:S(2)}) collective-permute-start(f32[2,8,1,258]{3,2,1,0:T(1,128)S(1)} %get-tuple-element.300), channel_id=1, source_target_pairs={{0,1},{1,2},{2,3},{4,5},{5,6},{6,7},{8,9},{9,10},{10,11},{12,13},{... | collective-permute-start | bytes 49544 | tf_op jit(solution)/shard_map/ppermute | solution.py:21
  182.1 6.6 %collective-permute-start.35 = (f32[2,8,1,258]{3,2,1,0:T(1,128)S(1)}, f32[2,8,1,258]{3,2,1,0:T(1,128)S(1)}, u32[]{:S(2)}, u32[]{:S(2)}) collective-permute-start(f32[2,8,1,258]{3,2,1,0:T(1,128)S(1)} %get-tuple-element.301), channel_id=1, source_target_pairs={{1,0},{2,1},{3,2},{5,4},{6,5},{7,6},{9,8},{10,9},{11,10},{13,12},{... | collective-permute-start | bytes 49544 | tf_op jit(solution)/shard_map/ppermute | solution.py:22
  184.4 4.7 collective-permute-start.41
  184.4 6.5 %collective-permute-start.40 = (f32[1,8,16,1]{3,2,1,0:T(8,128)S(1)}, f32[1,8,16,1]{3,2,1,0:T(8,128)S(1)}, u32[]{:S(2)}, u32[]{:S(2)}) collective-permute-start(f32[1,8,16,1]{3,2,1,0:T(8,128)S(1)} %get-tuple-element.381), channel_id=1, source_target_pairs={{0,4},{4,8},{8,12},{12,16},{16,20},{20,24},{24,28},{28,32},{32,36}... | collective-permute-start | bytes 1544 | tf_op jit(solution)/shard_map/ppermute | solution.py:21
  191.1 20.7 %collective-permute-start.43 = (f32[1,8,1,258]{3,2,1,0:T(1,128)S(1)}, f32[1,8,1,258]{3,2,1,0:T(1,128)S(1)}, u32[]{:S(2)}, u32[]{:S(2)}) collective-permute-start(f32[1,8,1,258]{3,2,1,0:T(1,128)S(1)} %get-tuple-element.348), channel_id=1, source_target_pairs={{1,0},{2,1},{3,2},{5,4},{6,5},{7,6},{9,8},{10,9},{11,10},{13,12},{... | collective-permute-start | bytes 24776 | tf_op jit(solution)/shard_map/ppermute | solution.py:22
  193.0 18.8 %collective-permute-start.42 = (f32[1,8,1,258]{3,2,1,0:T(1,128)S(1)}, f32[1,8,1,258]{3,2,1,0:T(1,128)S(1)}, u32[]{:S(2)}, u32[]{:S(2)}) collective-permute-start(f32[1,8,1,258]{3,2,1,0:T(1,128)S(1)} %get-tuple-element.347), channel_id=1, source_target_pairs={{0,1},{1,2},{2,3},{4,5},{5,6},{6,7},{8,9},{9,10},{10,11},{12,13},{... | collective-permute-start | bytes 24776 | tf_op jit(solution)/shard_map/ppermute | solution.py:21
  213.1 7.2 %collective-permute-start.44 = (f32[2,8,16,1]{3,2,1,0:T(8,128)S(1)}, f32[2,8,16,1]{3,2,1,0:T(8,128)S(1)}, u32[]{:S(2)}, u32[]{:S(2)}) collective-permute-start(f32[2,8,16,1]{3,2,1,0:T(8,128)S(1)} %get-tuple-element.345), channel_id=1, source_target_pairs={{0,4},{4,8},{8,12},{12,16},{16,20},{20,24},{24,28},{28,32},{32,36}... | collective-permute-start | bytes 3080 | tf_op jit(solution)/shard_map/ppermute | solution.py:21
  220.6 12.8 %collective-permute-start.47 = (f32[2,8,1,258]{3,2,1,0:T(1,128)S(1)}, f32[2,8,1,258]{3,2,1,0:T(1,128)S(1)}, u32[]{:S(2)}, u32[]{:S(2)}) collective-permute-start(f32[2,8,1,258]{3,2,1,0:T(1,128)S(1)} %get-tuple-element.296), channel_id=1, source_target_pairs={{1,0},{2,1},{3,2},{5,4},{6,5},{7,6},{9,8},{10,9},{11,10},{13,12},{... | collective-permute-start | bytes 49544 | tf_op jit(solution)/shard_map/ppermute | solution.py:22
  222.5 10.9 %collective-permute-start.46 = (f32[2,8,1,258]{3,2,1,0:T(1,128)S(1)}, f32[2,8,1,258]{3,2,1,0:T(1,128)S(1)}, u32[]{:S(2)}, u32[]{:S(2)}) collective-permute-start(f32[2,8,1,258]{3,2,1,0:T(1,128)S(1)} %get-tuple-element.295), channel_id=1, source_target_pairs={{0,1},{1,2},{2,3},{4,5},{5,6},{6,7},{8,9},{9,10},{10,11},{12,13},{... | collective-permute-start | bytes 49544 | tf_op jit(solution)/shard_map/ppermute | solution.py:21
  314.4 8.0 %collective-permute-start.32 = (f32[16,16,16,1]{2,1,3,0:T(8,128)}, f32[16,16,16,1]{2,1,3,0:T(8,128)}, u32[]{:S(2)}, u32[]{:S(2)}) collective-permute-start(f32[16,16,16,1]{2,1,3,0:T(8,128)} %copy.127), channel_id=1, source_target_pairs={{0,4},{4,8},{8,12},{12,16},{16,20},{20,24},{24,28},{28,32},{32,36}... | collective-permute-start | bytes 49160 | tf_op jit(solution)/shard_map/ppermute | solution.py:21
  331.4 10.0 %collective-permute-start.34 = (f32[16,16,1,258]{3,2,0,1:T(1,128)S(1)}, f32[16,16,1,258]{3,2,0,1:T(1,128)S(1)}, u32[]{:S(2)}, u32[]{:S(2)}) collective-permute-start(f32[16,16,1,258]{3,2,0,1:T(1,128)S(1)} %get-tuple-element.236), channel_id=1, source_target_pairs={{0,1},{1,2},{2,3},{4,5},{5,6},{6,7},{8,9},{9,10},{10,11},{12,13},{... | collective-permute-start | bytes 792584 | tf_op jit(solution)/shard_map/ppermute | solution.py:21
  336.6 10.6 %collective-permute-start.33 = (f32[16,16,1,258]{3,2,0,1:T(1,128)S(1)}, f32[16,16,1,258]{3,2,0,1:T(1,128)S(1)}, u32[]{:S(2)}, u32[]{:S(2)}) collective-permute-start(f32[16,16,1,258]{3,2,0,1:T(1,128)S(1)} %get-tuple-element.235), channel_id=1, source_target_pairs={{1,0},{2,1},{3,2},{5,4},{6,5},{7,6},{9,8},{10,9},{11,10},{13,12},{... | collective-permute-start | bytes 792584 | tf_op jit(solution)/shard_map/ppermute | solution.py:22
  381.8 7.5 %collective-permute-start.37 = (f32[16,16,16,1]{2,1,3,0:T(8,128)}, f32[16,16,16,1]{2,1,3,0:T(8,128)}, u32[]{:S(2)}, u32[]{:S(2)}) collective-permute-start(f32[16,16,16,1]{2,1,3,0:T(8,128)} %copy.151), channel_id=1, source_target_pairs={{0,4},{4,8},{8,12},{12,16},{16,20},{20,24},{24,28},{28,32},{32,36}... | collective-permute-start | bytes 49160 | tf_op jit(solution)/shard_map/ppermute | solution.py:21
  398.2 7.9 %collective-permute-start.39 = (f32[16,16,1,258]{3,2,0,1:T(1,128)S(1)}, f32[16,16,1,258]{3,2,0,1:T(1,128)S(1)}, u32[]{:S(2)}, u32[]{:S(2)}) collective-permute-start(f32[16,16,1,258]{3,2,0,1:T(1,128)S(1)} %get-tuple-element.234), channel_id=1, source_target_pairs={{0,1},{1,2},{2,3},{4,5},{5,6},{6,7},{8,9},{9,10},{10,11},{12,13},{... | collective-permute-start | bytes 792584 | tf_op jit(solution)/shard_map/ppermute | solution.py:21
  401.3 10.6 %collective-permute-start.38 = (f32[16,16,1,258]{3,2,0,1:T(1,128)S(1)}, f32[16,16,1,258]{3,2,0,1:T(1,128)S(1)}, u32[]{:S(2)}, u32[]{:S(2)}) collective-permute-start(f32[16,16,1,258]{3,2,0,1:T(1,128)S(1)} %get-tuple-element.233), channel_id=1, source_target_pairs={{1,0},{2,1},{3,2},{5,4},{6,5},{7,6},{9,8},{10,9},{11,10},{13,12},{... | collective-permute-start | bytes 792584 | tf_op jit(solution)/shard_map/ppermute | solution.py:22
  444.3 6.1 %collective-permute-start.48 = (f32[16,16,16,1]{2,1,3,0:T(8,128)}, f32[16,16,16,1]{2,1,3,0:T(8,128)}, u32[]{:S(2)}, u32[]{:S(2)}) collective-permute-start(f32[16,16,16,1]{2,1,3,0:T(8,128)} %copy.173), channel_id=1, source_target_pairs={{4,0},{8,4},{12,8},{16,12},{20,16},{24,20},{28,24},{32,28},{36,32}... | collective-permute-start | bytes 49160 | tf_op jit(solution)/shard_map/ppermute | solution.py:22
  446.5 7.5 %collective-permute-start.49 = (f32[16,16,16,1]{2,1,3,0:T(8,128)}, f32[16,16,16,1]{2,1,3,0:T(8,128)}, u32[]{:S(2)}, u32[]{:S(2)}) collective-permute-start(f32[16,16,16,1]{2,1,3,0:T(8,128)} %copy.175), channel_id=1, source_target_pairs={{0,4},{4,8},{8,12},{12,16},{16,20},{20,24},{24,28},{28,32},{32,36}... | collective-permute-start | bytes 49160 | tf_op jit(solution)/shard_map/ppermute | solution.py:21
  462.9 7.9 %collective-permute-start.51 = (f32[16,16,1,258]{3,2,0,1:T(1,128)S(1)}, f32[16,16,1,258]{3,2,0,1:T(1,128)S(1)}, u32[]{:S(2)}, u32[]{:S(2)}) collective-permute-start(f32[16,16,1,258]{3,2,0,1:T(1,128)S(1)} %get-tuple-element.232), channel_id=1, source_target_pairs={{0,1},{1,2},{2,3},{4,5},{5,6},{6,7},{8,9},{9,10},{10,11},{12,13},{... | collective-permute-start | bytes 792584 | tf_op jit(solution)/shard_map/ppermute | solution.py:21
  466.0 10.6 %collective-permute-start.50 = (f32[16,16,1,258]{3,2,0,1:T(1,128)S(1)}, f32[16,16,1,258]{3,2,0,1:T(1,128)S(1)}, u32[]{:S(2)}, u32[]{:S(2)}) collective-permute-start(f32[16,16,1,258]{3,2,0,1:T(1,128)S(1)} %get-tuple-element.231), channel_id=1, source_target_pairs={{1,0},{2,1},{3,2},{5,4},{6,5},{7,6},{9,8},{10,9},{11,10},{13,12},{... | collective-permute-start | bytes 792584 | tf_op jit(solution)/shard_map/ppermute | solution.py:22
  (237 other events, 2493.5 us)
where the time goes:
time: 516 us; the launch traced here: 506 us
  other arithmetic  135 us (26%)
  starting transfers between devices  133 us (26%)
  local copies, waits for them, and re-layouts  89.3 us (17%)
  blocking collectives  69.6 us (13%)
  waiting for transfers between devices  56.4 us (11%)
  matrix products  17.6 us (3%)
    ppermute x26, starting transfers between devices, extended(): before = lax.ppermute(last, axis, up)  77.9 us
    ppermute x26, starting transfers between devices, extended(): after = lax.ppermute(first, axis, down)  55 us
    all_gather x4, blocking collectives, body(): lax.all_gather(flux_pad, 'set', axis=1, tiled=True)  51.5 us
    sub x4, other arithmetic, tracer_update(): thickness * center  50.6 us
    ppermute x26, waiting for transfers between devices, extended(): after = lax.ppermute(first, axis, down)  30.8 us
    unnamed x530, local copies, waits for them, and re-layouts  27.9 us
    ppermute x26, waiting for transfers between devices, extended(): before = lax.ppermute(last, axis, up)  25.5 us
    mul x39, other arithmetic, column_mix(): result[level] = solved[level] + ratios[level] * result[level + 1]  24.2 us
  transfers between devices with their start and end apart: 52, of which 21 were waited for; matrix products, arithmetic and copies ran while one was open for 17% of the time, Pallas kernels for 0%

commit v1 on v0

v1 whole, which is shorter than its diff:
```python
import jax
import jax.numpy as jnp
from jax import lax
from jax.experimental import pallas as pl
from jax.experimental.pallas import tpu as pltpu
from jax.sharding import PartitionSpec as P

ITERS = 4
DT = 0.2
G = 1.0
ROTATION = 0.5
LV = 16
NT = 16
PER = 8
VMEM_LIMIT = 60 * 1024 * 1024
F32 = jnp.float32
ANY = pl.BlockSpec(memory_space=pl.ANY)
SMEM = pl.BlockSpec(memory_space=pltpu.SMEM)
VMEM = pl.BlockSpec(memory_space=pltpu.VMEM)


def sub_iota(rows=8):
    return lax.broadcasted_iota(jnp.int32, (rows, 128), 0)


def lane_iota(rows=8):
    return lax.broadcasted_iota(jnp.int32, (rows, 128), 1)


def from_east(tiles):
    rolled = [pltpu.roll(x, 127, 1) for x in tiles]
    lane = lane_iota(tiles[0].shape[0])
    last = len(tiles) - 1
    return [rolled[i] if i == last else jnp.where(lane == 127, rolled[i + 1], rolled[i]) for i in range(last + 1)]


def from_west(tiles):
    rolled = [pltpu.roll(x, 1, 1) for x in tiles]
    lane = lane_iota(tiles[0].shape[0])
    return [rolled[i] if i == 0 else jnp.where(lane == 0, rolled[i - 1], rolled[i]) for i in range(len(tiles))]


def coriolis_of(row, rows_total):
    return ROTATION * (2.0 * (row.astype(F32) + 0.5) / rows_total - 1.0)


def level_step(k, h_s, h_c, h_n, u_s, u_c, v_s, v_c, deep, cor_c, cor_s, diff, up, prev):
    d_c, d_e, d_n, d_s = deep
    h_e = from_east(h_c)
    count = len(h_c)
    u_new, v_new, u_flux, v_flux, s_flux = [], [], [], [], []
    for j in range(count):
        un = jnp.where(k < d_e[j], u_c[j] + DT * (cor_c * v_c[j] - G * (h_e[j] - h_c[j])), 0.0)
        vn = jnp.where(k < d_n[j], v_c[j] - DT * (cor_c * u_c[j] + G * (h_n[j] - h_c[j])), 0.0)
        vs = jnp.where(k < d_s[j], v_s[j] - DT * (cor_s * u_s[j] + G * (h_c[j] - h_s[j])), 0.0)
        u_new.append(un)
        v_new.append(vn)
        u_flux.append(un * 0.5 * (h_c[j] + h_e[j]))
        v_flux.append(vn * 0.5 * (h_c[j] + h_n[j]))
        s_flux.append(vs * 0.5 * (h_s[j] + h_c[j]))
    w_flux = from_west(u_flux)
    h_new, coefs, links, ratios = [], [], [], []
    for j in range(count):
        fe, fw, fn, fs = u_flux[j], w_flux[j], v_flux[j], s_flux[j]
        hn = h_c[j] - DT * ((fe - fw) + (fn - fs))
        link = jnp.where(k + 1 < d_c[j], DT * diff[j], 0.0)
        q = jnp.where(k < d_c[j], 1.0 / (hn + up[j] + link - up[j] * prev[j]), 0.0)
        r = link * q
        dq = DT * q
        ce = dq * jnp.maximum(-fe, 0.0)
        cw = dq * jnp.maximum(fw, 0.0)
        cn = dq * jnp.maximum(-fn, 0.0)
        cs = dq * jnp.maximum(fs, 0.0)
        out = (jnp.maximum(fe, 0.0) - jnp.minimum(fw, 0.0)) + (jnp.maximum(fn, 0.0) - jnp.minimum(fs, 0.0))
        ca = q * h_c[j] - dq * out
        h_new.append(hn)
        links.append(link)
        ratios.append(r)
        coefs.append((ca, ce, cw, cn, cs, up[j] * q, r))
    return h_new, u_new, v_new, coefs, links, ratios


def forward(k, coefs, cells, before):
    result = []
    for t, (c, s, n) in enumerate(cells):
        e = from_east(c)
        w = from_west(c)
        result.append([
            ((coefs[0][j] * c[j] + coefs[1][j] * e[j]) + (coefs[2][j] * w[j] + coefs[3][j] * n[j]))
            + (coefs[4][j] * s[j] + coefs[5][j] * before[t][j])
            for j in range(len(c))
        ])
    return result


def react(table, s, m):
    outs = []
    for a in range(PER):
        acc = None
        for b in range(PER):
            w = table[s * 64 + a * 8 + b]
            term = [w * x for x in m[b]]
            acc = term if acc is None else [p + q for p, q in zip(acc, term)]
        outs.append(acc)
    return outs


def fill_table(react_ref, table):
    for s in range(2):
        for a in range(PER):
            for b in range(PER):
                v = DT * react_ref[s, a, b] + (1.0 if a == b else 0.0)
                table[s * 64 + a * 8 + b] = jnp.full((8, 128), v, F32)


def zeros_like_tiles(rows, count):
    return [jnp.zeros((rows, 128), F32) for _ in range(count)]


def own_copies(tr, ho, hp, vo, vp, df, off, c_buf, h_buf, u_buf, v_buf, d_buf, sem):
    copies = []
    part = LV // 2
    other = part - off
    for j in range(2):
        lanes = pl.ds(128 * j, 128)
        rows = pl.ds(8, 16)
        copies.append(pltpu.make_async_copy(ho.at[:, :, lanes], h_buf.at[pl.ds(off, part), j, rows, :], sem.at[0 + j]))
        copies.append(pltpu.make_async_copy(hp.at[:, :, lanes], h_buf.at[pl.ds(other, part), j, rows, :], sem.at[2 + j]))
        copies.append(pltpu.make_async_copy(vo.at[0, :, :, lanes], u_buf.at[pl.ds(off, part), j, rows, :], sem.at[4 + j]))
        copies.append(pltpu.make_async_copy(vp.at[0, :, :, lanes], u_buf.at[pl.ds(other, part), j, rows, :], sem.at[6 + j]))
        copies.append(pltpu.make_async_copy(vo.at[1, :, :, lanes], v_buf.at[pl.ds(off, part), j, rows, :], sem.at[8 + j]))
        copies.append(pltpu.make_async_copy(vp.at[1, :, :, lanes], v_buf.at[pl.ds(other, part), j, rows, :], sem.at[10 + j]))
        copies.append(pltpu.make_async_copy(df.at[:, :, lanes], d_buf.at[:, j, rows, :], sem.at[12 + j]))
    tracer = []
    for s in range(2):
        for j in range(2):
            tracer.append(pltpu.make_async_copy(
                tr.at[pl.ds(8 * s, 8), :, :, pl.ds(128 * j, 128)],
                c_buf.at[pl.ds(8 * s, 8), :, j, pl.ds(8, 16), :], sem.at[14 + 2 * s + j]))
    return copies, tracer


OWN_SCRATCH = [
    pltpu.VMEM((NT, LV, 2, 32, 128), F32),
    pltpu.VMEM((LV, 2, 32, 128), F32),
    pltpu.VMEM((LV, 2, 32, 128), F32),
    pltpu.VMEM((LV, 2, 32, 128), F32),
    pltpu.VMEM((LV, 2, 32, 128), F32),
    pltpu.VMEM((2, 32, 128), jnp.int32),
    pltpu.SemaphoreType.DMA((18,)),
]


def fill_depth(land, level, p_buf):
    for j in range(2):
        lanes = slice(128 * j, 128 * j + 128)
        p_buf[j, 8:24, :] = jnp.where(land[:, lanes] == 1, level[:, lanes], 0)


def rows_kernel(scal, tr, ho, hp, vo, vp, df, land, level, y_up, y_dn, c_buf, h_buf, u_buf, v_buf, d_buf, p_buf, sem):
    off = scal[0] * (LV // 2)
    fields, tracer = own_copies(tr, ho, hp, vo, vp, df, off, c_buf, h_buf, u_buf, v_buf, d_buf, sem)
    for c in fields + tracer:
        c.start()
    fill_depth(land, level, p_buf)
    for c in fields + tracer:
        c.wait()
    low = sub_iota() < 4

    def put(index, j, first, second):
        y_up[index, j] = jnp.where(low, first(20), second(16))
        y_dn[index, j] = jnp.where(low, first(8), second(4))

    @pl.loop(0, LV)
    def _(k):
        for j in range(2):
            for t in range(PER):
                put(t * LV + k, j, lambda r: c_buf[t, k, j, r:r + 8, :], lambda r: c_buf[t + PER, k, j, r:r + 8, :])
            put(128 + k, j, lambda r: h_buf[k, j, r:r + 8, :], lambda r: u_buf[k, j, r:r + 8, :])
            put(144 + k, j, lambda r: v_buf[k, j, r:r + 8, :], lambda r: d_buf[k, j, r:r + 8, :])

    for j in range(2):
        get = lambda r: p_buf[j, r:r + 8, :].astype(F32)
        put(160, j, get, get)


def inner_kernel(rows_total, scal, tr, ho, hp, vo, vp, df, land, level, reaction, saved, saved_f, mid, mid_f,
                 c_buf, h_buf, u_buf, v_buf, d_buf, p_buf, sem, c_alt, solved, coef, table):
    off = scal[0] * (LV // 2)
    fields, tracer = own_copies(tr, ho, hp, vo, vp, df, off, c_buf, h_buf, u_buf, v_buf, d_buf, sem)
    for c in fields + tracer:
        c.start()
    fill_depth(land, level, p_buf)
    fill_table(reaction, table)
    six = sub_iota() < 6
    rows = lax.broadcasted_iota(jnp.int32, (16, 128), 0) + scal[1]
    cor_c = coriolis_of(rows, rows_total)
    cor_s = coriolis_of(rows - 1, rows_total)
    d_c = [p_buf[j, 8:24, :] for j in range(2)]
    d_e = [jnp.minimum(a, b) for a, b in zip(d_c, from_east(d_c))]
    d_n = [jnp.minimum(d_c[j], p_buf[j, 9:25, :]) for j in range(2)]
    d_s = [jnp.minimum(d_c[j], p_buf[j, 7:23, :]) for j in range(2)]
    for c in fields:
        c.wait()

    def keep(n, read):
        return jnp.where(six, read(4 + n), read(16 - n))

    def keep_fields(n):
        @pl.loop(0, LV)
        def _(k):
            for f, buf in enumerate((h_buf, u_buf, v_buf)):
                for j in range(2):
                    saved_f[n, f, k, j] = keep(n, lambda r: buf[k, j, r:r + 8, :])

    def keep_tracers(n, buf):
        @pl.loop(0, LV)
        def _(k):
            for t in range(NT):
                for j in range(2):
                    saved[n, t, k, j] = keep(n, lambda r: buf[t, k, j, r:r + 8, :])

    keep_fields(0)
    for c in tracer:
        c.wait()
    keep_tracers(0, c_buf)
    for n in range(1, ITERS + 1):
        src, dst = (c_buf, c_alt) if n % 2 else (c_alt, c_buf)

        def dynamics(k, carry):
            up, prev = carry
            read = lambda buf, r: [buf[k, j, r:r + 16, :] for j in range(2)]
            h_new, u_new, v_new, co, links, ratios = level_step(
                k, read(h_buf, 7), read(h_buf, 8), read(h_buf, 9), read(u_buf, 7), read(u_buf, 8),
                read(v_buf, 7), read(v_buf, 8), (d_c, d_e, d_n, d_s), cor_c, cor_s, read(d_buf, 8), up, prev)
            for j in range(2):
                h_buf[k, j, 8:24, :] = h_new[j]
                u_buf[k, j, 8:24, :] = u_new[j]
                v_buf[k, j, 8:24, :] = v_new[j]
                for c in range(7):
                    coef[c, k, j] = co[j][c]
            return links, ratios

        lax.fori_loop(0, LV, dynamics, (zeros_like_tiles(16, 2), zeros_like_tiles(16, 2)))
        if n < ITERS:
            keep_fields(n)
        else:
            @pl.loop(0, LV)
            def _(k):
                for f, buf in enumerate((h_buf, u_buf, v_buf)):
                    for j in range(2):
                        mid_f[f, k, j] = buf[k, j, 12:20, :]

        for r0 in ((8, 16) if n < ITERS else (12,)):
            @pl.loop(0, 2)
            def _(s):
                def down(k, before):
                    co = [[coef[c, k, j, r0 - 8:r0, :] for j in range(2)] for c in range(6)]
                    read = lambda t, r: [src[s * PER + t, k, j, r:r + 8, :] for j in range(2)]
                    now = forward(k, co, [(read(t, r0), read(t, r0 - 1), read(t, r0 + 1)) for t in range(PER)], before)
                    for t in range(PER):
                        for j in range(2):
                            solved[k, t, j] = now[t][j]
                    return now

                lax.fori_loop(0, LV, down, [zeros_like_tiles(8, 2) for _ in range(PER)])

                def upward(i, m):
                    k = LV - 1 - i
                    r = [coef[6, k, j, r0 - 8:r0, :] for j in range(2)]
                    m = [[solved[k, t, j] + r[j] * m[t][j] for j in range(2)] for t in range(PER)]
                    outs = react(table, s, m)
                    for t in range(PER):
                        for j in range(2):
                            if n < ITERS:
                                dst[s * PER + t, k, j, r0:r0 + 8, :] = outs[t][j]
                            else:
                                mid[s * PER + t, k, j] = outs[t][j]
                    return m

                lax.fori_loop(0, LV, upward, [zeros_like_tiles(8, 2) for _ in range(PER)])
        if n < ITERS:
            keep_tracers(n, dst)


def strip_pack_kernel(scal, tr, ho, hp, vo, vp, df, land, level, y_s, y_n, o_ref, x_r, x_l,
                      c_buf, h_buf, u_buf, v_buf, d_buf, p_buf, sem):
    off = scal[0] * (LV // 2)
    fields, tracer = own_copies(tr, ho, hp, vo, vp, df, off, c_buf, h_buf, u_buf, v_buf, d_buf, sem)
    for c in fields + tracer:
        c.start()
    fill_depth(land, level, p_buf)
    for c in fields + tracer:
        c.wait()
    low = sub_iota() < 4
    lane = lane_iota()
    place = lane & 31
    slot = lane >> 5

    def three(read, index, half, j):
        ys, yn = y_s[index, j], y_n[index, j]
        if half == 0:
            yn = pltpu.roll(yn, 4, 0)
        else:
            ys = pltpu.roll(ys, 4, 0)
        return [jnp.where(low, ys, read(4)), read(12), jnp.where(low, read(20), yn)]

    def pack(sources):
        acc = [None] * 3
        for q, (read, index, half) in enumerate(sources):
            left = three(lambda r: read(0, r), index, half, 0)
            right = three(lambda r: read(1, r), index, half, 1)
            for i in range(3):
                a = pltpu.roll(left[i], (4 + 32 * q) % 128, 1)
                b = pltpu.roll(right[i], (28 + 32 * q) % 128, 1)
                x = jnp.where(place < 16, a, b)
                acc[i] = x if acc[i] is None else jnp.where(slot == q, x, acc[i])
        return acc

    @pl.loop(0, LV)
    def _(k):
        def tracer_source(t):
            return (lambda j, r: c_buf[t, k, j, r:r + 8, :], (t % PER) * LV + k, t // PER)

        groups = [[tracer_source(4 * g + q) for q in range(4)] for g in range(4)]
        groups.append([
            (lambda j, r: h_buf[k, j, r:r + 8, :], 128 + k, 0), (lambda j, r: u_buf[k, j, r:r + 8, :], 128 + k, 1),
            (lambda j, r: v_buf[k, j, r:r + 8, :], 144 + k, 0), (lambda j, r: d_buf[k, j, r:r + 8, :], 144 + k, 1)])
        xr, xl = [jnp.zeros((8, 128), F32)] * 3, [jnp.zeros((8, 128), F32)] * 3
        for g in range(5):
            packed = pack(groups[g])
            here = (place >= 4 * g) & (place < 4 * g + 4)
            for i in range(3):
                o_ref[k, g, 8 * i:8 * i + 8, :] = packed[i]
                xr[i] = jnp.where(here, pltpu.roll(packed[i], (4 * g - 24) % 128, 1), xr[i])
                xl[i] = jnp.where(here, pltpu.roll(packed[i], (4 * g - 4) % 128, 1), xl[i])
        for i in range(3):
            x_r[k, 8 * i:8 * i + 8, :] = xr[i]
            x_l[k, 8 * i:8 * i + 8, :] = xl[i]

    packed = pack([(lambda j, r: p_buf[j, r:r + 8, :].astype(F32), 160, 0)] * 4)
    for i in range(3):
        for g in range(5):
            o_ref[LV, g, 8 * i:8 * i + 8, :] = packed[i]
        x_r[LV, 8 * i:8 * i + 8, :] = pltpu.roll(packed[i], (16 - 24) % 128, 1)
        x_l[LV, 8 * i:8 * i + 8, :] = pltpu.roll(packed[i], (16 - 4) % 128, 1)


def edge_kernel(rows_total, scal, saved, saved_f, y_s, y_n, df, land, level, reaction, out_c, out_f,
                c_buf, f_buf, d_buf, p_buf, solved, coef, table, sem):
    copies = []
    for n in range(ITERS):
        copies.append(pltpu.make_async_copy(saved_f.at[n], f_buf.at[n, :, :, :, pl.ds(0, 8), :], sem.at[n]))
    for j in range(2):
        copies.append(pltpu.make_async_copy(df.at[:, :, pl.ds(128 * j, 128)], d_buf.at[:, j, pl.ds(8, 16), :], sem.at[4 + j]))
    tracer = [pltpu.make_async_copy(saved.at[n], c_buf.at[n, :, :, :, pl.ds(0, 8), :], sem.at[6 + n]) for n in range(ITERS)]
    for c in copies + tracer:
        c.start()
    fill_table(reaction, table)
    fill_depth(land, level, p_buf)
    sub = sub_iota()
    low = sub < 4
    for c in copies:
        c.wait()
    tracer[0].wait()

    def put(ref, y, half, south):
        if half != (0 if south else 1):
            y = pltpu.roll(y, 4, 0)
        if south:
            pltpu.store(ref.at[pl.ds(0, 8), :], y, mask=low)
        else:
            pltpu.store(ref.at[pl.ds(4, 8), :], y, mask=jnp.logical_not(low))

    @pl.loop(0, LV)
    def _(k):
        for j in range(2):
            for t in range(PER):
                ys, yn = y_s[t * LV + k, j], y_n[t * LV + k, j]
                for half in range(2):
                    put(c_buf.at[0, t + PER * half, k, j], ys, half, True)
                    put(c_buf.at[0, t + PER * half, k, j], yn, half, False)
            for f, (index, half) in enumerate(((128, 0), (128, 1), (144, 0))):
                put(f_buf.at[0, f, k, j], y_s[index + k, j], half, True)
                put(f_buf.at[0, f, k, j], y_n[index + k, j], half, False)
            ys, yn = y_s[144 + k, j], y_n[144 + k, j]
            pltpu.store(d_buf.at[k, j, pl.ds(0, 8), :], ys, mask=jnp.logical_not(low))
            pltpu.store(d_buf.at[k, j, pl.ds(24, 8), :], pltpu.roll(yn, 4, 0), mask=low)

    for j in range(2):
        ys, yn = y_s[160, j].astype(jnp.int32), y_n[160, j].astype(jnp.int32)
        pltpu.store(p_buf.at[j, pl.ds(0, 8), :], ys, mask=jnp.logical_not(low))
        pltpu.store(p_buf.at[j, pl.ds(24, 8), :], yn, mask=low)

    def gather(read, shift):
        return jnp.where(low, read(shift), read(shift + 2))

    for n in range(1, ITERS + 1):
        if n < ITERS:
            tracer[n].wait()

        def at(buf, j, shift):
            return jnp.where(low, buf[j, 4 + n + shift:12 + n + shift, :], buf[j, 20 - n + shift:28 - n + shift, :])

        row = jnp.where(low, sub - 4 + n, sub + 12 - n) + scal[1]
        cor_c = coriolis_of(row, rows_total)
        cor_s = coriolis_of(row - 1, rows_total)
        d_c = [at(p_buf, j, 0) for j in range(2)]
        d_e = [jnp.minimum(a, b) for a, b in zip(d_c, from_east(d_c))]
        d_n = [jnp.minimum(d_c[j], at(p_buf, j, 1)) for j in range(2)]
        d_s = [jnp.minimum(d_c[j], at(p_buf, j, -1)) for j in range(2)]

        def dynamics(k, carry):
            up, prev = carry
            read = lambda f, shift: [gather(lambda r: f_buf[n - 1, f, k, j, r:r + 8, :], shift) for j in range(2)]
            diff = [at(d_buf.at[k], j, 0) for j in range(2)]
            h_new, u_new, v_new, co, links, ratios = level_step(
                k, read(0, 0), read(0, 1), read(0, 2), read(1, 0), read(1, 1), read(2, 0), read(2, 1),
                (d_c, d_e, d_n, d_s), cor_c, cor_s, diff, up, prev)
            for j in range(2):
                for f, x in enumerate((h_new[j], u_new[j], v_new[j])):
                    if n < ITERS:
                        pltpu.store(f_buf.at[n, f, k, j, pl.ds(0, 8), :], x, mask=low)
                        pltpu.store(f_buf.at[n, f, k, j, pl.ds(4, 8), :], x, mask=jnp.logical_not(low))
                    else:
                        out_f[f, k, j] = x
                for c in range(7):
                    coef[c, k, j] = co[j][c]
            return links, ratios

        lax.fori_loop(0, LV, dynamics, (zeros_like_tiles(8, 2), zeros_like_tiles(8, 2)))

        @pl.loop(0, 2)
        def _(s):
            def down(k, before):
                co = [[coef[c, k, j] for j in range(2)] for c in range(6)]

                def read(t, shift):
                    return [gather(lambda r: c_buf[n - 1, s * PER + t, k, j, r:r + 8, :], shift) for j in range(2)]

                now = forward(k, co, [(read(t, 1), read(t, 0), read(t, 2)) for t in range(PER)], before)
                for t in range(PER):
                    for j in range(2):
                        solved[k, t, j] = now[t][j]
                return now

            lax.fori_loop(0, LV, down, [zeros_like_tiles(8, 2) for _ in range(PER)])

            def upward(i, m):
                k = LV - 1 - i
                r = [coef[6, k, j] for j in range(2)]
                m = [[solved[k, t, j] + r[j] * m[t][j] for j in range(2)] for t in range(PER)]
                outs = react(table, s, m)
                for t in range(PER):
                    for j in range(2):
                        if n < ITERS:
                            pltpu.store(c_buf.at[n, s * PER + t, k, j, pl.ds(0, 8), :], outs[t][j], mask=low)
                            pltpu.store(c_buf.at[n, s * PER + t, k, j, pl.ds(4, 8), :], outs[t][j], mask=jnp.logical_not(low))
                        else:
                            out_c[s * PER + t, k, j] = outs[t][j]
                return m

            lax.fori_loop(0, LV, upward, [zeros_like_tiles(8, 2) for _ in range(PER)])


def strip_kernel(rows_total, scal, o_ref, x_r, x_l, reaction, mid, mid_f, edge, edge_f, out_c, out_h, out_v,
                 c_buf, c_alt, h_buf, u_buf, v_buf, d_buf, p_buf, solved, coef, table):
    lane = lane_iota()
    place = lane & 31
    slot = lane >> 5
    low = sub_iota() < 4
    for s in range(2):
        for go in range(2):
            for gi in range(2):
                for rho in range(4):
                    v = jnp.zeros((8, 128), F32)
                    for q in range(4):
                        a, b = 4 * go + q, 4 * gi + (q - rho) % 4
                        w = DT * reaction[s, a, b] + (1.0 if a == b else 0.0)
                        v = jnp.where(slot == q, jnp.full((8, 128), w, F32), v)
                    table[((s * 2 + go) * 2 + gi) * 4 + rho] = v

    def whole(k, g, i, xg):
        rows = slice(8 * i, 8 * i + 8)
        a = pltpu.roll(x_r[k, rows, :], (-4 * xg) % 128, 1)
        b = pltpu.roll(x_l[k, rows, :], (28 - 4 * xg) % 128, 1)
        return jnp.where(place < 4, a, jnp.where(place >= 28, b, o_ref[k, g, rows, :]))

    @pl.loop(0, LV)
    def _(k):
        for i in range(3):
            for g in range(4):
                c_buf[g, k, 8 + 8 * i:16 + 8 * i, :] = whole(k, g, i, g)
            x = whole(k, 4, i, 4)
            for f, buf in enumerate((h_buf, u_buf, v_buf, d_buf)):
                y = jnp.where(lane < 32, pltpu.roll(x, (-32 * f) % 128, 1), 0.0)
                y = y + pltpu.roll(y, 32, 1)
                y = y + pltpu.roll(y, 64, 1)
                buf[k, 8 + 8 * i:16 + 8 * i, :] = y

    for i in range(3):
        p_buf[8 + 8 * i:16 + 8 * i, :] = whole(LV, 4, i, 4).astype(jnp.int32)

    rows = lax.broadcasted_iota(jnp.int32, (24, 128), 0) - 4 + scal[1]
    cor_c = coriolis_of(rows, rows_total)
    cor_s = coriolis_of(rows - 1, rows_total)
    d_c = [p_buf[8:32, :]]
    d_e = [jnp.minimum(d_c[0], from_east(d_c)[0])]
    d_n = [jnp.minimum(d_c[0], p_buf[9:33, :])]
    d_s = [jnp.minimum(d_c[0], p_buf[7:31, :])]

    for n in range(1, ITERS + 1):
        src, dst = (c_buf, c_alt) if n % 2 else (c_alt, c_buf)

        def dynamics(k, carry):
            up, prev = carry
            read = lambda buf, r: [buf[k, r:r + 24, :]]
            h_new, u_new, v_new, co, links, ratios = level_step(
                k, read(h_buf, 7), read(h_buf, 8), read(h_buf, 9), read(u_buf, 7), read(u_buf, 8),
                read(v_buf, 7), read(v_buf, 8), (d_c, d_e, d_n, d_s), cor_c, cor_s, read(d_buf, 8), up, prev)
            h_buf[k, 8:32, :] = h_new[0]
            u_buf[k, 8:32, :] = u_new[0]
            v_buf[k, 8:32, :] = v_new[0]
            for c in range(7):
                coef[c, k] = co[0][c]
            return links, ratios

        lax.fori_loop(0, LV, dynamics, (zeros_like_tiles(24, 1), zeros_like_tiles(24, 1)))

        for r0 in ((8, 16, 24) if n < ITERS else (12, 20)):
            def down(k, before):
                co = [[coef[c, k, r0 - 8:r0, :]] for c in range(6)]
                read = lambda t, r: [src[t, k, r:r + 8, :]]
                now = forward(k, co, [(read(t, r0), read(t, r0 - 1), read(t, r0 + 1)) for t in range(4)], before)
                for t in range(4):
                    solved[k, t] = now[t][0]
                return now

            lax.fori_loop(0, LV, down, [zeros_like_tiles(8, 1) for _ in range(4)])

            def upward(i, m):
                k = LV - 1 - i
                r = coef[6, k, r0 - 8:r0, :]
                m = [solved[k, t] + r * m[t] for t in range(4)]
                turned = [[x] + [pltpu.roll(x, 32 * rho, 1) for rho in range(1, 4)] for x in m]
                for s in range(2):
                    for go in range(2):
                        acc = None
                        for gi in range(2):
                            for rho in range(4):
                                term = table[((s * 2 + go) * 2 + gi) * 4 + rho] * turned[2 * s + gi][rho]
                                acc = term if acc is None else acc + term
                        dst[2 * s + go, k, r0:r0 + 8, :] = acc
                return m

            lax.fori_loop(0, LV, upward, [jnp.zeros((8, 128), F32) for _ in range(4)])

    final = c_buf if ITERS % 2 == 0 else c_alt

    def merge(inner, outer, strip, q, j, i):
        turned = pltpu.roll(inner, 4, 0)
        body = jnp.where(low, outer, turned) if i == 0 else jnp.where(low, turned, outer)
        if j == 0:
            return jnp.where(lane < 4, pltpu.roll(strip, (-(32 * q + 4)) % 128, 1), body)
        return jnp.where(lane >= 124, pltpu.roll(strip, (100 - 32 * q) % 128, 1), body)

    @pl.loop(0, LV)
    def _(k):
        for t in range(NT):
            for i in range(2):
                strip = final[t // 4, k, 12 + 8 * i:20 + 8 * i, :]
                for j in range(2):
                    out_c[t, k, 8 * i:8 * i + 8, 128 * j:128 * j + 128] = merge(
                        mid[t, k, j], edge[t, k, j], strip, t % 4, j, i)

    off = scal[0] * (LV // 2)

    @pl.loop(0, LV // 2)
    def _(k):
        for f, buf in enumerate((h_buf, u_buf, v_buf)):
            for i in range(2):
                strip = buf[k + off, 12 + 8 * i:20 + 8 * i, :]
                for j in range(2):
                    x = merge(mid_f[f, k + off, j], edge_f[f, k + off, j], strip, 0, j, i)
                    if f == 0:
                        out_h[k, 8 * i:8 * i + 8, 128 * j:128 * j + 128] = x
                    else:
                        out_v[f - 1, k, 8 * i:8 * i + 8, 128 * j:128 * j + 128] = x


def sds(*shape):
    return jax.ShapeDtypeStruct(shape, F32)


def body(tracers, thickness, velocity, diffusivity, reaction, land_mask, level_count):
    rows_local = thickness.shape[1]
    rows_total = rows_local * lax.axis_size("ty")
    set_index = lax.axis_index("set").astype(jnp.int32)
    row_start = lax.axis_index("ty").astype(jnp.int32) * rows_local
    scal = jnp.stack([set_index, row_start])
    swap = [(0, 1), (1, 0)]
    h_pair = lax.ppermute(thickness, "set", swap)
    v_pair = lax.ppermute(velocity, "set", swap)
    own = (scal, tracers, thickness, h_pair, velocity, v_pair, diffusivity, land_mask, level_count)
    own_specs = [SMEM] + [ANY] * 6 + [VMEM] * 2
    params = pltpu.CompilerParams(vmem_limit_bytes=VMEM_LIMIT)
    y_up, y_dn = pl.pallas_call(
        rows_kernel, out_shape=[sds(161, 2, 8, 128)] * 2, in_specs=own_specs, out_specs=[VMEM] * 2,
        scratch_shapes=OWN_SCRATCH, compiler_params=params, name="edge_rows")(*own)
    ty = lax.axis_size("ty")
    north = [(i, i + 1) for i in range(ty - 1)]
    south = [(j, i) for i, j in north]
    y_s = lax.ppermute(y_up, "ty", north)
    y_n = lax.ppermute(y_dn, "ty", south)
    saved, saved_f, mid, mid_f = pl.pallas_call(
        lambda *a: inner_kernel(rows_total, *a),
        out_shape=[sds(ITERS, NT, LV, 2, 8, 128), sds(ITERS, 3, LV, 2, 8, 128), sds(NT, LV, 2, 8, 128), sds(3, LV, 2, 8, 128)],
        in_specs=own_specs + [SMEM], out_specs=[VMEM] * 4,
        scratch_shapes=OWN_SCRATCH + [
            pltpu.VMEM((NT, LV, 2, 32, 128), F32),
            pltpu.VMEM((LV, PER, 2, 8, 128), F32),
            pltpu.VMEM((7, LV, 2, 16, 128), F32),
            pltpu.VMEM((128, 8, 128), F32)],
        compiler_params=params, name="inner")(*own, reaction)
    o_ref, x_r, x_l = pl.pallas_call(
        strip_pack_kernel, out_shape=[sds(LV + 1, 5, 24, 128), sds(LV + 1, 24, 128), sds(LV + 1, 24, 128)],
        in_specs=own_specs + [VMEM] * 2, out_specs=[VMEM] * 3,
        scratch_shapes=OWN_SCRATCH, compiler_params=params, name="strip_pack")(*own, y_s, y_n)
    tx = lax.axis_size("tx")
    east = [(i, (i + 1) % tx) for i in range(tx)]
    west = [(j, i) for i, j in east]
    x_west = lax.ppermute(x_r, "tx", east)
    x_east = lax.ppermute(x_l, "tx", west)
    edge, edge_f = pl.pallas_call(
        lambda *a: edge_kernel(rows_total, *a),
        out_shape=[sds(NT, LV, 2, 8, 128), sds(3, LV, 2, 8, 128)],
        in_specs=[SMEM, ANY, ANY, VMEM, VMEM, ANY, VMEM, VMEM, SMEM], out_specs=[VMEM] * 2,
        scratch_shapes=[
            pltpu.VMEM((ITERS, NT, LV, 2, 16, 128), F32),
            pltpu.VMEM((ITERS, 3, LV, 2, 16, 128), F32),
            pltpu.VMEM((LV, 2, 32, 128), F32),
            pltpu.VMEM((2, 32, 128), jnp.int32),
            pltpu.VMEM((LV, PER, 2, 8, 128), F32),
            pltpu.VMEM((7, LV, 2, 8, 128), F32),
            pltpu.VMEM((128, 8, 128), F32),
            pltpu.SemaphoreType.DMA((10,))],
        compiler_params=params, name="edge")(scal, saved, saved_f, y_s, y_n, diffusivity, land_mask, level_count, reaction)
    return pl.pallas_call(
        lambda *a: strip_kernel(rows_total, *a),
        out_shape=[sds(*tracers.shape), sds(*thickness.shape), sds(*velocity.shape)],
        in_specs=[SMEM, VMEM, VMEM, VMEM, SMEM, VMEM, VMEM, VMEM, VMEM], out_specs=[VMEM] * 3,
        scratch_shapes=[
            pltpu.VMEM((4, LV, 40, 128), F32),
            pltpu.VMEM((4, LV, 40, 128), F32),
            pltpu.VMEM((LV, 40, 128), F32),
            pltpu.VMEM((LV, 40, 128), F32),
            pltpu.VMEM((LV, 40, 128), F32),
            pltpu.VMEM((LV, 40, 128), F32),
            pltpu.VMEM((40, 128), jnp.int32),
            pltpu.VMEM((LV, 4, 8, 128), F32),
            pltpu.VMEM((7, LV, 24, 128), F32),
            pltpu.VMEM((32, 8, 128), F32)],
        compiler_params=params, name="strips")(scal, o_ref, x_west, x_east, reaction, mid, mid_f, edge, edge_f)


def solution(mesh):
    placed = (
        P("set", None, "ty", "tx"),
        P("set", "ty", "tx"),
        P(None, "set", "ty", "tx"),
        P(None, "ty", "tx"),
        P("set", None, None),
        P("ty", "tx"),
        P("ty", "tx"),
    )

    def whole(*args):
        return tuple(body(*args))

    return jax.shard_map(
        whole,
        mesh=mesh,
        in_specs=placed,
        out_specs=(P("set", None, "ty", "tx"), P("set", "ty", "tx"), P(None, "set", "ty", "tx")),
        check_vma=False,
    )
```

time: 516 us -> 208 us (0.40); the launches traced: 506 us -> 208 us
  Pallas kernels: 0 us -> 160 us
  other arithmetic: 135 us -> 0.55 us
  starting transfers between devices: 133 us -> 16.1 us
  local copies, waits for them, and re-layouts: 89.3 us -> 3.19 us
  blocking collectives: 69.6 us -> 0 us
  waiting for transfers between devices: 56.4 us -> 27.2 us
  matrix products: 17.6 us -> 0 us
    pallas_call x0 -> x5, Pallas kernels: none -> 160 us  [the longest x1 54.4 us: body(): pl.pallas_call(lambda *a: inner_kernel(rows_total, *a), out_shape=[sds(IT...]
    ppermute x52 -> x6, starting transfers between devices: 133 us -> 16.1 us  [the longest x1 6.46 us: body(): y_s = lax.ppermute(y_up, 'ty', north)]
    all_gather x8 -> x0, blocking collectives: 69.6 us -> none  [the longest x4 51.5 us: body(): lax.all_gather(flux_pad, 'set', axis=1, tiled=True)]
    sub x12 -> x0, other arithmetic: 54.9 us -> none  [the longest x4 50.6 us: tracer_update(): thickness * center]
    mul x56 -> x0, other arithmetic: 48 us -> none  [the longest x39 24.2 us: column_mix(): result[level] = solved[level] + ratios[level] * result[level + 1]]
    slice x16 -> x0, local copies, waits for them, and re-layouts: 30.9 us -> none  [the longest x12 19.4 us: extended(): last = lax.slice_in_dim(shard, length - width, length, axis=dim)]
    ppermute x52 -> x6, waiting for transfers between devices: 56.4 us -> 27.2 us  [the longest x1 13 us: body(): y_s = lax.ppermute(y_up, 'ty', north)]
    ppermute x8 -> x0, local copies, waits for them, and re-layouts: 24.9 us -> none  [the longest x4 15.1 us: extended(): before = lax.ppermute(last, axis, up)]
  transfers between devices with their start and end apart: 52 -> 6, of which waited for: 21 -> 3; matrix products, arithmetic and copies ran while one was open for 17% -> 0% of each run, Pallas kernels for 0% -> 44%
where the time goes in v1:
time: 208 us
  Pallas kernels  160 us (77%)
  waiting for transfers between devices  27.2 us (13%)
  starting transfers between devices  16.1 us (8%)
  local copies, waits for them, and re-layouts  3.19 us (2%)
    pallas_call x1, Pallas kernels, body(): pl.pallas_call(lambda *a: inner_kernel(rows_total, *a), out_shape=[sds(IT...  54.4 us
    pallas_call x1, Pallas kernels, body(): pl.pallas_call(lambda *a: strip_kernel(rows_total, *a), out_shape=[sds(*t...  52.6 us
    pallas_call x1, Pallas kernels, body(): pl.pallas_call(lambda *a: edge_kernel(rows_total, *a), out_shape=[sds(NT,...  36.5 us
    ppermute x1, waiting for transfers between devices, body(): y_s = lax.ppermute(y_up, 'ty', north)  13 us
    pallas_call x1, Pallas kernels, body(): pl.pallas_call(strip_pack_kernel, out_shape=[sds(LV + 1, 5, 24, 128), sds...  10.9 us
    ppermute x1, waiting for transfers between devices, body(): h_pair = lax.ppermute(thickness, 'set', swap)  8.38 us
    ppermute x1, starting transfers between devices, body(): y_s = lax.ppermute(y_up, 'ty', north)  6.46 us
    ppermute x1, waiting for transfers between devices, body(): y_n = lax.ppermute(y_dn, 'ty', south)  5.79 us
  transfers between devices with their start and end apart: 6, of which 3 were waited for; matrix products, arithmetic and copies ran while one was open for 0% of the time, Pallas kernels for 44%

profile of v1, /device:TPU:1, one launch (start us, length us, event | category | flops | bytes accessed | tf_op | source)
XLA Modules:
  0.0 207.6 jit_solution(17990644009076781681)
XLA Ops:
  0.6 2.5 %collective-permute-start.1 = (f32[2,8,16,256]{3,2,1,0:T(8,128)}, f32[2,8,16,256]{3,2,1,0:T(8,128)S(1)}, u32[]{:S(2)}, u32[]{:S(2)}) collective-permute-start(f32[2,8,16,256]{3,2,1,0:T(8,128)} %a_4_.2), channel_id=1, source_target_pairs={{0,64},{64,0},{1,65},{65,1},{2,66},{66,2},{3,67},{67,3},{4,68},{68... | collective-permute-start | bytes 786440 | tf_op jit(solution)/shard_map/ppermute | solution.py:603
  3.2 0.1 collective-permute-start
  3.3 0.6 pad_add_fusion.scal.a_0_
  3.8 8.4 %collective-permute-done.hp.a_3_ = f32[8,16,256]{2,1,0:T(8,128)S(1)} collective-permute-done((f32[8,16,256]{2,1,0:T(8,128)}, f32[8,16,256]{2,1,0:T(8,128)S(1)}, u32[]{:S(2)}, u32[]{:S(2)}) %collective-permute-start) | collective-permute-done | bytes 131104 | tf_op jit(solution)/shard_map/ppermute | solution.py:602
  12.2 0.0 copy-start.3
  12.2 0.0 collective-permute-done.1.vp.a_5_
  12.2 0.7 copy-done.3
  12.9 0.0 copy-start.2
  12.9 0.7 copy-done.2
  13.6 5.5 %edge_rows.1 = (f32[161,2,8,128]{3,2,1,0:T(8,128)}, f32[161,2,8,128]{3,2,1,0:T(8,128)}) custom-call(s32[2]{0:T(128)} %pad_add_fusion.scal.a_0_, f32[16,16,16,256]{3,2,1,0:T(8,128)} %a_1_.1, f32[8,16,256]{2,1,0:T(8,128)} %a_2_.1, f32[8,16,256]{2,1,0:T(8,128)} %copy-done.3, f32[2,8,16,256]{3,2,1,0:T(8,128)} %a_4_.2, f32[2,8,16,256]{3,2,1,0:T(8,128)} %copy-done.2, ...), custom_call_target="tpu_custom_call" | custom-call | tf_op jit(solution)/shard_map/edge_rows/pallas_call | solution.py:607
  19.1 6.5 %collective-permute-start.2 = (f32[161,2,8,128]{3,2,1,0:T(8,128)}, f32[161,2,8,128]{3,2,1,0:T(8,128)S(1)}, u32[]{:S(2)}, u32[]{:S(2)}) collective-permute-start(f32[161,2,8,128]{3,2,1,0:T(8,128)} %get-tuple-element.14), channel_id=1, source_target_pairs={{0,1},{1,2},{2,3},{4,5},{5,6},{6,7},{8,9},{9,10},{10,11},{12,13},{... | collective-permute-start | bytes 3956744 | tf_op jit(solution)/shard_map/ppermute | solution.py:613
  25.6 1.9 collective-permute-start.3
  27.5 13.0 %collective-permute-done.2.y_s.a_3_ = f32[161,2,8,128]{3,2,1,0:T(8,128)S(1)} collective-permute-done((f32[161,2,8,128]{3,2,1,0:T(8,128)}, f32[161,2,8,128]{3,2,1,0:T(8,128)S(1)}, u32[]{:S(2)}, u32[]{:S(2)}) %collective-permute-start.2) | collective-permute-done | bytes 1318944 | tf_op jit(solution)/shard_map/ppermute | solution.py:613
  40.5 0.0 copy-start
  40.5 5.8 %collective-permute-done.3.y_n.a_4_ = f32[161,2,8,128]{3,2,1,0:T(8,128)S(1)} collective-permute-done((f32[161,2,8,128]{3,2,1,0:T(8,128)}, f32[161,2,8,128]{3,2,1,0:T(8,128)S(1)}, u32[]{:S(2)}, u32[]{:S(2)}) %collective-permute-start.3) | collective-permute-done | bytes 1318944 | tf_op jit(solution)/shard_map/ppermute | solution.py:614
  46.3 0.0 copy-done
  46.3 0.0 copy-start.1
  46.3 1.1 copy-done.1
  47.4 10.9 %strip_pack.1 = (f32[17,5,24,128]{3,2,1,0:T(8,128)}, f32[17,24,128]{2,1,0:T(8,128)}, f32[17,24,128]{2,1,0:T(8,128)}) custom-call(s32[2]{0:T(128)} %pad_add_fusion.scal.a_0_, f32[16,16,16,256]{3,2,1,0:T(8,128)} %a_1_.1, f32[8,16,256]{2,1,0:T(8,128)} %a_2_.1, f32[8,16,256]{2,1,0:T(8,128)} %copy-done.3, f32[2,8,16,256]{3,2,1,0:T(8,128)} %a_4_.2, ...), custom_call_target="tpu_custom_call" | custom-call | tf_op jit(solution)/shard_map/strip_pack/pallas_call | solution.py:625
  58.3 1.4 collective-permute-start.4
  59.7 3.7 %collective-permute-start.5 = (f32[17,24,128]{2,1,0:T(8,128)}, f32[17,24,128]{2,1,0:T(8,128)S(1)}, u32[]{:S(2)}, u32[]{:S(2)}) collective-permute-start(f32[17,24,128]{2,1,0:T(8,128)} %get-tuple-element.18), channel_id=1, source_target_pairs={{4,0},{8,4},{12,8},{16,12},{20,16},{24,20},{28,24},{32,28},{36,32}... | collective-permute-start | bytes 626696 | tf_op jit(solution)/shard_map/ppermute | solution.py:633
  63.4 54.4 %inner.1 = (f32[4,16,16,2,8,128]{5,4,3,2,1,0:T(8,128)}, f32[4,3,16,2,8,128]{5,4,3,2,1,0:T(8,128)}, f32[16,16,2,8,128]{4,3,2,1,0:T(8,128)}, f32[3,16,2,8,128]{4,3,2,1,0:T(8,128)}) custom-call(s32[2]{0:T(128)} %pad_add_fusion.scal.a_0_, f32[16,16,16,256]{3,2,1,0:T(8,128)} %a_1_.1, f32[8,16,256]{2,1,0:T(8,128)} %a_2_.1, f32[8,16,256]{2,1,0:T(8,128)} %copy-done.3, ...), custom_call_target="tpu_custom_call" | custom-call | tf_op jit(solution)/shard_map/inner/pallas_call | solution.py:615
  117.7 36.5 %edge.1 = (f32[16,16,2,8,128]{4,3,2,1,0:T(8,128)}, f32[3,16,2,8,128]{4,3,2,1,0:T(8,128)}) custom-call(s32[2]{0:T(128)} %pad_add_fusion.scal.a_0_, f32[4,16,16,2,8,128]{5,4,3,2,1,0:T(8,128)} %get-tuple-element.21.a_1_, f32[4,3,16,2,8,128]{5,4,3,2,1,0:T(8,128)} %get-tuple-element.22.a_2_, f32[161,2,8,128]{3,2,1,0:T(8,128)} %copy-done, ...), custom_call_target="tpu_custom_call" | custom-call | tf_op jit(solution)/shard_map/edge/pallas_call | solution.py:634
  154.2 0.0 collective-permute-done.4.a_2_
  154.2 0.0 copy-start.4
  154.3 0.0 collective-permute-done.5.a_3_
  154.3 0.0 copy-start.5
  154.3 0.6 copy-done.4
  154.9 0.1 copy-done.5
  155.0 52.6 %strips.1 = (f32[16,16,16,256]{3,2,1,0:T(8,128)}, f32[8,16,256]{2,1,0:T(8,128)}, f32[2,8,16,256]{3,2,1,0:T(8,128)}) custom-call(s32[2]{0:T(128)} %pad_add_fusion.scal.a_0_, f32[17,5,24,128]{3,2,1,0:T(8,128)} %get-tuple-element.16.a_1_, f32[17,24,128]{2,1,0:T(8,128)} %copy-done.4, f32[17,24,128]{2,1,0:T(8,128)} %copy-done.5, f32[2,8,8]{2,1,0:T(8,128)} %a_4_.3, ...), custom_call_target="tpu_custom_call" | custom-call | tf_op jit(solution)/shard_map/strips/pallas_call | solution.py:648
Async XLA Ops:
  0.6 11.6 %collective-permute-start.1 = (f32[2,8,16,256]{3,2,1,0:T(8,128)}, f32[2,8,16,256]{3,2,1,0:T(8,128)S(1)}, u32[]{:S(2)}, u32[]{:S(2)}) collective-permute-start(f32[2,8,16,256]{3,2,1,0:T(8,128)} %a_4_.2), channel_id=1, source_target_pairs={{0,64},{64,0},{1,65},{65,1},{2,66},{66,2},{3,67},{67,3},{4,68},{68... | collective-permute-start | bytes 786440 | tf_op jit(solution)/shard_map/ppermute | solution.py:603
  3.2 9.0 %collective-permute-start = (f32[8,16,256]{2,1,0:T(8,128)}, f32[8,16,256]{2,1,0:T(8,128)S(1)}, u32[]{:S(2)}, u32[]{:S(2)}) collective-permute-start(f32[8,16,256]{2,1,0:T(8,128)} %a_2_.1), channel_id=1, source_target_pairs={{0,64},{64,0},{1,65},{65,1},{2,66},{66,2},{3,67},{67,3},{4,68},{68... | collective-permute-start | bytes 393224 | tf_op jit(solution)/shard_map/ppermute | solution.py:602
  12.2 0.7 copy-start.3
  12.9 0.7 copy-start.2
  19.1 21.4 %collective-permute-start.2 = (f32[161,2,8,128]{3,2,1,0:T(8,128)}, f32[161,2,8,128]{3,2,1,0:T(8,128)S(1)}, u32[]{:S(2)}, u32[]{:S(2)}) collective-permute-start(f32[161,2,8,128]{3,2,1,0:T(8,128)} %get-tuple-element.14), channel_id=1, source_target_pairs={{0,1},{1,2},{2,3},{4,5},{5,6},{6,7},{8,9},{9,10},{10,11},{12,13},{... | collective-permute-start | bytes 3956744 | tf_op jit(solution)/shard_map/ppermute | solution.py:613
  25.6 20.7 %collective-permute-start.3 = (f32[161,2,8,128]{3,2,1,0:T(8,128)}, f32[161,2,8,128]{3,2,1,0:T(8,128)S(1)}, u32[]{:S(2)}, u32[]{:S(2)}) collective-permute-start(f32[161,2,8,128]{3,2,1,0:T(8,128)} %get-tuple-element.15), channel_id=1, source_target_pairs={{1,0},{2,1},{3,2},{5,4},{6,5},{7,6},{9,8},{10,9},{11,10},{13,12},{... | collective-permute-start | bytes 3956744 | tf_op jit(solution)/shard_map/ppermute | solution.py:614
  40.5 5.8 %copy-start = (f32[161,2,8,128]{3,2,1,0:T(8,128)}, f32[161,2,8,128]{3,2,1,0:T(8,128)S(1)}, u32[]{:S(2)}) copy-start(f32[161,2,8,128]{3,2,1,0:T(8,128)S(1)} %collective-permute-done.2.y_s.a_3_) | copy-start | bytes 3956740
  46.3 1.1 copy-start.1
  58.3 95.9 %collective-permute-start.4 = (f32[17,24,128]{2,1,0:T(8,128)}, f32[17,24,128]{2,1,0:T(8,128)S(1)}, u32[]{:S(2)}, u32[]{:S(2)}) collective-permute-start(f32[17,24,128]{2,1,0:T(8,128)} %get-tuple-element.17), channel_id=1, source_target_pairs={{0,4},{4,8},{8,12},{12,16},{16,20},{20,24},{24,28},{28,32},{32,36}... | collective-permute-start | bytes 626696 | tf_op jit(solution)/shard_map/ppermute | solution.py:632
  59.7 94.6 %collective-permute-start.5 = (f32[17,24,128]{2,1,0:T(8,128)}, f32[17,24,128]{2,1,0:T(8,128)S(1)}, u32[]{:S(2)}, u32[]{:S(2)}) collective-permute-start(f32[17,24,128]{2,1,0:T(8,128)} %get-tuple-element.18), channel_id=1, source_target_pairs={{4,0},{8,4},{12,8},{16,12},{20,16},{24,20},{28,24},{32,28},{36,32}... | collective-permute-start | bytes 626696 | tf_op jit(solution)/shard_map/ppermute | solution.py:633
  154.2 0.7 copy-start.4
  154.3 0.8 copy-start.5

commit v2 on v1

--- a/solution.py
+++ b/solution.py
@@ -27,17 +27,17 @@
     return lax.broadcasted_iota(jnp.int32, (rows, 128), 1)
 
 
-def from_east(tiles):
+def from_east(tiles, joined=True):
     rolled = [pltpu.roll(x, 127, 1) for x in tiles]
     lane = lane_iota(tiles[0].shape[0])
     last = len(tiles) - 1
-    return [rolled[i] if i == last else jnp.where(lane == 127, rolled[i + 1], rolled[i]) for i in range(last + 1)]
-
-
-def from_west(tiles):
+    return [rolled[i] if i == last or not joined else jnp.where(lane == 127, rolled[i + 1], rolled[i]) for i in range(last + 1)]
+
+
+def from_west(tiles, joined=True):
     rolled = [pltpu.roll(x, 1, 1) for x in tiles]
     lane = lane_iota(tiles[0].shape[0])
-    return [rolled[i] if i == 0 else jnp.where(lane == 0, rolled[i - 1], rolled[i]) for i in range(len(tiles))]
+    return [rolled[i] if i == 0 or not joined else jnp.where(lane == 0, rolled[i - 1], rolled[i]) for i in range(len(tiles))]
 
 
 def coriolis_of(row, rows_total):
@@ -80,11 +80,11 @@
     return h_new, u_new, v_new, coefs, links, ratios
 
 
-def forward(k, coefs, cells, before):
+def forward(coefs, cells, before, joined=True):
     result = []
     for t, (c, s, n) in enumerate(cells):
-        e = from_east(c)
-        w = from_west(c)
+        e = from_east(c, joined)
+        w = from_west(c, joined)
         result.append([
             ((coefs[0][j] * c[j] + coefs[1][j] * e[j]) + (coefs[2][j] * w[j] + coefs[3][j] * n[j]))
             + (coefs[4][j] * s[j] + coefs[5][j] * before[t][j])
@@ -171,7 +171,7 @@
         y_up[index, j] = jnp.where(low, first(20), second(16))
         y_dn[index, j] = jnp.where(low, first(8), second(4))
 
-    @pl.loop(0, LV)
+    @pl.loop(0, LV, unroll=2)
     def _(k):
         for j in range(2):
             for t in range(PER):
@@ -184,8 +184,8 @@
         put(160, j, get, get)
 
 
-def inner_kernel(rows_total, scal, tr, ho, hp, vo, vp, df, land, level, reaction, saved, saved_f, mid, mid_f,
-                 c_buf, h_buf, u_buf, v_buf, d_buf, p_buf, sem, c_alt, solved, coef, table):
+def inner_kernel(rows_total, scal, tr, ho, hp, vo, vp, df, land, level, reaction, saved_out, saved_f, mid, mid_f,
+                 c_buf, h_buf, u_buf, v_buf, d_buf, p_buf, sem, c_alt, solved, coef, table, saved, out_sem):
     off = scal[0] * (LV // 2)
     fields, tracer = own_copies(tr, ho, hp, vo, vp, df, off, c_buf, h_buf, u_buf, v_buf, d_buf, sem)
     for c in fields + tracer:
@@ -224,6 +224,8 @@
     for c in tracer:
         c.wait()
     keep_tracers(0, c_buf)
+    leaving = [pltpu.make_async_copy(saved.at[n], saved_out.at[n], out_sem.at[n]) for n in range(ITERS)]
+    leaving[0].start()
     for n in range(1, ITERS + 1):
         src, dst = (c_buf, c_alt) if n % 2 else (c_alt, c_buf)
 
@@ -241,7 +243,7 @@
                     coef[c, k, j] = co[j][c]
             return links, ratios
 
-        lax.fori_loop(0, LV, dynamics, (zeros_like_tiles(16, 2), zeros_like_tiles(16, 2)))
+        lax.fori_loop(0, LV, dynamics, (zeros_like_tiles(16, 2), zeros_like_tiles(16, 2)), unroll=4)
         if n < ITERS:
             keep_fields(n)
         else:
@@ -257,13 +259,13 @@
                 def down(k, before):
                     co = [[coef[c, k, j, r0 - 8:r0, :] for j in range(2)] for c in range(6)]
                     read = lambda t, r: [src[s * PER + t, k, j, r:r + 8, :] for j in range(2)]
-                    now = forward(k, co, [(read(t, r0), read(t, r0 - 1), read(t, r0 + 1)) for t in range(PER)], before)
+                    now = forward(co, [(read(t, r0), read(t, r0 - 1), read(t, r0 + 1)) for t in range(PER)], before)
                     for t in range(PER):
                         for j in range(2):
                             solved[k, t, j] = now[t][j]
                     return now
 
-                lax.fori_loop(0, LV, down, [zeros_like_tiles(8, 2) for _ in range(PER)])
+                lax.fori_loop(0, LV, down, [zeros_like_tiles(8, 2) for _ in range(PER)], unroll=8)
 
                 def upward(i, m):
                     k = LV - 1 - i
@@ -278,9 +280,12 @@
                                 mid[s * PER + t, k, j] = outs[t][j]
                     return m
 
-                lax.fori_loop(0, LV, upward, [zeros_like_tiles(8, 2) for _ in range(PER)])
+                lax.fori_loop(0, LV, upward, [zeros_like_tiles(8, 2) for _ in range(PER)], unroll=4)
         if n < ITERS:
             keep_tracers(n, dst)
+            leaving[n].start()
+    for c in leaving:
+        c.wait()
 
 
 def strip_pack_kernel(scal, tr, ho, hp, vo, vp, df, land, level, y_s, y_n, o_ref, x_r, x_l,
@@ -317,7 +322,7 @@
                 acc[i] = x if acc[i] is None else jnp.where(slot == q, x, acc[i])
         return acc
 
-    @pl.loop(0, LV)
+    @pl.loop(0, LV, unroll=2)
     def _(k):
         def tracer_source(t):
             return (lambda j, r: c_buf[t, k, j, r:r + 8, :], (t % PER) * LV + k, t // PER)
@@ -372,7 +377,7 @@
         else:
             pltpu.store(ref.at[pl.ds(4, 8), :], y, mask=jnp.logical_not(low))
 
-    @pl.loop(0, LV)
+    @pl.loop(0, LV, unroll=2)
     def _(k):
         for j in range(2):
             for t in range(PER):
@@ -428,7 +433,7 @@
                     coef[c, k, j] = co[j][c]
             return links, ratios
 
-        lax.fori_loop(0, LV, dynamics, (zeros_like_tiles(8, 2), zeros_like_tiles(8, 2)))
+        lax.fori_loop(0, LV, dynamics, (zeros_like_tiles(8, 2), zeros_like_tiles(8, 2)), unroll=8)
 
         @pl.loop(0, 2)
         def _(s):
@@ -438,13 +443,13 @@
                 def read(t, shift):
                     return [gather(lambda r: c_buf[n - 1, s * PER + t, k, j, r:r + 8, :], shift) for j in range(2)]
 
-                now = forward(k, co, [(read(t, 1), read(t, 0), read(t, 2)) for t in range(PER)], before)
+                now = forward(co, [(read(t, 1), read(t, 0), read(t, 2)) for t in range(PER)], before)
                 for t in range(PER):
                     for j in range(2):
                         solved[k, t, j] = now[t][j]
                 return now
 
-            lax.fori_loop(0, LV, down, [zeros_like_tiles(8, 2) for _ in range(PER)])
+            lax.fori_loop(0, LV, down, [zeros_like_tiles(8, 2) for _ in range(PER)], unroll=8)
 
             def upward(i, m):
                 k = LV - 1 - i
@@ -460,7 +465,7 @@
                             out_c[s * PER + t, k, j] = outs[t][j]
                 return m
 
-            lax.fori_loop(0, LV, upward, [zeros_like_tiles(8, 2) for _ in range(PER)])
+            lax.fori_loop(0, LV, upward, [zeros_like_tiles(8, 2) for _ in range(PER)], unroll=4)
 
 
 def strip_kernel(rows_total, scal, o_ref, x_r, x_l, reaction, mid, mid_f, edge, edge_f, out_c, out_h, out_v,
@@ -486,7 +491,7 @@
         b = pltpu.roll(x_l[k, rows, :], (28 - 4 * xg) % 128, 1)
         return jnp.where(place < 4, a, jnp.where(place >= 28, b, o_ref[k, g, rows, :]))
 
-    @pl.loop(0, LV)
+    @pl.loop(0, LV, unroll=4)
     def _(k):
         for i in range(3):
             for g in range(4):
@@ -525,24 +530,28 @@
                 coef[c, k] = co[0][c]
             return links, ratios
 
-        lax.fori_loop(0, LV, dynamics, (zeros_like_tiles(24, 1), zeros_like_tiles(24, 1)))
-
-        for r0 in ((8, 16, 24) if n < ITERS else (12, 20)):
-            def down(k, before):
-                co = [[coef[c, k, r0 - 8:r0, :]] for c in range(6)]
-                read = lambda t, r: [src[t, k, r:r + 8, :]]
-                now = forward(k, co, [(read(t, r0), read(t, r0 - 1), read(t, r0 + 1)) for t in range(4)], before)
-                for t in range(4):
-                    solved[k, t] = now[t][0]
-                return now
-
-            lax.fori_loop(0, LV, down, [zeros_like_tiles(8, 1) for _ in range(4)])
-
-            def upward(i, m):
-                k = LV - 1 - i
-                r = coef[6, k, r0 - 8:r0, :]
-                m = [solved[k, t] + r * m[t] for t in range(4)]
-                turned = [[x] + [pltpu.roll(x, 32 * rho, 1) for rho in range(1, 4)] for x in m]
+        lax.fori_loop(0, LV, dynamics, (zeros_like_tiles(24, 1), zeros_like_tiles(24, 1)), unroll=8)
+
+        starts = (8, 16, 24) if n < ITERS else (12, 20)
+        tiles = len(starts)
+
+        def down(k, before):
+            co = [[coef[c, k, r0 - 8:r0, :] for r0 in starts] for c in range(6)]
+            read = lambda t, shift: [src[t, k, r0 + shift:r0 + shift + 8, :] for r0 in starts]
+            now = forward(co, [(read(t, 0), read(t, -1), read(t, 1)) for t in range(4)], before, joined=False)
+            for t in range(4):
+                for i in range(tiles):
+                    solved[k, t, i] = now[t][i]
+            return now
+
+        lax.fori_loop(0, LV, down, [zeros_like_tiles(8, tiles) for _ in range(4)], unroll=4)
+
+        def upward(i, m):
+            k = LV - 1 - i
+            r = [coef[6, k, r0 - 8:r0, :] for r0 in starts]
+            m = [[solved[k, t, i] + r[i] * m[t][i] for i in range(tiles)] for t in range(4)]
+            for i, r0 in enumerate(starts):
+                turned = [[m[t][i]] + [pltpu.roll(m[t][i], 32 * rho, 1) for rho in range(1, 4)] for t in range(4)]
                 for s in range(2):
                     for go in range(2):
                         acc = None
@@ -551,9 +560,9 @@
                                 term = table[((s * 2 + go) * 2 + gi) * 4 + rho] * turned[2 * s + gi][rho]
                                 acc = term if acc is None else acc + term
                         dst[2 * s + go, k, r0:r0 + 8, :] = acc
-                return m
-
-            lax.fori_loop(0, LV, upward, [jnp.zeros((8, 128), F32) for _ in range(4)])
+            return m
+
+        lax.fori_loop(0, LV, upward, [zeros_like_tiles(8, tiles) for _ in range(4)], unroll=4)
 
     final = c_buf if ITERS % 2 == 0 else c_alt
 
@@ -564,7 +573,7 @@
             return jnp.where(lane < 4, pltpu.roll(strip, (-(32 * q + 4)) % 128, 1), body)
         return jnp.where(lane >= 124, pltpu.roll(strip, (100 - 32 * q) % 128, 1), body)
 
-    @pl.loop(0, LV)
+    @pl.loop(0, LV, unroll=2)
     def _(k):
         for t in range(NT):
             for i in range(2):
@@ -575,7 +584,7 @@
 
     off = scal[0] * (LV // 2)
 
-    @pl.loop(0, LV // 2)
+    @pl.loop(0, LV // 2, unroll=4)
     def _(k):
         for f, buf in enumerate((h_buf, u_buf, v_buf)):
             for i in range(2):
@@ -615,13 +624,16 @@
     saved, saved_f, mid, mid_f = pl.pallas_call(
         lambda *a: inner_kernel(rows_total, *a),
         out_shape=[sds(ITERS, NT, LV, 2, 8, 128), sds(ITERS, 3, LV, 2, 8, 128), sds(NT, LV, 2, 8, 128), sds(3, LV, 2, 8, 128)],
-        in_specs=own_specs + [SMEM], out_specs=[VMEM] * 4,
+        in_specs=own_specs + [SMEM], out_specs=[ANY] + [VMEM] * 3,
         scratch_shapes=OWN_SCRATCH + [
             pltpu.VMEM((NT, LV, 2, 32, 128), F32),
             pltpu.VMEM((LV, PER, 2, 8, 128), F32),
             pltpu.VMEM((7, LV, 2, 16, 128), F32),
-            pltpu.VMEM((128, 8, 128), F32)],
+            pltpu.VMEM((128, 8, 128), F32),
+            pltpu.VMEM((ITERS, NT, LV, 2, 8, 128), F32),
+            pltpu.SemaphoreType.DMA((ITERS,))],
         compiler_params=params, name="inner")(*own, reaction)
+    y_s, y_n, mid_f = lax.optimization_barrier((y_s, y_n, mid_f))
     o_ref, x_r, x_l = pl.pallas_call(
         strip_pack_kernel, out_shape=[sds(LV + 1, 5, 24, 128), sds(LV + 1, 24, 128), sds(LV + 1, 24, 128)],
         in_specs=own_specs + [VMEM] * 2, out_specs=[VMEM] * 3,
@@ -657,7 +669,7 @@
             pltpu.VMEM((LV, 40, 128), F32),
             pltpu.VMEM((LV, 40, 128), F32),
             pltpu.VMEM((40, 128), jnp.int32),
-            pltpu.VMEM((LV, 4, 8, 128), F32),
+            pltpu.VMEM((LV, 4, 3, 8, 128), F32),
             pltpu.VMEM((7, LV, 24, 128), F32),
             pltpu.VMEM((32, 8, 128), F32)],
         compiler_params=params, name="strips")(scal, o_ref, x_west, x_east, reaction, mid, mid_f, edge, edge_f)

time: 208 us -> 115 us (0.55)
  Pallas kernels: 160 us -> 85.6 us
  waiting for transfers between devices: 27.2 us -> 8.4 us
    pallas_call x1, Pallas kernels: 52.6 us -> 17.6 us  [body(): pl.pallas_call(lambda *a: strip_kernel(rows_total, *a), out_shape=[sds(*t...]
    pallas_call x1, Pallas kernels: 54.4 us -> 30.7 us  [body(): pl.pallas_call(lambda *a: inner_kernel(rows_total, *a), out_shape=[sds(IT...]
    pallas_call x1, Pallas kernels: 36.5 us -> 19.7 us  [body(): pl.pallas_call(lambda *a: edge_kernel(rows_total, *a), out_shape=[sds(NT,...]
    ppermute x1, waiting for transfers between devices: 13 us -> 0.01 us  [body(): y_s = lax.ppermute(y_up, 'ty', north)]
    ppermute x1, waiting for transfers between devices: 5.79 us -> 0.01 us  [body(): y_n = lax.ppermute(y_dn, 'ty', south)]
  transfers between devices with their start and end apart: 6 -> 6, of which waited for: 3 -> 1; matrix products, arithmetic and copies ran while one was open for 0% -> 0% of each run, Pallas kernels for 44% -> 44%
where the time goes in v2:
time: 115 us
  Pallas kernels  85.6 us (74%)
  starting transfers between devices  16.3 us (14%)
  waiting for transfers between devices  8.4 us (7%)
  local copies, waits for them, and re-layouts  3.56 us (3%)
    pallas_call x1, Pallas kernels, body(): pl.pallas_call(lambda *a: inner_kernel(rows_total, *a), out_shape=[sds(IT...  30.7 us
    pallas_call x1, Pallas kernels, body(): pl.pallas_call(lambda *a: edge_kernel(rows_total, *a), out_shape=[sds(NT,...  19.7 us
    pallas_call x1, Pallas kernels, body(): pl.pallas_call(lambda *a: strip_kernel(rows_total, *a), out_shape=[sds(*t...  17.6 us
    pallas_call x1, Pallas kernels, body(): pl.pallas_call(strip_pack_kernel, out_shape=[sds(LV + 1, 5, 24, 128), sds...  12.1 us
    ppermute x1, waiting for transfers between devices, body(): h_pair = lax.ppermute(thickness, 'set', swap)  8.38 us
    ppermute x1, starting transfers between devices, body(): y_s = lax.ppermute(y_up, 'ty', north)  6.46 us
    pallas_call x1, Pallas kernels, body(): pl.pallas_call(rows_kernel, out_shape=[sds(161, 2, 8, 128)] * 2, in_specs...  5.5 us
    ppermute x1, starting transfers between devices, body(): x_east = lax.ppermute(x_l, 'tx', west)  3.89 us
  transfers between devices with their start and end apart: 6, of which 1 were waited for; matrix products, arithmetic and copies ran while one was open for 0% of the time, Pallas kernels for 44%

profile of v2, /device:TPU:1, one launch (start us, length us, event | category | flops | bytes accessed | tf_op | source)
XLA Modules:
  0.0 115.1 jit_solution(3789243829825254060)
XLA Ops:
  0.6 2.5 %collective-permute-start.1 = (f32[2,8,16,256]{3,2,1,0:T(8,128)}, f32[2,8,16,256]{3,2,1,0:T(8,128)S(1)}, u32[]{:S(2)}, u32[]{:S(2)}) collective-permute-start(f32[2,8,16,256]{3,2,1,0:T(8,128)} %vo.3), channel_id=1, source_target_pairs={{0,64},{64,0},{1,65},{65,1},{2,66},{66,2},{3,67},{67,3},{4,68},{68... | collective-permute-start | bytes 786440 | tf_op jit(solution)/shard_map/ppermute | solution.py:612
  3.2 0.1 collective-permute-start
  3.3 0.6 pad_add_fusion.scal.a_0_
  3.8 8.4 %collective-permute-done.hp.a_3_ = f32[8,16,256]{2,1,0:T(8,128)S(1)} collective-permute-done((f32[8,16,256]{2,1,0:T(8,128)}, f32[8,16,256]{2,1,0:T(8,128)S(1)}, u32[]{:S(2)}, u32[]{:S(2)}) %collective-permute-start) | collective-permute-done | bytes 131104 | tf_op jit(solution)/shard_map/ppermute | solution.py:611
  12.2 0.0 copy-start.3
  12.2 0.0 collective-permute-done.1.vp.a_5_
  12.2 0.7 copy-done.3
  12.9 0.0 copy-start.2
  12.9 0.7 copy-done.2
  13.6 5.5 %edge_rows.1 = (f32[161,2,8,128]{3,2,1,0:T(8,128)}, f32[161,2,8,128]{3,2,1,0:T(8,128)}) custom-call(s32[2]{0:T(128)} %pad_add_fusion.scal.a_0_, f32[16,16,16,256]{3,2,1,0:T(8,128)} %tr.3, f32[8,16,256]{2,1,0:T(8,128)} %ho.3, f32[8,16,256]{2,1,0:T(8,128)} %copy-done.3, f32[2,8,16,256]{3,2,1,0:T(8,128)} %vo.3, f32[2,8,16,256]{3,2,1,0:T(8,128)} %copy-done.2, ...), custom_call_target="tpu_custom_call" | custom-call | tf_op jit(solution)/shard_map/edge_rows/pallas_call | solution.py:616
  19.1 6.5 %collective-permute-start.2 = (f32[161,2,8,128]{3,2,1,0:T(8,128)}, f32[161,2,8,128]{3,2,1,0:T(8,128)S(1)}, u32[]{:S(2)}, u32[]{:S(2)}) collective-permute-start(f32[161,2,8,128]{3,2,1,0:T(8,128)} %get-tuple-element.17), channel_id=1, source_target_pairs={{0,1},{1,2},{2,3},{4,5},{5,6},{6,7},{8,9},{9,10},{10,11},{12,13},{... | collective-permute-start | bytes 3956744 | tf_op jit(solution)/shard_map/ppermute | solution.py:622
  25.5 1.9 %collective-permute-start.3 = (f32[161,2,8,128]{3,2,1,0:T(8,128)}, f32[161,2,8,128]{3,2,1,0:T(8,128)S(1)}, u32[]{:S(2)}, u32[]{:S(2)}) collective-permute-start(f32[161,2,8,128]{3,2,1,0:T(8,128)} %get-tuple-element.18), channel_id=1, source_target_pairs={{1,0},{2,1},{3,2},{5,4},{6,5},{7,6},{9,8},{10,9},{11,10},{13,12},{... | collective-permute-start | bytes 3956744 | tf_op jit(solution)/shard_map/ppermute | solution.py:623
  27.5 30.7 %inner.1 = (f32[4,16,16,2,8,128]{5,4,3,2,1,0:T(8,128)}, f32[4,3,16,2,8,128]{5,4,3,2,1,0:T(8,128)}, f32[16,16,2,8,128]{4,3,2,1,0:T(8,128)}, f32[3,16,2,8,128]{4,3,2,1,0:T(8,128)}) custom-call(s32[2]{0:T(128)} %pad_add_fusion.scal.a_0_, f32[16,16,16,256]{3,2,1,0:T(8,128)} %tr.3, f32[8,16,256]{2,1,0:T(8,128)} %ho.3, f32[8,16,256]{2,1,0:T(8,128)} %copy-done.3, ...), custom_call_target="tpu_custom_call" | custom-call | tf_op jit(solution)/shard_map/inner/pallas_call | solution.py:624
  58.2 0.0 collective-permute-done.2.y_s.a_3_
  58.2 0.0 copy-start
  58.2 0.0 collective-permute-done.3.y_n.a_4_
  58.2 0.0 copy-start.1
  58.2 1.1 copy-done
  59.3 0.4 copy-done.1
  59.7 12.1 %strip_pack.1 = (f32[17,5,24,128]{3,2,1,0:T(8,128)}, f32[17,24,128]{2,1,0:T(8,128)}, f32[17,24,128]{2,1,0:T(8,128)}) custom-call(s32[2]{0:T(128)} %pad_add_fusion.scal.a_0_, f32[16,16,16,256]{3,2,1,0:T(8,128)} %tr.3, f32[8,16,256]{2,1,0:T(8,128)} %ho.3, f32[8,16,256]{2,1,0:T(8,128)} %copy-done.3, f32[2,8,16,256]{3,2,1,0:T(8,128)} %vo.3, ...), custom_call_target="tpu_custom_call" | custom-call | tf_op jit(solution)/shard_map/strip_pack/pallas_call | solution.py:637
  71.8 1.4 %collective-permute-start.4 = (f32[17,24,128]{2,1,0:T(8,128)}, f32[17,24,128]{2,1,0:T(8,128)S(1)}, u32[]{:S(2)}, u32[]{:S(2)}) collective-permute-start(f32[17,24,128]{2,1,0:T(8,128)} %get-tuple-element.23), channel_id=1, source_target_pairs={{0,4},{4,8},{8,12},{12,16},{16,20},{20,24},{24,28},{28,32},{32,36}... | collective-permute-start | bytes 626696 | tf_op jit(solution)/shard_map/ppermute | solution.py:644
  73.2 3.9 %collective-permute-start.5 = (f32[17,24,128]{2,1,0:T(8,128)}, f32[17,24,128]{2,1,0:T(8,128)S(1)}, u32[]{:S(2)}, u32[]{:S(2)}) collective-permute-start(f32[17,24,128]{2,1,0:T(8,128)} %get-tuple-element.24), channel_id=1, source_target_pairs={{4,0},{8,4},{12,8},{16,12},{20,16},{24,20},{28,24},{32,28},{36,32}... | collective-permute-start | bytes 626696 | tf_op jit(solution)/shard_map/ppermute | solution.py:645
  77.1 19.7 %edge.1 = (f32[16,16,2,8,128]{4,3,2,1,0:T(8,128)}, f32[3,16,2,8,128]{4,3,2,1,0:T(8,128)}) custom-call(s32[2]{0:T(128)} %pad_add_fusion.scal.a_0_, f32[4,16,16,2,8,128]{5,4,3,2,1,0:T(8,128)} %get-tuple-element.27.a_1_, f32[4,3,16,2,8,128]{5,4,3,2,1,0:T(8,128)} %get-tuple-element.28.a_2_, f32[161,2,8,128]{3,2,1,0:T(8,128)} %copy-done, ...), custom_call_target="tpu_custom_call" | custom-call | tf_op jit(solution)/shard_map/edge/pallas_call | solution.py:646
  96.8 0.0 collective-permute-done.4.a_2_
  96.8 0.0 copy-start.4
  96.8 0.0 collective-permute-done.5.a_3_
  96.8 0.0 copy-start.5
  96.8 0.6 copy-done.4
  97.4 0.1 copy-done.5
  97.5 17.6 %strips.1 = (f32[16,16,16,256]{3,2,1,0:T(8,128)}, f32[8,16,256]{2,1,0:T(8,128)}, f32[2,8,16,256]{3,2,1,0:T(8,128)}) custom-call(s32[2]{0:T(128)} %pad_add_fusion.scal.a_0_, f32[17,5,24,128]{3,2,1,0:T(8,128)} %get-tuple-element.22.a_1_, f32[17,24,128]{2,1,0:T(8,128)} %copy-done.4, f32[17,24,128]{2,1,0:T(8,128)} %copy-done.5, f32[2,8,8]{2,1,0:T(8,128)} %a_4_.3, ...), custom_call_target="tpu_custom_call" | custom-call | tf_op jit(solution)/shard_map/strips/pallas_call | solution.py:660
Async XLA Ops:
  0.6 11.6 %collective-permute-start.1 = (f32[2,8,16,256]{3,2,1,0:T(8,128)}, f32[2,8,16,256]{3,2,1,0:T(8,128)S(1)}, u32[]{:S(2)}, u32[]{:S(2)}) collective-permute-start(f32[2,8,16,256]{3,2,1,0:T(8,128)} %vo.3), channel_id=1, source_target_pairs={{0,64},{64,0},{1,65},{65,1},{2,66},{66,2},{3,67},{67,3},{4,68},{68... | collective-permute-start | bytes 786440 | tf_op jit(solution)/shard_map/ppermute | solution.py:612
  3.2 9.0 %collective-permute-start = (f32[8,16,256]{2,1,0:T(8,128)}, f32[8,16,256]{2,1,0:T(8,128)S(1)}, u32[]{:S(2)}, u32[]{:S(2)}) collective-permute-start(f32[8,16,256]{2,1,0:T(8,128)} %ho.3), channel_id=1, source_target_pairs={{0,64},{64,0},{1,65},{65,1},{2,66},{66,2},{3,67},{67,3},{4,68},{68... | collective-permute-start | bytes 393224 | tf_op jit(solution)/shard_map/ppermute | solution.py:611
  12.2 0.7 copy-start.3
  12.9 0.7 copy-start.2
  19.1 39.1 %collective-permute-start.2 = (f32[161,2,8,128]{3,2,1,0:T(8,128)}, f32[161,2,8,128]{3,2,1,0:T(8,128)S(1)}, u32[]{:S(2)}, u32[]{:S(2)}) collective-permute-start(f32[161,2,8,128]{3,2,1,0:T(8,128)} %get-tuple-element.17), channel_id=1, source_target_pairs={{0,1},{1,2},{2,3},{4,5},{5,6},{6,7},{8,9},{9,10},{10,11},{12,13},{... | collective-permute-start | bytes 3956744 | tf_op jit(solution)/shard_map/ppermute | solution.py:622
  25.5 32.7 %collective-permute-start.3 = (f32[161,2,8,128]{3,2,1,0:T(8,128)}, f32[161,2,8,128]{3,2,1,0:T(8,128)S(1)}, u32[]{:S(2)}, u32[]{:S(2)}) collective-permute-start(f32[161,2,8,128]{3,2,1,0:T(8,128)} %get-tuple-element.18), channel_id=1, source_target_pairs={{1,0},{2,1},{3,2},{5,4},{6,5},{7,6},{9,8},{10,9},{11,10},{13,12},{... | collective-permute-start | bytes 3956744 | tf_op jit(solution)/shard_map/ppermute | solution.py:623
  58.2 1.1 copy-start
  58.2 1.5 %copy-start.1 = (f32[161,2,8,128]{3,2,1,0:T(8,128)}, f32[161,2,8,128]{3,2,1,0:T(8,128)S(1)}, u32[]{:S(2)}) copy-start(f32[161,2,8,128]{3,2,1,0:T(8,128)S(1)} %collective-permute-done.3.y_n.a_4_) | copy-start | bytes 3956740
  71.8 24.9 %collective-permute-start.4 = (f32[17,24,128]{2,1,0:T(8,128)}, f32[17,24,128]{2,1,0:T(8,128)S(1)}, u32[]{:S(2)}, u32[]{:S(2)}) collective-permute-start(f32[17,24,128]{2,1,0:T(8,128)} %get-tuple-element.23), channel_id=1, source_target_pairs={{0,4},{4,8},{8,12},{12,16},{16,20},{20,24},{24,28},{28,32},{32,36}... | collective-permute-start | bytes 626696 | tf_op jit(solution)/shard_map/ppermute | solution.py:644
  73.2 23.6 %collective-permute-start.5 = (f32[17,24,128]{2,1,0:T(8,128)}, f32[17,24,128]{2,1,0:T(8,128)S(1)}, u32[]{:S(2)}, u32[]{:S(2)}) collective-permute-start(f32[17,24,128]{2,1,0:T(8,128)} %get-tuple-element.24), channel_id=1, source_target_pairs={{4,0},{8,4},{12,8},{16,12},{20,16},{24,20},{28,24},{32,28},{36,32}... | collective-permute-start | bytes 626696 | tf_op jit(solution)/shard_map/ppermute | solution.py:645
  96.8 0.7 copy-start.4
  96.8 0.8 copy-start.5

commit v3 on v2

--- a/solution.py
+++ b/solution.py
@@ -117,13 +117,13 @@
     return [jnp.zeros((rows, 128), F32) for _ in range(count)]
 
 
-def own_copies(tr, ho, hp, vo, vp, df, off, c_buf, h_buf, u_buf, v_buf, d_buf, sem):
+def field_copies(ho, hp, vo, vp, df, off, h_buf, u_buf, v_buf, d_buf, sem):
     copies = []
     part = LV // 2
     other = part - off
+    rows = pl.ds(8, 16)
     for j in range(2):
         lanes = pl.ds(128 * j, 128)
-        rows = pl.ds(8, 16)
         copies.append(pltpu.make_async_copy(ho.at[:, :, lanes], h_buf.at[pl.ds(off, part), j, rows, :], sem.at[0 + j]))
         copies.append(pltpu.make_async_copy(hp.at[:, :, lanes], h_buf.at[pl.ds(other, part), j, rows, :], sem.at[2 + j]))
         copies.append(pltpu.make_async_copy(vo.at[0, :, :, lanes], u_buf.at[pl.ds(off, part), j, rows, :], sem.at[4 + j]))
@@ -131,67 +131,144 @@
         copies.append(pltpu.make_async_copy(vo.at[1, :, :, lanes], v_buf.at[pl.ds(off, part), j, rows, :], sem.at[8 + j]))
         copies.append(pltpu.make_async_copy(vp.at[1, :, :, lanes], v_buf.at[pl.ds(other, part), j, rows, :], sem.at[10 + j]))
         copies.append(pltpu.make_async_copy(df.at[:, :, lanes], d_buf.at[:, j, rows, :], sem.at[12 + j]))
-    tracer = []
-    for s in range(2):
-        for j in range(2):
-            tracer.append(pltpu.make_async_copy(
-                tr.at[pl.ds(8 * s, 8), :, :, pl.ds(128 * j, 128)],
-                c_buf.at[pl.ds(8 * s, 8), :, j, pl.ds(8, 16), :], sem.at[14 + 2 * s + j]))
-    return copies, tracer
-
-
-OWN_SCRATCH = [
-    pltpu.VMEM((NT, LV, 2, 32, 128), F32),
+    return copies
+
+
+def tracer_copies(tr, c_buf, sem):
+    return [[pltpu.make_async_copy(
+        tr.at[pl.ds(8 * s, 8), :, :, pl.ds(128 * j, 128)],
+        c_buf.at[pl.ds(8 * s, 8), :, j, pl.ds(8, 16), :], sem.at[2 * s + j]) for j in range(2)] for s in range(2)]
+
+
+def depth_copies(land, level, l_buf, sem):
+    return [pltpu.make_async_copy(x.at[:, pl.ds(128 * j, 128)], l_buf.at[i, j], sem.at[2 * i + j])
+            for i, x in enumerate((land, level)) for j in range(2)]
+
+
+def fill_depth(l_buf, p_buf):
+    for j in range(2):
+        p_buf[j, 8:24, :] = jnp.where(l_buf[0, j] == 1, l_buf[1, j], 0)
+
+
+FIELD_SCRATCH = [
     pltpu.VMEM((LV, 2, 32, 128), F32),
     pltpu.VMEM((LV, 2, 32, 128), F32),
     pltpu.VMEM((LV, 2, 32, 128), F32),
     pltpu.VMEM((LV, 2, 32, 128), F32),
+    pltpu.SemaphoreType.DMA((14,)),
+]
+DEPTH_SCRATCH = [
+    pltpu.VMEM((2, 2, 16, 128), jnp.int32),
     pltpu.VMEM((2, 32, 128), jnp.int32),
-    pltpu.SemaphoreType.DMA((18,)),
+    pltpu.SemaphoreType.DMA((4,)),
 ]
-
-
-def fill_depth(land, level, p_buf):
-    for j in range(2):
-        lanes = slice(128 * j, 128 * j + 128)
-        p_buf[j, 8:24, :] = jnp.where(land[:, lanes] == 1, level[:, lanes], 0)
-
-
-def rows_kernel(scal, tr, ho, hp, vo, vp, df, land, level, y_up, y_dn, c_buf, h_buf, u_buf, v_buf, d_buf, p_buf, sem):
-    off = scal[0] * (LV // 2)
-    fields, tracer = own_copies(tr, ho, hp, vo, vp, df, off, c_buf, h_buf, u_buf, v_buf, d_buf, sem)
-    for c in fields + tracer:
+TRACER_SCRATCH = [
+    pltpu.VMEM((NT, LV, 2, 32, 128), F32),
+    pltpu.SemaphoreType.DMA((4,)),
+]
+
+
+def pack_lanes(sources):
+    lane = lane_iota()
+    place, slot = lane & 31, lane >> 5
+    acc = None
+    for q, (left, right) in enumerate(sources):
+        a = pltpu.roll(left, (4 + 32 * q) % 128, 1)
+        b = pltpu.roll(right, (28 + 32 * q) % 128, 1)
+        x = jnp.where(place < 16, a, b)
+        acc = x if acc is None else jnp.where(slot == q, x, acc)
+    return acc
+
+
+def to_east(packed, g):
+    return pltpu.roll(packed, (4 * g - 24) % 128, 1)
+
+
+def to_west(packed, g):
+    return pltpu.roll(packed, (4 * g - 4) % 128, 1)
+
+
+def tracer_pack_kernel(tr, y_up, y_dn, own, x_r, x_l, c_buf, c_sem):
+    copies = tracer_copies(tr, c_buf, c_sem)
+    for c in copies[0] + copies[1]:
         c.start()
-    fill_depth(land, level, p_buf)
-    for c in fields + tracer:
-        c.wait()
     low = sub_iota() < 4
-
-    def put(index, j, first, second):
-        y_up[index, j] = jnp.where(low, first(20), second(16))
-        y_dn[index, j] = jnp.where(low, first(8), second(4))
+    place = lane_iota() & 31
+    for c in copies[0] + copies[1]:
+        c.wait()
 
     @pl.loop(0, LV, unroll=2)
     def _(k):
         for j in range(2):
             for t in range(PER):
-                put(t * LV + k, j, lambda r: c_buf[t, k, j, r:r + 8, :], lambda r: c_buf[t + PER, k, j, r:r + 8, :])
-            put(128 + k, j, lambda r: h_buf[k, j, r:r + 8, :], lambda r: u_buf[k, j, r:r + 8, :])
-            put(144 + k, j, lambda r: v_buf[k, j, r:r + 8, :], lambda r: d_buf[k, j, r:r + 8, :])
+                read = lambda b, r: c_buf[t + b, k, j, r:r + 8, :]
+                y_up[t * LV + k, j] = jnp.where(low, read(0, 20), read(PER, 16))
+                y_dn[t * LV + k, j] = jnp.where(low, read(0, 8), read(PER, 4))
+        for i in range(2):
+            rows = slice(8 * i, 8 * i + 8)
+            xr, xl = None, None
+            for g in range(4):
+                packed = pack_lanes([[c_buf[4 * g + q, k, j, 8 + 8 * i:16 + 8 * i, :] for j in range(2)] for q in range(4)])
+                own[k, g, rows, :] = packed
+                here = place >= 4 * g
+                xr = to_east(packed, g) if g == 0 else jnp.where(here, to_east(packed, g), xr)
+                xl = to_west(packed, g) if g == 0 else jnp.where(here, to_west(packed, g), xl)
+            x_r[k, rows, :] = xr
+            x_l[k, rows, :] = xl
+
+
+def field_pack_kernel(scal, ho, hp, vo, vp, df, land, level, up_in, dn_in, y_up, y_dn, own,
+                      h_buf, u_buf, v_buf, d_buf, sem, l_buf, p_buf, l_sem, f_up, f_dn, out_sem):
+    off = scal[0] * (LV // 2)
+    copies = field_copies(ho, hp, vo, vp, df, off, h_buf, u_buf, v_buf, d_buf, sem) + depth_copies(land, level, l_buf, l_sem)
+    for c in copies:
+        c.start()
+    low = sub_iota() < 4
+    for c in copies:
+        c.wait()
+    fill_depth(l_buf, p_buf)
+
+    def put(index, j, first, second):
+        f_up[index, j] = jnp.where(low, first(20), second(16))
+        f_dn[index, j] = jnp.where(low, first(8), second(4))
+
+    @pl.loop(0, LV, unroll=4)
+    def _(k):
+        for j in range(2):
+            put(k, j, lambda r: h_buf[k, j, r:r + 8, :], lambda r: u_buf[k, j, r:r + 8, :])
+            put(16 + k, j, lambda r: v_buf[k, j, r:r + 8, :], lambda r: d_buf[k, j, r:r + 8, :])
 
     for j in range(2):
         get = lambda r: p_buf[j, r:r + 8, :].astype(F32)
-        put(160, j, get, get)
+        put(32, j, get, get)
+    leaving = [pltpu.make_async_copy(f, y.at[pl.ds(128, 33)], out_sem.at[i]) for i, (f, y) in enumerate(((f_up, y_up), (f_dn, y_dn)))]
+    for c in leaving:
+        c.start()
+
+    @pl.loop(0, LV, unroll=4)
+    def _(k):
+        for i in range(2):
+            rows = slice(8 + 8 * i, 16 + 8 * i)
+            own[k, 8 * i:8 * i + 8, :] = pack_lanes([[buf[k, j, rows, :] for j in range(2)] for buf in (h_buf, u_buf, v_buf, d_buf)])
+
+    for i in range(2):
+        own[LV, 8 * i:8 * i + 8, :] = pack_lanes([[p_buf[j, 8 + 8 * i:16 + 8 * i, :].astype(F32) for j in range(2)]] * 4)
+    for c in leaving:
+        c.wait()
 
 
 def inner_kernel(rows_total, scal, tr, ho, hp, vo, vp, df, land, level, reaction, saved_out, saved_f, mid, mid_f,
-                 c_buf, h_buf, u_buf, v_buf, d_buf, p_buf, sem, c_alt, solved, coef, table, saved, out_sem):
+                 h_buf, u_buf, v_buf, d_buf, sem, l_buf, p_buf, l_sem, c_buf, c_sem, c_alt, solved, coef, table, saved, out_sem):
     off = scal[0] * (LV // 2)
-    fields, tracer = own_copies(tr, ho, hp, vo, vp, df, off, c_buf, h_buf, u_buf, v_buf, d_buf, sem)
-    for c in fields + tracer:
+    fields = field_copies(ho, hp, vo, vp, df, off, h_buf, u_buf, v_buf, d_buf, sem)
+    depths = depth_copies(land, level, l_buf, l_sem)
+    tracer = tracer_copies(tr, c_buf, c_sem)
+    for c in depths + fields + tracer[0] + tracer[1]:
         c.start()
-    fill_depth(land, level, p_buf)
     fill_table(reaction, table)
+    for c in depths:
+        c.wait()
+    fill_depth(l_buf, p_buf)
     six = sub_iota() < 6
     rows = lax.broadcasted_iota(jnp.int32, (16, 128), 0) + scal[1]
     cor_c = coriolis_of(rows, rows_total)
@@ -221,7 +298,7 @@
                     saved[n, t, k, j] = keep(n, lambda r: buf[t, k, j, r:r + 8, :])
 
     keep_fields(0)
-    for c in tracer:
+    for c in tracer[0] + tracer[1]:
         c.wait()
     keep_tracers(0, c_buf)
     leaving = [pltpu.make_async_copy(saved.at[n], saved_out.at[n], out_sem.at[n]) for n in range(ITERS)]
@@ -288,72 +365,59 @@
         c.wait()
 
 
-def strip_pack_kernel(scal, tr, ho, hp, vo, vp, df, land, level, y_s, y_n, o_ref, x_r, x_l,
-                      c_buf, h_buf, u_buf, v_buf, d_buf, p_buf, sem):
-    off = scal[0] * (LV // 2)
-    fields, tracer = own_copies(tr, ho, hp, vo, vp, df, off, c_buf, h_buf, u_buf, v_buf, d_buf, sem)
-    for c in fields + tracer:
+def halo_pack_kernel(y_s, y_n, own_f, r_own, l_own, halo, x_r, x_l, s_buf, n_buf, sem):
+    copies = [pltpu.make_async_copy(y_s, s_buf, sem.at[0]), pltpu.make_async_copy(y_n, n_buf, sem.at[1])]
+    for c in copies:
         c.start()
-    fill_depth(land, level, p_buf)
-    for c in fields + tracer:
-        c.wait()
     low = sub_iota() < 4
-    lane = lane_iota()
-    place = lane & 31
-    slot = lane >> 5
-
-    def three(read, index, half, j):
-        ys, yn = y_s[index, j], y_n[index, j]
-        if half == 0:
-            yn = pltpu.roll(yn, 4, 0)
-        else:
-            ys = pltpu.roll(ys, 4, 0)
-        return [jnp.where(low, ys, read(4)), read(12), jnp.where(low, read(20), yn)]
-
-    def pack(sources):
-        acc = [None] * 3
-        for q, (read, index, half) in enumerate(sources):
-            left = three(lambda r: read(0, r), index, half, 0)
-            right = three(lambda r: read(1, r), index, half, 1)
-            for i in range(3):
-                a = pltpu.roll(left[i], (4 + 32 * q) % 128, 1)
-                b = pltpu.roll(right[i], (28 + 32 * q) % 128, 1)
-                x = jnp.where(place < 16, a, b)
-                acc[i] = x if acc[i] is None else jnp.where(slot == q, x, acc[i])
-        return acc
+    place = lane_iota() & 31
+    for i in range(2):
+        rows = slice(8 * i, 8 * i + 8)
+        x_r[LV, rows, :] = to_east(own_f[LV, rows, :], 4)
+        x_l[LV, rows, :] = to_west(own_f[LV, rows, :], 4)
+
+    @pl.loop(0, LV, unroll=4)
+    def _(k):
+        for i in range(2):
+            rows = slice(8 * i, 8 * i + 8)
+            x_r[k, rows, :] = jnp.where(place >= 16, to_east(own_f[k, rows, :], 4), r_own[k, rows, :])
+            x_l[k, rows, :] = jnp.where(place >= 16, to_west(own_f[k, rows, :], 4), l_own[k, rows, :])
+
+    for c in copies:
+        c.wait()
+
+    def pair(index, j):
+        ys, yn = s_buf[index, j], n_buf[index, j]
+        return jnp.where(low, ys, pltpu.roll(yn, 4, 0)), jnp.where(low, pltpu.roll(ys, 4, 0), yn)
 
     @pl.loop(0, LV, unroll=2)
     def _(k):
-        def tracer_source(t):
-            return (lambda j, r: c_buf[t, k, j, r:r + 8, :], (t % PER) * LV + k, t // PER)
-
-        groups = [[tracer_source(4 * g + q) for q in range(4)] for g in range(4)]
-        groups.append([
-            (lambda j, r: h_buf[k, j, r:r + 8, :], 128 + k, 0), (lambda j, r: u_buf[k, j, r:r + 8, :], 128 + k, 1),
-            (lambda j, r: v_buf[k, j, r:r + 8, :], 144 + k, 0), (lambda j, r: d_buf[k, j, r:r + 8, :], 144 + k, 1)])
-        xr, xl = [jnp.zeros((8, 128), F32)] * 3, [jnp.zeros((8, 128), F32)] * 3
+        pairs = [[pair(t * LV + k, j) for j in range(2)] for t in range(PER)]
+        hu = [pair(128 + k, j) for j in range(2)]
+        vd = [pair(144 + k, j) for j in range(2)]
+        groups = [[[pairs[4 * (g % 2) + q][j][g // 2] for j in range(2)] for q in range(4)] for g in range(4)]
+        groups.append([[x[j][w] for j in range(2)] for x in (hu, vd) for w in range(2)])
+        xr, xl = None, None
         for g in range(5):
-            packed = pack(groups[g])
-            here = (place >= 4 * g) & (place < 4 * g + 4)
-            for i in range(3):
-                o_ref[k, g, 8 * i:8 * i + 8, :] = packed[i]
-                xr[i] = jnp.where(here, pltpu.roll(packed[i], (4 * g - 24) % 128, 1), xr[i])
-                xl[i] = jnp.where(here, pltpu.roll(packed[i], (4 * g - 4) % 128, 1), xl[i])
-        for i in range(3):
-            x_r[k, 8 * i:8 * i + 8, :] = xr[i]
-            x_l[k, 8 * i:8 * i + 8, :] = xl[i]
-
-    packed = pack([(lambda j, r: p_buf[j, r:r + 8, :].astype(F32), 160, 0)] * 4)
-    for i in range(3):
-        for g in range(5):
-            o_ref[LV, g, 8 * i:8 * i + 8, :] = packed[i]
-        x_r[LV, 8 * i:8 * i + 8, :] = pltpu.roll(packed[i], (16 - 24) % 128, 1)
-        x_l[LV, 8 * i:8 * i + 8, :] = pltpu.roll(packed[i], (16 - 4) % 128, 1)
-
-
-def edge_kernel(rows_total, scal, saved, saved_f, y_s, y_n, df, land, level, reaction, out_c, out_f,
-                c_buf, f_buf, d_buf, p_buf, solved, coef, table, sem):
-    copies = []
+            packed = pack_lanes(groups[g])
+            halo[k, g] = packed
+            here = place >= 4 * g
+            xr = to_east(packed, g) if g == 0 else jnp.where(here, to_east(packed, g), xr)
+            xl = to_west(packed, g) if g == 0 else jnp.where(here, to_west(packed, g), xl)
+        x_r[k, 16:24, :] = xr
+        x_l[k, 16:24, :] = xl
+
+    packed = pack_lanes([[pair(160, j)[0] for j in range(2)]] * 4)
+    for g in range(5):
+        halo[LV, g] = packed
+    x_r[LV, 16:24, :] = to_east(packed, 4)
+    x_l[LV, 16:24, :] = to_west(packed, 4)
+
+
+def edge_kernel(rows_total, scal, saved, saved_f, south, north, df, land, level, reaction, out_c, out_f,
+                c_buf, f_buf, d_buf, l_buf, p_buf, l_sem, solved, coef, table, y_s, y_n, sem):
+    copies = [pltpu.make_async_copy(south, y_s, sem.at[10]), pltpu.make_async_copy(north, y_n, sem.at[11])]
+    copies += depth_copies(land, level, l_buf, l_sem)
     for n in range(ITERS):
         copies.append(pltpu.make_async_copy(saved_f.at[n], f_buf.at[n, :, :, :, pl.ds(0, 8), :], sem.at[n]))
     for j in range(2):
@@ -362,11 +426,11 @@
     for c in copies + tracer:
         c.start()
     fill_table(reaction, table)
-    fill_depth(land, level, p_buf)
     sub = sub_iota()
     low = sub < 4
     for c in copies:
         c.wait()
+    fill_depth(l_buf, p_buf)
     tracer[0].wait()
 
     def put(ref, y, half, south):
@@ -468,8 +532,11 @@
             lax.fori_loop(0, LV, upward, [zeros_like_tiles(8, 2) for _ in range(PER)], unroll=4)
 
 
-def strip_kernel(rows_total, scal, o_ref, x_r, x_l, reaction, mid, mid_f, edge, edge_f, out_c, out_h, out_v,
-                 c_buf, c_alt, h_buf, u_buf, v_buf, d_buf, p_buf, solved, coef, table):
+def strip_kernel(rows_total, scal, own, own_f, halo, x_w, x_e, reaction, mid_in, mid_f, edge_in, edge_f, out, out_h, out_v,
+                 c_buf, c_alt, h_buf, u_buf, v_buf, d_buf, p_buf, solved, coef, table, mid, edge, out_c, sem):
+    arriving = [pltpu.make_async_copy(mid_in, mid, sem.at[0]), pltpu.make_async_copy(edge_in, edge, sem.at[1])]
+    for c in arriving:
+        c.start()
     lane = lane_iota()
     place = lane & 31
     slot = lane >> 5
@@ -487,24 +554,37 @@
 
     def whole(k, g, i, xg):
         rows = slice(8 * i, 8 * i + 8)
-        a = pltpu.roll(x_r[k, rows, :], (-4 * xg) % 128, 1)
-        b = pltpu.roll(x_l[k, rows, :], (28 - 4 * xg) % 128, 1)
-        return jnp.where(place < 4, a, jnp.where(place >= 28, b, o_ref[k, g, rows, :]))
+        a = pltpu.roll(x_w[k, rows, :], (-4 * xg) % 128, 1)
+        b = pltpu.roll(x_e[k, rows, :], (28 - 4 * xg) % 128, 1)
+        if i == 2:
+            body = halo[k, g]
+        elif g == 4:
+            body = own_f[k, rows, :]
+        else:
+            body = own[k, g, rows, :]
+        return jnp.where(place < 4, a, jnp.where(place >= 28, b, body))
+
+    def put(ref, i, x):
+        if i < 2:
+            ref[12 + 8 * i:20 + 8 * i, :] = x
+        else:
+            pltpu.store(ref.at[pl.ds(8, 8), :], x, mask=low)
+            pltpu.store(ref.at[pl.ds(24, 8), :], x, mask=jnp.logical_not(low))
 
     @pl.loop(0, LV, unroll=4)
     def _(k):
         for i in range(3):
             for g in range(4):
-                c_buf[g, k, 8 + 8 * i:16 + 8 * i, :] = whole(k, g, i, g)
+                put(c_buf.at[g, k], i, whole(k, g, i, g))
             x = whole(k, 4, i, 4)
             for f, buf in enumerate((h_buf, u_buf, v_buf, d_buf)):
                 y = jnp.where(lane < 32, pltpu.roll(x, (-32 * f) % 128, 1), 0.0)
                 y = y + pltpu.roll(y, 32, 1)
                 y = y + pltpu.roll(y, 64, 1)
-                buf[k, 8 + 8 * i:16 + 8 * i, :] = y
+                put(buf.at[k], i, y)
 
     for i in range(3):
-        p_buf[8 + 8 * i:16 + 8 * i, :] = whole(LV, 4, i, 4).astype(jnp.int32)
+        put(p_buf, i, whole(LV, 4, i, 4).astype(jnp.int32))
 
     rows = lax.broadcasted_iota(jnp.int32, (24, 128), 0) - 4 + scal[1]
     cor_c = coriolis_of(rows, rows_total)
@@ -573,14 +653,21 @@
             return jnp.where(lane < 4, pltpu.roll(strip, (-(32 * q + 4)) % 128, 1), body)
         return jnp.where(lane >= 124, pltpu.roll(strip, (100 - 32 * q) % 128, 1), body)
 
-    @pl.loop(0, LV, unroll=2)
-    def _(k):
-        for t in range(NT):
-            for i in range(2):
-                strip = final[t // 4, k, 12 + 8 * i:20 + 8 * i, :]
-                for j in range(2):
-                    out_c[t, k, 8 * i:8 * i + 8, 128 * j:128 * j + 128] = merge(
-                        mid[t, k, j], edge[t, k, j], strip, t % 4, j, i)
+    for c in arriving:
+        c.wait()
+    leaving = []
+    for part in range(4):
+        @pl.loop(4 * part, 4 * part + 4, unroll=2)
+        def _(k):
+            for t in range(NT):
+                for i in range(2):
+                    strip = final[t // 4, k, 12 + 8 * i:20 + 8 * i, :]
+                    for j in range(2):
+                        out_c[t, k, 8 * i:8 * i + 8, 128 * j:128 * j + 128] = merge(
+                            mid[t, k, j], edge[t, k, j], strip, t % 4, j, i)
+        levels = pl.ds(4 * part, 4)
+        leaving.append(pltpu.make_async_copy(out_c.at[:, levels], out.at[:, levels], sem.at[2 + part]))
+        leaving[part].start()
 
     off = scal[0] * (LV // 2)
 
@@ -595,6 +682,8 @@
                         out_h[k, 8 * i:8 * i + 8, 128 * j:128 * j + 128] = x
                     else:
                         out_v[f - 1, k, 8 * i:8 * i + 8, 128 * j:128 * j + 128] = x
+    for c in leaving:
+        c.wait()
 
 
 def sds(*shape):
@@ -607,15 +696,23 @@
     set_index = lax.axis_index("set").astype(jnp.int32)
     row_start = lax.axis_index("ty").astype(jnp.int32) * rows_local
     scal = jnp.stack([set_index, row_start])
+    params = pltpu.CompilerParams(vmem_limit_bytes=VMEM_LIMIT)
     swap = [(0, 1), (1, 0)]
     h_pair = lax.ppermute(thickness, "set", swap)
     v_pair = lax.ppermute(velocity, "set", swap)
-    own = (scal, tracers, thickness, h_pair, velocity, v_pair, diffusivity, land_mask, level_count)
-    own_specs = [SMEM] + [ANY] * 6 + [VMEM] * 2
-    params = pltpu.CompilerParams(vmem_limit_bytes=VMEM_LIMIT)
-    y_up, y_dn = pl.pallas_call(
-        rows_kernel, out_shape=[sds(161, 2, 8, 128)] * 2, in_specs=own_specs, out_specs=[VMEM] * 2,
-        scratch_shapes=OWN_SCRATCH, compiler_params=params, name="edge_rows")(*own)
+    up_part, dn_part, own, r_own, l_own = pl.pallas_call(
+        tracer_pack_kernel,
+        out_shape=[sds(161, 2, 8, 128), sds(161, 2, 8, 128), sds(LV, 4, 16, 128), sds(LV, 16, 128), sds(LV, 16, 128)],
+        in_specs=[ANY], out_specs=[VMEM] * 5, scratch_shapes=TRACER_SCRATCH,
+        compiler_params=params, name="tracer_pack")(tracers)
+    h_pair, v_pair, up_part, dn_part = lax.optimization_barrier((h_pair, v_pair, up_part, dn_part))
+    fields = (thickness, h_pair, velocity, v_pair, diffusivity, land_mask, level_count)
+    y_up, y_dn, own_f = pl.pallas_call(
+        field_pack_kernel, out_shape=[sds(161, 2, 8, 128), sds(161, 2, 8, 128), sds(LV + 1, 16, 128)],
+        in_specs=[SMEM] + [ANY] * 9, out_specs=[ANY, ANY, VMEM], input_output_aliases={8: 0, 9: 1},
+        scratch_shapes=FIELD_SCRATCH + DEPTH_SCRATCH + [
+            pltpu.VMEM((33, 2, 8, 128), F32), pltpu.VMEM((33, 2, 8, 128), F32), pltpu.SemaphoreType.DMA((2,))],
+        compiler_params=params, name="field_pack")(scal, *fields, up_part, dn_part)
     ty = lax.axis_size("ty")
     north = [(i, i + 1) for i in range(ty - 1)]
     south = [(j, i) for i, j in north]
@@ -624,43 +721,45 @@
     saved, saved_f, mid, mid_f = pl.pallas_call(
         lambda *a: inner_kernel(rows_total, *a),
         out_shape=[sds(ITERS, NT, LV, 2, 8, 128), sds(ITERS, 3, LV, 2, 8, 128), sds(NT, LV, 2, 8, 128), sds(3, LV, 2, 8, 128)],
-        in_specs=own_specs + [SMEM], out_specs=[ANY] + [VMEM] * 3,
-        scratch_shapes=OWN_SCRATCH + [
+        in_specs=[SMEM] + [ANY] * 8 + [SMEM], out_specs=[ANY] + [VMEM] * 3,
+        scratch_shapes=FIELD_SCRATCH + DEPTH_SCRATCH + TRACER_SCRATCH + [
             pltpu.VMEM((NT, LV, 2, 32, 128), F32),
             pltpu.VMEM((LV, PER, 2, 8, 128), F32),
             pltpu.VMEM((7, LV, 2, 16, 128), F32),
             pltpu.VMEM((128, 8, 128), F32),
             pltpu.VMEM((ITERS, NT, LV, 2, 8, 128), F32),
             pltpu.SemaphoreType.DMA((ITERS,))],
-        compiler_params=params, name="inner")(*own, reaction)
+        compiler_params=params, name="inner")(scal, tracers, *fields, reaction)
     y_s, y_n, mid_f = lax.optimization_barrier((y_s, y_n, mid_f))
-    o_ref, x_r, x_l = pl.pallas_call(
-        strip_pack_kernel, out_shape=[sds(LV + 1, 5, 24, 128), sds(LV + 1, 24, 128), sds(LV + 1, 24, 128)],
-        in_specs=own_specs + [VMEM] * 2, out_specs=[VMEM] * 3,
-        scratch_shapes=OWN_SCRATCH, compiler_params=params, name="strip_pack")(*own, y_s, y_n)
+    halo, x_r, x_l = pl.pallas_call(
+        halo_pack_kernel, out_shape=[sds(LV + 1, 5, 8, 128), sds(LV + 1, 24, 128), sds(LV + 1, 24, 128)],
+        in_specs=[ANY, ANY] + [VMEM] * 3, out_specs=[VMEM] * 3,
+        scratch_shapes=[pltpu.VMEM((161, 2, 8, 128), F32), pltpu.VMEM((161, 2, 8, 128), F32), pltpu.SemaphoreType.DMA((2,))],
+        compiler_params=params, name="halo_pack")(y_s, y_n, own_f, r_own, l_own)
     tx = lax.axis_size("tx")
     east = [(i, (i + 1) % tx) for i in range(tx)]
     west = [(j, i) for i, j in east]
-    x_west = lax.ppermute(x_r, "tx", east)
-    x_east = lax.ppermute(x_l, "tx", west)
+    x_w = lax.ppermute(x_r, "tx", east)
+    x_e = lax.ppermute(x_l, "tx", west)
     edge, edge_f = pl.pallas_call(
         lambda *a: edge_kernel(rows_total, *a),
         out_shape=[sds(NT, LV, 2, 8, 128), sds(3, LV, 2, 8, 128)],
-        in_specs=[SMEM, ANY, ANY, VMEM, VMEM, ANY, VMEM, VMEM, SMEM], out_specs=[VMEM] * 2,
+        in_specs=[SMEM] + [ANY] * 7 + [SMEM], out_specs=[VMEM] * 2,
         scratch_shapes=[
             pltpu.VMEM((ITERS, NT, LV, 2, 16, 128), F32),
             pltpu.VMEM((ITERS, 3, LV, 2, 16, 128), F32),
-            pltpu.VMEM((LV, 2, 32, 128), F32),
-            pltpu.VMEM((2, 32, 128), jnp.int32),
+            pltpu.VMEM((LV, 2, 32, 128), F32)] + DEPTH_SCRATCH + [
             pltpu.VMEM((LV, PER, 2, 8, 128), F32),
             pltpu.VMEM((7, LV, 2, 8, 128), F32),
             pltpu.VMEM((128, 8, 128), F32),
-            pltpu.SemaphoreType.DMA((10,))],
+            pltpu.VMEM((161, 2, 8, 128), F32),
+            pltpu.VMEM((161, 2, 8, 128), F32),
+            pltpu.SemaphoreType.DMA((12,))],
         compiler_params=params, name="edge")(scal, saved, saved_f, y_s, y_n, diffusivity, land_mask, level_count, reaction)
     return pl.pallas_call(
         lambda *a: strip_kernel(rows_total, *a),
         out_shape=[sds(*tracers.shape), sds(*thickness.shape), sds(*velocity.shape)],
-        in_specs=[SMEM, VMEM, VMEM, VMEM, SMEM, VMEM, VMEM, VMEM, VMEM], out_specs=[VMEM] * 3,
+        in_specs=[SMEM] + [VMEM] * 5 + [SMEM, ANY, VMEM, ANY, VMEM], out_specs=[ANY, VMEM, VMEM],
         scratch_shapes=[
             pltpu.VMEM((4, LV, 40, 128), F32),
             pltpu.VMEM((4, LV, 40, 128), F32),
@@ -671,8 +770,12 @@
             pltpu.VMEM((40, 128), jnp.int32),
             pltpu.VMEM((LV, 4, 3, 8, 128), F32),
             pltpu.VMEM((7, LV, 24, 128), F32),
-            pltpu.VMEM((32, 8, 128), F32)],
-        compiler_params=params, name="strips")(scal, o_ref, x_west, x_east, reaction, mid, mid_f, edge, edge_f)
+            pltpu.VMEM((32, 8, 128), F32),
+            pltpu.VMEM((NT, LV, 2, 8, 128), F32),
+            pltpu.VMEM((NT, LV, 2, 8, 128), F32),
+            pltpu.VMEM((NT, LV, 16, 256), F32),
+            pltpu.SemaphoreType.DMA((6,))],
+        compiler_params=params, name="strips")(scal, own, own_f, halo, x_w, x_e, reaction, mid, mid_f, edge, edge_f)
 
 
 def solution(mesh):

time: 115 us -> 105 us (0.913)
  waiting for transfers between devices: 8.4 us -> 0.9 us
  Pallas kernels: 85.6 us -> 83 us
    ppermute x1, waiting for transfers between devices: 8.38 us -> 0.89 us  [body(): h_pair = lax.ppermute(thickness, 'set', swap)]
    pallas_call x1, Pallas kernels: 17.6 us -> 15.9 us  [body(): pl.pallas_call(lambda *a: strip_kernel(rows_total, *a), out_shape=[sds(*t...]
    pallas_call x2 -> x3, Pallas kernels: 17.6 us -> 16.9 us  [the longest x1 7.47 us: body(): pl.pallas_call(tracer_pack_kernel, out_shape=[sds(161, 2, 8, 128), sds(16...]
  transfers between devices with their start and end apart: 6 -> 6, of which waited for: 1 -> 1; matrix products, arithmetic and copies ran while one was open for 0% -> 1% of each run, Pallas kernels for 44% -> 55%
where the time goes in v3:
time: 105 us
  Pallas kernels  83 us (79%)
  starting transfers between devices  16.3 us (16%)
  local copies, waits for them, and re-layouts  2.92 us (3%)
    pallas_call x1, Pallas kernels, body(): pl.pallas_call(lambda *a: inner_kernel(rows_total, *a), out_shape=[sds(IT...  30.6 us
    pallas_call x1, Pallas kernels, body(): pl.pallas_call(lambda *a: edge_kernel(rows_total, *a), out_shape=[sds(NT,...  19.6 us
    pallas_call x1, Pallas kernels, body(): pl.pallas_call(lambda *a: strip_kernel(rows_total, *a), out_shape=[sds(*t...  15.9 us
    pallas_call x1, Pallas kernels, body(): pl.pallas_call(tracer_pack_kernel, out_shape=[sds(161, 2, 8, 128), sds(16...  7.47 us
    ppermute x1, starting transfers between devices, body(): y_s = lax.ppermute(y_up, 'ty', north)  6.46 us
    pallas_call x1, Pallas kernels, body(): pl.pallas_call(halo_pack_kernel, out_shape=[sds(LV + 1, 5, 8, 128), sds(L...  5.69 us
    ppermute x1, starting transfers between devices, body(): x_e = lax.ppermute(x_l, 'tx', west)  3.89 us
    pallas_call x1, Pallas kernels, body(): pl.pallas_call(field_pack_kernel, out_shape=[sds(161, 2, 8, 128), sds(161...  3.69 us
  transfers between devices with their start and end apart: 6, of which 1 were waited for; matrix products, arithmetic and copies ran while one was open for 1% of the time, Pallas kernels for 55%

profile of v3, /device:TPU:1, one launch (start us, length us, event | category | flops | bytes accessed | tf_op | source)
XLA Modules:
  0.0 104.6 jit_solution(4546103525239102942)
XLA Ops:
  0.6 2.5 %collective-permute-start.1 = (f32[2,8,16,256]{3,2,1,0:T(8,128)}, f32[2,8,16,256]{3,2,1,0:T(8,128)S(1)}, u32[]{:S(2)}, u32[]{:S(2)}) collective-permute-start(f32[2,8,16,256]{3,2,1,0:T(8,128)} %a_4_.1), channel_id=1, source_target_pairs={{0,64},{64,0},{1,65},{65,1},{2,66},{66,2},{3,67},{67,3},{4,68},{68... | collective-permute-start | bytes 786440 | tf_op jit(solution)/shard_map/ppermute | solution.py:702
  3.2 0.1 collective-permute-start
  3.3 7.5 %tracer_pack.1 = (f32[161,2,8,128]{3,2,1,0:T(8,128)}, f32[161,2,8,128]{3,2,1,0:T(8,128)}, f32[16,4,16,128]{3,2,1,0:T(8,128)}, f32[16,16,128]{2,1,0:T(8,128)}, f32[16,16,128]{2,1,0:T(8,128)}) custom-call(f32[16,16,16,256]{3,2,1,0:T(8,128)} %a_1_.1), custom_call_target="tpu_custom_call" | custom-call | tf_op jit(solution)/shard_map/tracer_pack/pallas_call | solution.py:703
  10.8 0.6 pad_add_fusion.scal.a_0_
  11.3 0.9 collective-permute-done.hp.a_3_
  12.2 0.0 copy-start.3
  12.2 0.0 collective-permute-done.1.vp.a_5_
  12.2 0.0 copy-start.2
  12.2 0.7 copy-done.3
  12.9 0.1 copy-done.2
  13.0 3.7 %field_pack.1 = (f32[161,2,8,128]{3,2,1,0:T(8,128)}, f32[161,2,8,128]{3,2,1,0:T(8,128)}, f32[17,16,128]{2,1,0:T(8,128)}) custom-call(s32[2]{0:T(128)} %pad_add_fusion.scal.a_0_, f32[8,16,256]{2,1,0:T(8,128)} %a_2_.1, f32[8,16,256]{2,1,0:T(8,128)} %copy-done.3, f32[2,8,16,256]{3,2,1,0:T(8,128)} %a_4_.1, ...), custom_call_target="tpu_custom_call", output_to_operand_aliasing={{0}: (8, {}), {1}: (9, {})} | custom-call | tf_op jit(solution)/shard_map/field_pack/pallas_call | solution.py:710
  16.6 6.5 %collective-permute-start.2 = (f32[161,2,8,128]{3,2,1,0:T(8,128)}, f32[161,2,8,128]{3,2,1,0:T(8,128)S(1)}, u32[]{:S(2)}, u32[]{:S(2)}) collective-permute-start(f32[161,2,8,128]{3,2,1,0:T(8,128)} %get-tuple-element.35), channel_id=1, source_target_pairs={{0,1},{1,2},{2,3},{4,5},{5,6},{6,7},{8,9},{9,10},{10,11},{12,13},{... | collective-permute-start | bytes 3956744 | tf_op jit(solution)/shard_map/ppermute | solution.py:719
  23.1 1.9 %collective-permute-start.3 = (f32[161,2,8,128]{3,2,1,0:T(8,128)}, f32[161,2,8,128]{3,2,1,0:T(8,128)S(1)}, u32[]{:S(2)}, u32[]{:S(2)}) collective-permute-start(f32[161,2,8,128]{3,2,1,0:T(8,128)} %get-tuple-element.36), channel_id=1, source_target_pairs={{1,0},{2,1},{3,2},{5,4},{6,5},{7,6},{9,8},{10,9},{11,10},{13,12},{... | collective-permute-start | bytes 3956744 | tf_op jit(solution)/shard_map/ppermute | solution.py:720
  25.0 30.6 %inner.1 = (f32[4,16,16,2,8,128]{5,4,3,2,1,0:T(8,128)}, f32[4,3,16,2,8,128]{5,4,3,2,1,0:T(8,128)}, f32[16,16,2,8,128]{4,3,2,1,0:T(8,128)}, f32[3,16,2,8,128]{4,3,2,1,0:T(8,128)}) custom-call(s32[2]{0:T(128)} %pad_add_fusion.scal.a_0_, f32[16,16,16,256]{3,2,1,0:T(8,128)} %a_1_.1, f32[8,16,256]{2,1,0:T(8,128)} %a_2_.1, f32[8,16,256]{2,1,0:T(8,128)} %copy-done.3, ...), custom_call_target="tpu_custom_call" | custom-call | tf_op jit(solution)/shard_map/inner/pallas_call | solution.py:721
  55.7 0.0 collective-permute-done.2.y_s.a_3_
  55.7 0.0 copy-start
  55.7 0.0 collective-permute-done.3.y_n.a_4_
  55.7 0.0 copy-start.1
  55.7 1.1 %copy-done = f32[161,2,8,128]{3,2,1,0:T(8,128)} copy-done((f32[161,2,8,128]{3,2,1,0:T(8,128)}, f32[161,2,8,128]{3,2,1,0:T(8,128)S(1)}, u32[]{:S(2)}) %copy-start) | copy-done | bytes 1318936
  56.8 0.4 copy-done.1
  57.2 5.7 %halo_pack.1 = (f32[17,5,8,128]{3,2,1,0:T(8,128)}, f32[17,24,128]{2,1,0:T(8,128)}, f32[17,24,128]{2,1,0:T(8,128)}) custom-call(f32[161,2,8,128]{3,2,1,0:T(8,128)} %copy-done, f32[161,2,8,128]{3,2,1,0:T(8,128)} %copy-done.1, f32[17,16,128]{2,1,0:T(8,128)} %get-tuple-element.34.own_f.a_2_, f32[16,16,128]{2,1,0:T(8,128)} %get-tuple-element.40.r_own, ...), custom_call_target="tpu_custom_call" | custom-call | tf_op jit(solution)/shard_map/halo_pack/pallas_call | solution.py:734
  62.9 1.4 %collective-permute-start.4 = (f32[17,24,128]{2,1,0:T(8,128)}, f32[17,24,128]{2,1,0:T(8,128)S(1)}, u32[]{:S(2)}, u32[]{:S(2)}) collective-permute-start(f32[17,24,128]{2,1,0:T(8,128)} %get-tuple-element.43), channel_id=1, source_target_pairs={{0,4},{4,8},{8,12},{12,16},{16,20},{20,24},{24,28},{28,32},{32,36}... | collective-permute-start | bytes 626696 | tf_op jit(solution)/shard_map/ppermute | solution.py:742
  64.3 3.9 %collective-permute-start.5 = (f32[17,24,128]{2,1,0:T(8,128)}, f32[17,24,128]{2,1,0:T(8,128)S(1)}, u32[]{:S(2)}, u32[]{:S(2)}) collective-permute-start(f32[17,24,128]{2,1,0:T(8,128)} %get-tuple-element.44), channel_id=1, source_target_pairs={{4,0},{8,4},{12,8},{16,12},{20,16},{24,20},{28,24},{32,28},{36,32}... | collective-permute-start | bytes 626696 | tf_op jit(solution)/shard_map/ppermute | solution.py:743
  68.1 19.6 %edge.1 = (f32[16,16,2,8,128]{4,3,2,1,0:T(8,128)}, f32[3,16,2,8,128]{4,3,2,1,0:T(8,128)}) custom-call(s32[2]{0:T(128)} %pad_add_fusion.scal.a_0_, f32[4,16,16,2,8,128]{5,4,3,2,1,0:T(8,128)} %get-tuple-element.47.a_1_, f32[4,3,16,2,8,128]{5,4,3,2,1,0:T(8,128)} %get-tuple-element.48.a_2_, f32[161,2,8,128]{3,2,1,0:T(8,128)} %copy-done, ...), custom_call_target="tpu_custom_call" | custom-call | tf_op jit(solution)/shard_map/edge/pallas_call | solution.py:744
  87.8 0.0 collective-permute-done.4.a_4_
  87.8 0.0 copy-start.4
  87.8 0.0 collective-permute-done.5.a_5_
  87.8 0.0 copy-start.5
  87.8 0.6 copy-done.4
  88.5 0.1 copy-done.5
  88.6 15.9 %strips.1 = (f32[16,16,16,256]{3,2,1,0:T(8,128)}, f32[8,16,256]{2,1,0:T(8,128)}, f32[2,8,16,256]{3,2,1,0:T(8,128)}) custom-call(s32[2]{0:T(128)} %pad_add_fusion.scal.a_0_, f32[16,4,16,128]{3,2,1,0:T(8,128)} %get-tuple-element.27.a_1_, f32[17,16,128]{2,1,0:T(8,128)} %get-tuple-element.34.own_f.a_2_, f32[17,5,8,128]{3,2,1,0:T(8,128)} %get-tuple-element.42.a_3_, ...), custom_call_target="tpu_custom_call" | custom-call | tf_op jit(solution)/shard_map/strips/pallas_call | solution.py:759
Async XLA Ops:
  0.6 11.6 %collective-permute-start.1 = (f32[2,8,16,256]{3,2,1,0:T(8,128)}, f32[2,8,16,256]{3,2,1,0:T(8,128)S(1)}, u32[]{:S(2)}, u32[]{:S(2)}) collective-permute-start(f32[2,8,16,256]{3,2,1,0:T(8,128)} %a_4_.1), channel_id=1, source_target_pairs={{0,64},{64,0},{1,65},{65,1},{2,66},{66,2},{3,67},{67,3},{4,68},{68... | collective-permute-start | bytes 786440 | tf_op jit(solution)/shard_map/ppermute | solution.py:702
  3.2 9.0 %collective-permute-start = (f32[8,16,256]{2,1,0:T(8,128)}, f32[8,16,256]{2,1,0:T(8,128)S(1)}, u32[]{:S(2)}, u32[]{:S(2)}) collective-permute-start(f32[8,16,256]{2,1,0:T(8,128)} %a_2_.1), channel_id=1, source_target_pairs={{0,64},{64,0},{1,65},{65,1},{2,66},{66,2},{3,67},{67,3},{4,68},{68... | collective-permute-start | bytes 393224 | tf_op jit(solution)/shard_map/ppermute | solution.py:701
  12.2 0.7 copy-start.3
  12.2 0.7 copy-start.2
  16.6 39.1 %collective-permute-start.2 = (f32[161,2,8,128]{3,2,1,0:T(8,128)}, f32[161,2,8,128]{3,2,1,0:T(8,128)S(1)}, u32[]{:S(2)}, u32[]{:S(2)}) collective-permute-start(f32[161,2,8,128]{3,2,1,0:T(8,128)} %get-tuple-element.35), channel_id=1, source_target_pairs={{0,1},{1,2},{2,3},{4,5},{5,6},{6,7},{8,9},{9,10},{10,11},{12,13},{... | collective-permute-start | bytes 3956744 | tf_op jit(solution)/shard_map/ppermute | solution.py:719
  23.1 32.6 %collective-permute-start.3 = (f32[161,2,8,128]{3,2,1,0:T(8,128)}, f32[161,2,8,128]{3,2,1,0:T(8,128)S(1)}, u32[]{:S(2)}, u32[]{:S(2)}) collective-permute-start(f32[161,2,8,128]{3,2,1,0:T(8,128)} %get-tuple-element.36), channel_id=1, source_target_pairs={{1,0},{2,1},{3,2},{5,4},{6,5},{7,6},{9,8},{10,9},{11,10},{13,12},{... | collective-permute-start | bytes 3956744 | tf_op jit(solution)/shard_map/ppermute | solution.py:720
  55.7 1.1 %copy-start = (f32[161,2,8,128]{3,2,1,0:T(8,128)}, f32[161,2,8,128]{3,2,1,0:T(8,128)S(1)}, u32[]{:S(2)}) copy-start(f32[161,2,8,128]{3,2,1,0:T(8,128)S(1)} %collective-permute-done.2.y_s.a_3_) | copy-start | bytes 3956740
  55.7 1.5 %copy-start.1 = (f32[161,2,8,128]{3,2,1,0:T(8,128)}, f32[161,2,8,128]{3,2,1,0:T(8,128)S(1)}, u32[]{:S(2)}) copy-start(f32[161,2,8,128]{3,2,1,0:T(8,128)S(1)} %collective-permute-done.3.y_n.a_4_) | copy-start | bytes 3956740
  62.9 24.9 %collective-permute-start.4 = (f32[17,24,128]{2,1,0:T(8,128)}, f32[17,24,128]{2,1,0:T(8,128)S(1)}, u32[]{:S(2)}, u32[]{:S(2)}) collective-permute-start(f32[17,24,128]{2,1,0:T(8,128)} %get-tuple-element.43), channel_id=1, source_target_pairs={{0,4},{4,8},{8,12},{12,16},{16,20},{20,24},{24,28},{28,32},{32,36}... | collective-permute-start | bytes 626696 | tf_op jit(solution)/shard_map/ppermute | solution.py:742
  64.3 23.6 %collective-permute-start.5 = (f32[17,24,128]{2,1,0:T(8,128)}, f32[17,24,128]{2,1,0:T(8,128)S(1)}, u32[]{:S(2)}, u32[]{:S(2)}) collective-permute-start(f32[17,24,128]{2,1,0:T(8,128)} %get-tuple-element.44), channel_id=1, source_target_pairs={{4,0},{8,4},{12,8},{16,12},{20,16},{24,20},{28,24},{32,28},{36,32}... | collective-permute-start | bytes 626696 | tf_op jit(solution)/shard_map/ppermute | solution.py:743
  87.8 0.7 copy-start.4
  87.8 0.7 copy-start.5

commit v4 on v3

--- a/solution.py
+++ b/solution.py
@@ -12,7 +12,6 @@
 LV = 16
 NT = 16
 PER = 8
-VMEM_LIMIT = 60 * 1024 * 1024
 F32 = jnp.float32
 ANY = pl.BlockSpec(memory_space=pl.ANY)
 SMEM = pl.BlockSpec(memory_space=pltpu.SMEM)
@@ -105,67 +104,8 @@
     return outs
 
 
-def fill_table(react_ref, table):
-    for s in range(2):
-        for a in range(PER):
-            for b in range(PER):
-                v = DT * react_ref[s, a, b] + (1.0 if a == b else 0.0)
-                table[s * 64 + a * 8 + b] = jnp.full((8, 128), v, F32)
-
-
 def zeros_like_tiles(rows, count):
     return [jnp.zeros((rows, 128), F32) for _ in range(count)]
-
-
-def field_copies(ho, hp, vo, vp, df, off, h_buf, u_buf, v_buf, d_buf, sem):
-    copies = []
-    part = LV // 2
-    other = part - off
-    rows = pl.ds(8, 16)
-    for j in range(2):
-        lanes = pl.ds(128 * j, 128)
-        copies.append(pltpu.make_async_copy(ho.at[:, :, lanes], h_buf.at[pl.ds(off, part), j, rows, :], sem.at[0 + j]))
-        copies.append(pltpu.make_async_copy(hp.at[:, :, lanes], h_buf.at[pl.ds(other, part), j, rows, :], sem.at[2 + j]))
-        copies.append(pltpu.make_async_copy(vo.at[0, :, :, lanes], u_buf.at[pl.ds(off, part), j, rows, :], sem.at[4 + j]))
-        copies.append(pltpu.make_async_copy(vp.at[0, :, :, lanes], u_buf.at[pl.ds(other, part), j, rows, :], sem.at[6 + j]))
-        copies.append(pltpu.make_async_copy(vo.at[1, :, :, lanes], v_buf.at[pl.ds(off, part), j, rows, :], sem.at[8 + j]))
-        copies.append(pltpu.make_async_copy(vp.at[1, :, :, lanes], v_buf.at[pl.ds(other, part), j, rows, :], sem.at[10 + j]))
-        copies.append(pltpu.make_async_copy(df.at[:, :, lanes], d_buf.at[:, j, rows, :], sem.at[12 + j]))
-    return copies
-
-
-def tracer_copies(tr, c_buf, sem):
-    return [[pltpu.make_async_copy(
-        tr.at[pl.ds(8 * s, 8), :, :, pl.ds(128 * j, 128)],
-        c_buf.at[pl.ds(8 * s, 8), :, j, pl.ds(8, 16), :], sem.at[2 * s + j]) for j in range(2)] for s in range(2)]
-
-
-def depth_copies(land, level, l_buf, sem):
-    return [pltpu.make_async_copy(x.at[:, pl.ds(128 * j, 128)], l_buf.at[i, j], sem.at[2 * i + j])
-            for i, x in enumerate((land, level)) for j in range(2)]
-
-
-def fill_depth(l_buf, p_buf):
-    for j in range(2):
-        p_buf[j, 8:24, :] = jnp.where(l_buf[0, j] == 1, l_buf[1, j], 0)
-
-
-FIELD_SCRATCH = [
-    pltpu.VMEM((LV, 2, 32, 128), F32),
-    pltpu.VMEM((LV, 2, 32, 128), F32),
-    pltpu.VMEM((LV, 2, 32, 128), F32),
-    pltpu.VMEM((LV, 2, 32, 128), F32),
-    pltpu.SemaphoreType.DMA((14,)),
-]
-DEPTH_SCRATCH = [
-    pltpu.VMEM((2, 2, 16, 128), jnp.int32),
-    pltpu.VMEM((2, 32, 128), jnp.int32),
-    pltpu.SemaphoreType.DMA((4,)),
-]
-TRACER_SCRATCH = [
-    pltpu.VMEM((NT, LV, 2, 32, 128), F32),
-    pltpu.SemaphoreType.DMA((4,)),
-]
 
 
 def pack_lanes(sources):
@@ -188,13 +128,31 @@
     return pltpu.roll(packed, (4 * g - 4) % 128, 1)
 
 
-def tracer_pack_kernel(tr, y_up, y_dn, own, x_r, x_l, c_buf, c_sem):
-    copies = tracer_copies(tr, c_buf, c_sem)
-    for c in copies[0] + copies[1]:
+def tracer_pack_kernel(tr, reaction, y_up, y_dn, own, x_r, x_l, c_buf, kept, table, s_table, sem):
+    copies = [pltpu.make_async_copy(
+        tr.at[pl.ds(8 * s, 8), :, :, pl.ds(128 * j, 128)],
+        c_buf.at[pl.ds(8 * s, 8), :, j, pl.ds(8, 16), :], sem.at[2 * s + j]) for s in range(2) for j in range(2)]
+    for c in copies:
         c.start()
     low = sub_iota() < 4
     place = lane_iota() & 31
-    for c in copies[0] + copies[1]:
+    slot = lane_iota() >> 5
+    for s in range(2):
+        for a in range(PER):
+            for b in range(PER):
+                v = DT * reaction[s, a, b] + (1.0 if a == b else 0.0)
+                table[s * 64 + a * 8 + b] = jnp.full((8, 128), v, F32)
+    for s in range(2):
+        for go in range(2):
+            for gi in range(2):
+                for rho in range(4):
+                    v = jnp.zeros((8, 128), F32)
+                    for q in range(4):
+                        a, b = 4 * go + q, 4 * gi + (q - rho) % 4
+                        w = DT * reaction[s, a, b] + (1.0 if a == b else 0.0)
+                        v = jnp.where(slot == q, jnp.full((8, 128), w, F32), v)
+                    s_table[((s * 2 + go) * 2 + gi) * 4 + rho] = v
+    for c in copies:
         c.wait()
 
     @pl.loop(0, LV, unroll=2)
@@ -204,6 +162,8 @@
                 read = lambda b, r: c_buf[t + b, k, j, r:r + 8, :]
                 y_up[t * LV + k, j] = jnp.where(low, read(0, 20), read(PER, 16))
                 y_dn[t * LV + k, j] = jnp.where(low, read(0, 8), read(PER, 4))
+            for t in range(NT):
+                kept[t, k, j] = keep_rows(0, lambda r: c_buf[t, k, j, r:r + 8, :])
         for i in range(2):
             rows = slice(8 * i, 8 * i + 8)
             xr, xl = None, None
@@ -217,16 +177,34 @@
             x_l[k, rows, :] = xl
 
 
-def field_pack_kernel(scal, ho, hp, vo, vp, df, land, level, up_in, dn_in, y_up, y_dn, own,
-                      h_buf, u_buf, v_buf, d_buf, sem, l_buf, p_buf, l_sem, f_up, f_dn, out_sem):
+def keep_rows(n, read):
+    return jnp.where(sub_iota() < 6, read(4 + n), read(16 - n))
+
+
+def field_pack_kernel(scal, ho, hp, vo, vp, df, land, level, up_in, dn_in, y_up, y_dn, own, h_buf, u_buf, v_buf, d_buf, p_buf,
+                      f_up, f_dn, l_buf, sem, out_sem):
     off = scal[0] * (LV // 2)
-    copies = field_copies(ho, hp, vo, vp, df, off, h_buf, u_buf, v_buf, d_buf, sem) + depth_copies(land, level, l_buf, l_sem)
+    part = LV // 2
+    rows = pl.ds(8, 16)
+    copies = []
+    for j in range(2):
+        lanes = pl.ds(128 * j, 128)
+        for i, (h, v, at) in enumerate(((ho, vo, off), (hp, vp, part - off))):
+            levels = pl.ds(at, part)
+            copies.append(pltpu.make_async_copy(h.at[:, :, lanes], h_buf.at[levels, j, rows, :], sem.at[6 * j + 3 * i]))
+            copies.append(pltpu.make_async_copy(v.at[0, :, :, lanes], u_buf.at[levels, j, rows, :], sem.at[6 * j + 3 * i + 1]))
+            copies.append(pltpu.make_async_copy(v.at[1, :, :, lanes], v_buf.at[levels, j, rows, :], sem.at[6 * j + 3 * i + 2]))
+        copies.append(pltpu.make_async_copy(df.at[:, :, lanes], d_buf.at[:, j, rows, :], sem.at[12 + j]))
+        copies.append(pltpu.make_async_copy(land.at[:, lanes], l_buf.at[0, j], sem.at[14 + j]))
+        copies.append(pltpu.make_async_copy(level.at[:, lanes], l_buf.at[1, j], sem.at[16 + j]))
     for c in copies:
         c.start()
     low = sub_iota() < 4
     for c in copies:
         c.wait()
-    fill_depth(l_buf, p_buf)
+
+    for j in range(2):
+        p_buf[j, 8:24, :] = jnp.where(l_buf[0, j] == 1, l_buf[1, j], 0)
 
     def put(index, j, first, second):
         f_up[index, j] = jnp.where(low, first(20), second(16))
@@ -248,8 +226,8 @@
     @pl.loop(0, LV, unroll=4)
     def _(k):
         for i in range(2):
-            rows = slice(8 + 8 * i, 16 + 8 * i)
-            own[k, 8 * i:8 * i + 8, :] = pack_lanes([[buf[k, j, rows, :] for j in range(2)] for buf in (h_buf, u_buf, v_buf, d_buf)])
+            own[k, 8 * i:8 * i + 8, :] = pack_lanes(
+                [[buf[k, j, 8 + 8 * i:16 + 8 * i, :] for j in range(2)] for buf in (h_buf, u_buf, v_buf, d_buf)])
 
     for i in range(2):
         own[LV, 8 * i:8 * i + 8, :] = pack_lanes([[p_buf[j, 8 + 8 * i:16 + 8 * i, :].astype(F32) for j in range(2)]] * 4)
@@ -257,19 +235,8 @@
         c.wait()
 
 
-def inner_kernel(rows_total, scal, tr, ho, hp, vo, vp, df, land, level, reaction, saved_out, saved_f, mid, mid_f,
-                 h_buf, u_buf, v_buf, d_buf, sem, l_buf, p_buf, l_sem, c_buf, c_sem, c_alt, solved, coef, table, saved, out_sem):
-    off = scal[0] * (LV // 2)
-    fields = field_copies(ho, hp, vo, vp, df, off, h_buf, u_buf, v_buf, d_buf, sem)
-    depths = depth_copies(land, level, l_buf, l_sem)
-    tracer = tracer_copies(tr, c_buf, c_sem)
-    for c in depths + fields + tracer[0] + tracer[1]:
-        c.start()
-    fill_table(reaction, table)
-    for c in depths:
-        c.wait()
-    fill_depth(l_buf, p_buf)
-    six = sub_iota() < 6
+def inner_kernel(rows_total, scal, c_first, h_first, u_first, v_first, d_buf, p_buf, table, saved, saved_f, mid, mid_f,
+                 h_buf, u_buf, v_buf, c_one, c_two, solved, coef):
     rows = lax.broadcasted_iota(jnp.int32, (16, 128), 0) + scal[1]
     cor_c = coriolis_of(rows, rows_total)
     cor_s = coriolis_of(rows - 1, rows_total)
@@ -277,41 +244,17 @@
     d_e = [jnp.minimum(a, b) for a, b in zip(d_c, from_east(d_c))]
     d_n = [jnp.minimum(d_c[j], p_buf[j, 9:25, :]) for j in range(2)]
     d_s = [jnp.minimum(d_c[j], p_buf[j, 7:23, :]) for j in range(2)]
-    for c in fields:
-        c.wait()
-
-    def keep(n, read):
-        return jnp.where(six, read(4 + n), read(16 - n))
-
-    def keep_fields(n):
-        @pl.loop(0, LV)
-        def _(k):
-            for f, buf in enumerate((h_buf, u_buf, v_buf)):
-                for j in range(2):
-                    saved_f[n, f, k, j] = keep(n, lambda r: buf[k, j, r:r + 8, :])
-
-    def keep_tracers(n, buf):
-        @pl.loop(0, LV)
-        def _(k):
-            for t in range(NT):
-                for j in range(2):
-                    saved[n, t, k, j] = keep(n, lambda r: buf[t, k, j, r:r + 8, :])
-
-    keep_fields(0)
-    for c in tracer[0] + tracer[1]:
-        c.wait()
-    keep_tracers(0, c_buf)
-    leaving = [pltpu.make_async_copy(saved.at[n], saved_out.at[n], out_sem.at[n]) for n in range(ITERS)]
-    leaving[0].start()
+    buffers = (c_first, c_one, c_two, c_one, None)
     for n in range(1, ITERS + 1):
-        src, dst = (c_buf, c_alt) if n % 2 else (c_alt, c_buf)
+        src, dst = buffers[n - 1], buffers[n]
+        old = (h_first, u_first, v_first) if n == 1 else (h_buf, u_buf, v_buf)
 
         def dynamics(k, carry):
             up, prev = carry
             read = lambda buf, r: [buf[k, j, r:r + 16, :] for j in range(2)]
             h_new, u_new, v_new, co, links, ratios = level_step(
-                k, read(h_buf, 7), read(h_buf, 8), read(h_buf, 9), read(u_buf, 7), read(u_buf, 8),
-                read(v_buf, 7), read(v_buf, 8), (d_c, d_e, d_n, d_s), cor_c, cor_s, read(d_buf, 8), up, prev)
+                k, read(old[0], 7), read(old[0], 8), read(old[0], 9), read(old[1], 7), read(old[1], 8),
+                read(old[2], 7), read(old[2], 8), (d_c, d_e, d_n, d_s), cor_c, cor_s, read(d_buf, 8), up, prev)
             for j in range(2):
                 h_buf[k, j, 8:24, :] = h_new[j]
                 u_buf[k, j, 8:24, :] = u_new[j]
@@ -321,13 +264,14 @@
             return links, ratios
 
         lax.fori_loop(0, LV, dynamics, (zeros_like_tiles(16, 2), zeros_like_tiles(16, 2)), unroll=4)
-        if n < ITERS:
-            keep_fields(n)
-        else:
-            @pl.loop(0, LV)
-            def _(k):
-                for f, buf in enumerate((h_buf, u_buf, v_buf)):
-                    for j in range(2):
+
+        @pl.loop(0, LV)
+        def _(k):
+            for f, buf in enumerate((h_buf, u_buf, v_buf)):
+                for j in range(2):
+                    if n < ITERS:
+                        saved_f[n - 1, f, k, j] = keep_rows(n, lambda r: buf[k, j, r:r + 8, :])
+                    else:
                         mid_f[f, k, j] = buf[k, j, 12:20, :]
 
         for r0 in ((8, 16) if n < ITERS else (12,)):
@@ -359,16 +303,14 @@
 
                 lax.fori_loop(0, LV, upward, [zeros_like_tiles(8, 2) for _ in range(PER)], unroll=4)
         if n < ITERS:
-            keep_tracers(n, dst)
-            leaving[n].start()
-    for c in leaving:
-        c.wait()
-
-
-def halo_pack_kernel(y_s, y_n, own_f, r_own, l_own, halo, x_r, x_l, s_buf, n_buf, sem):
-    copies = [pltpu.make_async_copy(y_s, s_buf, sem.at[0]), pltpu.make_async_copy(y_n, n_buf, sem.at[1])]
-    for c in copies:
-        c.start()
+            @pl.loop(0, LV)
+            def _(k):
+                for t in range(NT):
+                    for j in range(2):
+                        saved[n - 1, t, k, j] = keep_rows(n, lambda r: dst[t, k, j, r:r + 8, :])
+
+
+def halo_pack_kernel(y_s, y_n, own_f, r_own, l_own, halo, x_r, x_l):
     low = sub_iota() < 4
     place = lane_iota() & 31
     for i in range(2):
@@ -383,11 +325,8 @@
             x_r[k, rows, :] = jnp.where(place >= 16, to_east(own_f[k, rows, :], 4), r_own[k, rows, :])
             x_l[k, rows, :] = jnp.where(place >= 16, to_west(own_f[k, rows, :], 4), l_own[k, rows, :])
 
-    for c in copies:
-        c.wait()
-
     def pair(index, j):
-        ys, yn = s_buf[index, j], n_buf[index, j]
+        ys, yn = y_s[index, j], y_n[index, j]
         return jnp.where(low, ys, pltpu.roll(yn, 4, 0)), jnp.where(low, pltpu.roll(ys, 4, 0), yn)
 
     @pl.loop(0, LV, unroll=2)
@@ -414,32 +353,21 @@
     x_l[LV, 16:24, :] = to_west(packed, 4)
 
 
-def edge_kernel(rows_total, scal, saved, saved_f, south, north, df, land, level, reaction, out_c, out_f,
-                c_buf, f_buf, d_buf, l_buf, p_buf, l_sem, solved, coef, table, y_s, y_n, sem):
-    copies = [pltpu.make_async_copy(south, y_s, sem.at[10]), pltpu.make_async_copy(north, y_n, sem.at[11])]
-    copies += depth_copies(land, level, l_buf, l_sem)
-    for n in range(ITERS):
-        copies.append(pltpu.make_async_copy(saved_f.at[n], f_buf.at[n, :, :, :, pl.ds(0, 8), :], sem.at[n]))
-    for j in range(2):
-        copies.append(pltpu.make_async_copy(df.at[:, :, pl.ds(128 * j, 128)], d_buf.at[:, j, pl.ds(8, 16), :], sem.at[4 + j]))
-    tracer = [pltpu.make_async_copy(saved.at[n], c_buf.at[n, :, :, :, pl.ds(0, 8), :], sem.at[6 + n]) for n in range(ITERS)]
-    for c in copies + tracer:
+def edge_kernel(rows_total, scal, kept, saved, saved_f, h_first, u_first, v_first, y_s, y_n, d_first, p_first, table,
+                out_c, out_f, c_buf, f_buf, d_buf, p_buf, solved, coef, sem):
+    tracer = [None] + [pltpu.make_async_copy(saved.at[n - 1], c_buf.at[n, :, :, :, pl.ds(0, 8), :], sem.at[n]) for n in range(1, ITERS)]
+    fields = [None] + [pltpu.make_async_copy(saved_f.at[n - 1], f_buf.at[n, :, :, :, pl.ds(0, 8), :], sem.at[3 + n]) for n in range(1, ITERS)]
+    for c in fields[1:] + tracer[1:]:
         c.start()
-    fill_table(reaction, table)
     sub = sub_iota()
     low = sub < 4
-    for c in copies:
-        c.wait()
-    fill_depth(l_buf, p_buf)
-    tracer[0].wait()
-
-    def put(ref, y, half, south):
-        if half != (0 if south else 1):
-            y = pltpu.roll(y, 4, 0)
-        if south:
-            pltpu.store(ref.at[pl.ds(0, 8), :], y, mask=low)
-        else:
-            pltpu.store(ref.at[pl.ds(4, 8), :], y, mask=jnp.logical_not(low))
+    high = jnp.logical_not(low)
+
+    def put(ref, inside, ys, yn, half):
+        south = ys if half == 0 else pltpu.roll(ys, 4, 0)
+        north = yn if half == 1 else pltpu.roll(yn, 4, 0)
+        ref[0:8, :] = jnp.where(low, south, inside)
+        pltpu.store(ref.at[pl.ds(4, 8), :], north, mask=high)
 
     @pl.loop(0, LV, unroll=2)
     def _(k):
@@ -447,25 +375,27 @@
             for t in range(PER):
                 ys, yn = y_s[t * LV + k, j], y_n[t * LV + k, j]
                 for half in range(2):
-                    put(c_buf.at[0, t + PER * half, k, j], ys, half, True)
-                    put(c_buf.at[0, t + PER * half, k, j], yn, half, False)
-            for f, (index, half) in enumerate(((128, 0), (128, 1), (144, 0))):
-                put(f_buf.at[0, f, k, j], y_s[index + k, j], half, True)
-                put(f_buf.at[0, f, k, j], y_n[index + k, j], half, False)
+                    put(c_buf.at[0, t + PER * half, k, j], kept[t + PER * half, k, j], ys, yn, half)
+            for f, (buf, index, half) in enumerate(((h_first, 128, 0), (u_first, 128, 1), (v_first, 144, 0))):
+                inside = keep_rows(0, lambda r: buf[k, j, r:r + 8, :])
+                put(f_buf.at[0, f, k, j], inside, y_s[index + k, j], y_n[index + k, j], half)
             ys, yn = y_s[144 + k, j], y_n[144 + k, j]
-            pltpu.store(d_buf.at[k, j, pl.ds(0, 8), :], ys, mask=jnp.logical_not(low))
-            pltpu.store(d_buf.at[k, j, pl.ds(24, 8), :], pltpu.roll(yn, 4, 0), mask=low)
+            d_buf[k, j, 0:8, :] = ys
+            d_buf[k, j, 8:16, :] = d_first[k, j, 8:16, :]
+            d_buf[k, j, 16:24, :] = d_first[k, j, 16:24, :]
+            d_buf[k, j, 24:32, :] = pltpu.roll(yn, 4, 0)
 
     for j in range(2):
-        ys, yn = y_s[160, j].astype(jnp.int32), y_n[160, j].astype(jnp.int32)
-        pltpu.store(p_buf.at[j, pl.ds(0, 8), :], ys, mask=jnp.logical_not(low))
-        pltpu.store(p_buf.at[j, pl.ds(24, 8), :], yn, mask=low)
+        p_buf[j, 0:8, :] = y_s[160, j].astype(jnp.int32)
+        p_buf[j, 8:24, :] = p_first[j, 8:24, :]
+        p_buf[j, 24:32, :] = y_n[160, j].astype(jnp.int32)
 
     def gather(read, shift):
         return jnp.where(low, read(shift), read(shift + 2))
 
     for n in range(1, ITERS + 1):
         if n < ITERS:
+            fields[n].wait()
             tracer[n].wait()
 
         def at(buf, j, shift):
@@ -532,25 +462,11 @@
             lax.fori_loop(0, LV, upward, [zeros_like_tiles(8, 2) for _ in range(PER)], unroll=4)
 
 
-def strip_kernel(rows_total, scal, own, own_f, halo, x_w, x_e, reaction, mid_in, mid_f, edge_in, edge_f, out, out_h, out_v,
-                 c_buf, c_alt, h_buf, u_buf, v_buf, d_buf, p_buf, solved, coef, table, mid, edge, out_c, sem):
-    arriving = [pltpu.make_async_copy(mid_in, mid, sem.at[0]), pltpu.make_async_copy(edge_in, edge, sem.at[1])]
-    for c in arriving:
-        c.start()
+def strip_kernel(rows_total, scal, own, own_f, halo, x_w, x_e, table, mid, mid_f, edge, edge_f, out, out_h, out_v,
+                 c_buf, c_alt, h_buf, u_buf, v_buf, d_buf, p_buf, solved, coef, out_c, sem):
     lane = lane_iota()
     place = lane & 31
-    slot = lane >> 5
     low = sub_iota() < 4
-    for s in range(2):
-        for go in range(2):
-            for gi in range(2):
-                for rho in range(4):
-                    v = jnp.zeros((8, 128), F32)
-                    for q in range(4):
-                        a, b = 4 * go + q, 4 * gi + (q - rho) % 4
-                        w = DT * reaction[s, a, b] + (1.0 if a == b else 0.0)
-                        v = jnp.where(slot == q, jnp.full((8, 128), w, F32), v)
-                    table[((s * 2 + go) * 2 + gi) * 4 + rho] = v
 
     def whole(k, g, i, xg):
         rows = slice(8 * i, 8 * i + 8)
@@ -653,8 +569,6 @@
             return jnp.where(lane < 4, pltpu.roll(strip, (-(32 * q + 4)) % 128, 1), body)
         return jnp.where(lane >= 124, pltpu.roll(strip, (100 - 32 * q) % 128, 1), body)
 
-    for c in arriving:
-        c.wait()
     leaving = []
     for part in range(4):
         @pl.loop(4 * part, 4 * part + 4, unroll=2)
@@ -666,7 +580,7 @@
                         out_c[t, k, 8 * i:8 * i + 8, 128 * j:128 * j + 128] = merge(
                             mid[t, k, j], edge[t, k, j], strip, t % 4, j, i)
         levels = pl.ds(4 * part, 4)
-        leaving.append(pltpu.make_async_copy(out_c.at[:, levels], out.at[:, levels], sem.at[2 + part]))
+        leaving.append(pltpu.make_async_copy(out_c.at[:, levels], out.at[:, levels], sem.at[part]))
         leaving[part].start()
 
     off = scal[0] * (LV // 2)
@@ -686,6 +600,10 @@
         c.wait()
 
 
+def room(mebibytes):
+    return pltpu.CompilerParams(vmem_limit_bytes=mebibytes * 1024 * 1024)
+
+
 def sds(*shape):
     return jax.ShapeDtypeStruct(shape, F32)
 
@@ -696,23 +614,28 @@
     set_index = lax.axis_index("set").astype(jnp.int32)
     row_start = lax.axis_index("ty").astype(jnp.int32) * rows_local
     scal = jnp.stack([set_index, row_start])
-    params = pltpu.CompilerParams(vmem_limit_bytes=VMEM_LIMIT)
     swap = [(0, 1), (1, 0)]
     h_pair = lax.ppermute(thickness, "set", swap)
     v_pair = lax.ppermute(velocity, "set", swap)
-    up_part, dn_part, own, r_own, l_own = pl.pallas_call(
+    field = sds(LV, 2, 32, 128)
+    y_shape = sds(161, 2, 8, 128)
+    up_part, dn_part, own, r_own, l_own, c_first, kept, table, s_table = pl.pallas_call(
         tracer_pack_kernel,
-        out_shape=[sds(161, 2, 8, 128), sds(161, 2, 8, 128), sds(LV, 4, 16, 128), sds(LV, 16, 128), sds(LV, 16, 128)],
-        in_specs=[ANY], out_specs=[VMEM] * 5, scratch_shapes=TRACER_SCRATCH,
-        compiler_params=params, name="tracer_pack")(tracers)
+        out_shape=[y_shape, y_shape, sds(LV, 4, 16, 128), sds(LV, 16, 128), sds(LV, 16, 128), sds(NT, LV, 2, 32, 128),
+                   sds(NT, LV, 2, 8, 128), sds(128, 8, 128), sds(32, 8, 128)],
+        in_specs=[ANY, SMEM], out_specs=[VMEM] * 9,
+        scratch_shapes=[pltpu.SemaphoreType.DMA((4,))],
+        compiler_params=room(4), name="tracer_pack")(tracers, reaction)
     h_pair, v_pair, up_part, dn_part = lax.optimization_barrier((h_pair, v_pair, up_part, dn_part))
-    fields = (thickness, h_pair, velocity, v_pair, diffusivity, land_mask, level_count)
-    y_up, y_dn, own_f = pl.pallas_call(
-        field_pack_kernel, out_shape=[sds(161, 2, 8, 128), sds(161, 2, 8, 128), sds(LV + 1, 16, 128)],
-        in_specs=[SMEM] + [ANY] * 9, out_specs=[ANY, ANY, VMEM], input_output_aliases={8: 0, 9: 1},
-        scratch_shapes=FIELD_SCRATCH + DEPTH_SCRATCH + [
-            pltpu.VMEM((33, 2, 8, 128), F32), pltpu.VMEM((33, 2, 8, 128), F32), pltpu.SemaphoreType.DMA((2,))],
-        compiler_params=params, name="field_pack")(scal, *fields, up_part, dn_part)
+    y_up, y_dn, own_f, h_first, u_first, v_first, d_first, p_first = pl.pallas_call(
+        field_pack_kernel, out_shape=[y_shape, y_shape, sds(LV + 1, 16, 128)] + [field] * 4 + [jax.ShapeDtypeStruct((2, 32, 128), jnp.int32)],
+        in_specs=[SMEM] + [ANY] * 9, out_specs=[ANY, ANY] + [VMEM] * 6,
+        input_output_aliases={8: 0, 9: 1},
+        scratch_shapes=[pltpu.VMEM((33, 2, 8, 128), F32), pltpu.VMEM((33, 2, 8, 128), F32),
+                        pltpu.VMEM((2, 2, 16, 128), jnp.int32),
+                        pltpu.SemaphoreType.DMA((18,)), pltpu.SemaphoreType.DMA((2,))],
+        compiler_params=room(4), name="field_pack")(
+            scal, thickness, h_pair, velocity, v_pair, diffusivity, land_mask, level_count, up_part, dn_part)
     ty = lax.axis_size("ty")
     north = [(i, i + 1) for i in range(ty - 1)]
     south = [(j, i) for i, j in north]
@@ -720,22 +643,19 @@
     y_n = lax.ppermute(y_dn, "ty", south)
     saved, saved_f, mid, mid_f = pl.pallas_call(
         lambda *a: inner_kernel(rows_total, *a),
-        out_shape=[sds(ITERS, NT, LV, 2, 8, 128), sds(ITERS, 3, LV, 2, 8, 128), sds(NT, LV, 2, 8, 128), sds(3, LV, 2, 8, 128)],
-        in_specs=[SMEM] + [ANY] * 8 + [SMEM], out_specs=[ANY] + [VMEM] * 3,
-        scratch_shapes=FIELD_SCRATCH + DEPTH_SCRATCH + TRACER_SCRATCH + [
+        out_shape=[sds(ITERS - 1, NT, LV, 2, 8, 128), sds(ITERS - 1, 3, LV, 2, 8, 128), sds(NT, LV, 2, 8, 128), sds(3, LV, 2, 8, 128)],
+        in_specs=[SMEM] + [VMEM] * 7, out_specs=[VMEM] * 4,
+        scratch_shapes=[pltpu.VMEM((LV, 2, 32, 128), F32)] * 3 + [
+            pltpu.VMEM((NT, LV, 2, 32, 128), F32),
             pltpu.VMEM((NT, LV, 2, 32, 128), F32),
             pltpu.VMEM((LV, PER, 2, 8, 128), F32),
-            pltpu.VMEM((7, LV, 2, 16, 128), F32),
-            pltpu.VMEM((128, 8, 128), F32),
-            pltpu.VMEM((ITERS, NT, LV, 2, 8, 128), F32),
-            pltpu.SemaphoreType.DMA((ITERS,))],
-        compiler_params=params, name="inner")(scal, tracers, *fields, reaction)
+            pltpu.VMEM((7, LV, 2, 16, 128), F32)],
+        compiler_params=room(24), name="inner")(scal, c_first, h_first, u_first, v_first, d_first, p_first, table)
     y_s, y_n, mid_f = lax.optimization_barrier((y_s, y_n, mid_f))
     halo, x_r, x_l = pl.pallas_call(
         halo_pack_kernel, out_shape=[sds(LV + 1, 5, 8, 128), sds(LV + 1, 24, 128), sds(LV + 1, 24, 128)],
-        in_specs=[ANY, ANY] + [VMEM] * 3, out_specs=[VMEM] * 3,
-        scratch_shapes=[pltpu.VMEM((161, 2, 8, 128), F32), pltpu.VMEM((161, 2, 8, 128), F32), pltpu.SemaphoreType.DMA((2,))],
-        compiler_params=params, name="halo_pack")(y_s, y_n, own_f, r_own, l_own)
+        in_specs=[VMEM] * 5, out_specs=[VMEM] * 3,
+        compiler_params=room(4), name="halo_pack")(y_s, y_n, own_f, r_own, l_own)
     tx = lax.axis_size("tx")
     east = [(i, (i + 1) % tx) for i in range(tx)]
     west = [(j, i) for i, j in east]
@@ -744,22 +664,21 @@
     edge, edge_f = pl.pallas_call(
         lambda *a: edge_kernel(rows_total, *a),
         out_shape=[sds(NT, LV, 2, 8, 128), sds(3, LV, 2, 8, 128)],
-        in_specs=[SMEM] + [ANY] * 7 + [SMEM], out_specs=[VMEM] * 2,
+        in_specs=[SMEM] + [VMEM] * 11, out_specs=[VMEM] * 2,
         scratch_shapes=[
             pltpu.VMEM((ITERS, NT, LV, 2, 16, 128), F32),
             pltpu.VMEM((ITERS, 3, LV, 2, 16, 128), F32),
-            pltpu.VMEM((LV, 2, 32, 128), F32)] + DEPTH_SCRATCH + [
+            pltpu.VMEM((LV, 2, 32, 128), F32),
+            pltpu.VMEM((2, 32, 128), jnp.int32),
             pltpu.VMEM((LV, PER, 2, 8, 128), F32),
             pltpu.VMEM((7, LV, 2, 8, 128), F32),
-            pltpu.VMEM((128, 8, 128), F32),
-            pltpu.VMEM((161, 2, 8, 128), F32),
-            pltpu.VMEM((161, 2, 8, 128), F32),
-            pltpu.SemaphoreType.DMA((12,))],
-        compiler_params=params, name="edge")(scal, saved, saved_f, y_s, y_n, diffusivity, land_mask, level_count, reaction)
+            pltpu.SemaphoreType.DMA((2 * ITERS,))],
+        compiler_params=room(24), name="edge")(
+            scal, kept, saved, saved_f, h_first, u_first, v_first, y_s, y_n, d_first, p_first, table)
     return pl.pallas_call(
         lambda *a: strip_kernel(rows_total, *a),
         out_shape=[sds(*tracers.shape), sds(*thickness.shape), sds(*velocity.shape)],
-        in_specs=[SMEM] + [VMEM] * 5 + [SMEM, ANY, VMEM, ANY, VMEM], out_specs=[ANY, VMEM, VMEM],
+        in_specs=[SMEM] + [VMEM] * 10, out_specs=[ANY, VMEM, VMEM],
         scratch_shapes=[
             pltpu.VMEM((4, LV, 40, 128), F32),
             pltpu.VMEM((4, LV, 40, 128), F32),
@@ -770,12 +689,9 @@
             pltpu.VMEM((40, 128), jnp.int32),
             pltpu.VMEM((LV, 4, 3, 8, 128), F32),
             pltpu.VMEM((7, LV, 24, 128), F32),
-            pltpu.VMEM((32, 8, 128), F32),
-            pltpu.VMEM((NT, LV, 2, 8, 128), F32),
-            pltpu.VMEM((NT, LV, 2, 8, 128), F32),
             pltpu.VMEM((NT, LV, 16, 256), F32),
-            pltpu.SemaphoreType.DMA((6,))],
-        compiler_params=params, name="strips")(scal, own, own_f, halo, x_w, x_e, reaction, mid, mid_f, edge, edge_f)
+            pltpu.SemaphoreType.DMA((4,))],
+        compiler_params=room(14), name="strips")(scal, own, own_f, halo, x_w, x_e, s_table, mid, mid_f, edge, edge_f)
 
 
 def solution(mesh):

time: 105 us -> 85.7 us (0.82)
  Pallas kernels: 83 us -> 64.5 us
    pallas_call x1, Pallas kernels: 30.6 us -> 25.2 us  [body(): pl.pallas_call(lambda *a: inner_kernel(rows_total, *a), out_shape=[sds(IT...]
    pallas_call x2, Pallas kernels: 11.2 us -> 6.76 us  [the longest x1 5.13 us: body(): pl.pallas_call(tracer_pack_kernel, out_shape=[y_shape, y_shape, sds(LV, 4...]
    pallas_call x1, Pallas kernels: 19.6 us -> 15.4 us  [body(): pl.pallas_call(lambda *a: edge_kernel(rows_total, *a), out_shape=[sds(NT,...]
    pallas_call x1, Pallas kernels: 5.69 us -> 2.53 us  [body(): pl.pallas_call(halo_pack_kernel, out_shape=[sds(LV + 1, 5, 8, 128), sds(L...]
    pallas_call x1, Pallas kernels: 15.9 us -> 14.7 us  [body(): pl.pallas_call(lambda *a: strip_kernel(rows_total, *a), out_shape=[sds(*t...]
    unnamed x12 -> x14, local copies, waits for them, and re-layouts: 2.92 us -> 2.9 us
  transfers between devices with their start and end apart: 6 -> 6, of which waited for: 1 -> 1; matrix products, arithmetic and copies ran while one was open for 1% -> 0% of each run, Pallas kernels for 55% -> 54%
where the time goes in v4:
time: 85.7 us; the launch traced here: 85.4 us
  Pallas kernels  64.5 us (75%)
  starting transfers between devices  16.2 us (19%)
  local copies, waits for them, and re-layouts  2.9 us (3%)
  between operations  0.92 us (1%)
    pallas_call x1, Pallas kernels, body(): pl.pallas_call(lambda *a: inner_kernel(rows_total, *a), out_shape=[sds(IT...  25.2 us
    pallas_call x1, Pallas kernels, body(): pl.pallas_call(lambda *a: edge_kernel(rows_total, *a), out_shape=[sds(NT,...  15.4 us
    pallas_call x1, Pallas kernels, body(): pl.pallas_call(lambda *a: strip_kernel(rows_total, *a), out_shape=[sds(*t...  14.7 us
    ppermute x1, starting transfers between devices, body(): y_s = lax.ppermute(y_up, 'ty', north)  6.46 us
    pallas_call x1, Pallas kernels, body(): pl.pallas_call(tracer_pack_kernel, out_shape=[y_shape, y_shape, sds(LV, 4...  5.13 us
    ppermute x1, starting transfers between devices, body(): x_e = lax.ppermute(x_l, 'tx', west)  3.84 us
    unnamed x14, local copies, waits for them, and re-layouts  2.9 us
    ppermute x1, starting transfers between devices, body(): v_pair = lax.ppermute(velocity, 'set', swap)  2.55 us
  transfers between devices with their start and end apart: 6, of which 1 were waited for; matrix products, arithmetic and copies ran while one was open for 0% of the time, Pallas kernels for 54%

profile of v4, /device:TPU:1, one launch (start us, length us, event | category | flops | bytes accessed | tf_op | source)
XLA Modules:
  0.0 85.4 jit_solution(16250408823399118053)
XLA Ops:
  0.6 2.5 %collective-permute-start.1 = (f32[2,8,16,256]{3,2,1,0:T(8,128)}, f32[2,8,16,256]{3,2,1,0:T(8,128)S(1)}, u32[]{:S(2)}, u32[]{:S(2)}) collective-permute-start(f32[2,8,16,256]{3,2,1,0:T(8,128)} %vo.1), channel_id=1, source_target_pairs={{0,64},{64,0},{1,65},{65,1},{2,66},{66,2},{3,67},{67,3},{4,68},{68... | collective-permute-start | bytes 786440 | tf_op jit(solution)/shard_map/ppermute | solution.py:619
  3.2 0.1 collective-permute-start
  3.3 0.0 copy-start
  3.3 2.2 %copy-done = f32[16,16,16,256]{3,2,1,0:T(8,128)S(1)} copy-done((f32[16,16,16,256]{3,2,1,0:T(8,128)S(1)}, f32[16,16,16,256]{3,2,1,0:T(8,128)}, u32[]{:S(2)}) %copy-start) | copy-done | bytes 4194328
  5.5 0.0 copy-start.6
  5.5 0.7 copy-done.6
  6.2 0.0 copy-start.1
  6.2 0.0 copy-start.2
  6.2 0.0 copy-start.3
  6.2 0.0 copy-start.4
  6.2 0.0 copy-start.5
  6.2 5.1 %tracer_pack.1 = (f32[161,2,8,128]{3,2,1,0:T(8,128)S(1)}, f32[161,2,8,128]{3,2,1,0:T(8,128)S(1)}, f32[16,4,16,128]{3,2,1,0:T(8,128)S(1)}, f32[16,16,128]{2,1,0:T...) custom-call(f32[16,16,16,256]{3,2,1,0:T(8,128)S(1)} %copy-done, ...), custom_call_target="tpu_custom_call" | custom-call | tf_op jit(solution)/shard_map/tracer_pack/pallas_call | solution.py:622
  11.3 0.1 pad_add_fusion.scal.a_0_
  11.4 0.8 collective-permute-done.hp
  12.2 0.0 collective-permute-done.1.vp
  12.2 0.0 copy-done.1
  12.2 0.0 copy-done.2
  12.2 0.0 copy-done.3
  12.2 0.0 copy-done.4
  12.2 0.0 copy-done.5
  12.2 1.6 %field_pack.1 = (f32[161,2,8,128]{3,2,1,0:T(8,128)S(1)}, f32[161,2,8,128]{3,2,1,0:T(8,128)S(1)}, f32[17,16,128]{2,1,0:T(8,128)S(1)}, f32[16,2,32,128]{3,2,1,0:T(...) custom-call(s32[2]{0:T(128)S(1)} %pad_add_fusion.scal.a_0_, ...), custom_call_target="tpu_custom_call", output_to_operand_aliasing={{0}: (8, {}), {1}: (9, {})} | custom-call | tf_op jit(solution)/shard_map/field_pack/pallas_call | solution.py:630
  13.9 6.5 %collective-permute-start.2 = (f32[161,2,8,128]{3,2,1,0:T(8,128)S(1)}, f32[161,2,8,128]{3,2,1,0:T(8,128)S(1)}, u32[]{:S(2)}, u32[]{:S(2)}) collective-permute-start(f32[161,2,8,128]{3,2,1,0:T(8,128)S(1)} %get-tuple-element.44), channel_id=1, source_target_pairs={{0,1},{1,2},{2,3},{4,5},{5,6},{6,7},{8,9},{9,10},{10,11},{12,13},{... | collective-permute-start | bytes 3956744 | tf_op jit(solution)/shard_map/ppermute | solution.py:642
  20.4 1.9 %collective-permute-start.3 = (f32[161,2,8,128]{3,2,1,0:T(8,128)S(1)}, f32[161,2,8,128]{3,2,1,0:T(8,128)S(1)}, u32[]{:S(2)}, u32[]{:S(2)}) collective-permute-start(f32[161,2,8,128]{3,2,1,0:T(8,128)S(1)} %get-tuple-element.45), channel_id=1, source_target_pairs={{1,0},{2,1},{3,2},{5,4},{6,5},{7,6},{9,8},{10,9},{11,10},{13,12},{... | collective-permute-start | bytes 3956744 | tf_op jit(solution)/shard_map/ppermute | solution.py:643
  22.3 25.2 %inner.1 = (f32[3,16,16,2,8,128]{5,4,3,2,1,0:T(8,128)S(1)}, f32[3,3,16,2,8,128]{5,4,3,2,1,0:T(8,128)S(1)}, f32[16,16,2,8,128]{4,3,2,1,0:T(8,128)S(1)}, f32[3,16,2,8,128]{4,3,2,1,0:T(8,128)S(1)}) custom-call(s32[2]{0:T(128)S(1)} %pad_add_fusion.scal.a_0_, f32[16,16,2,32,128]{4,3,2,1,0:T(8,128)S(1)} %get-tuple-element.46.a_1_, ...), custom_call_target="tpu_custom_call" | custom-call | tf_op jit(solution)/shard_map/inner/pallas_call | solution.py:644
  47.5 0.0 collective-permute-done.2.y_s.a_7_
  47.5 0.0 collective-permute-done.3.y_n.a_8_
  47.5 2.5 %halo_pack.1 = (f32[17,5,8,128]{3,2,1,0:T(8,128)S(1)}, f32[17,24,128]{2,1,0:T(8,128)S(1)}, f32[17,24,128]{2,1,0:T(8,128)S(1)}) custom-call(f32[161,2,8,128]{3,2,1,0:T(8,128)S(1)} %collective-permute-done.2.y_s.a_7_, f32[161,2,8,128]{3,2,1,0:T(8,128)S(1)} %collective-permute-done.3.y_n.a_8_, f32[17,16,128]{2,1,0:T(8,128)S(1)} %get-tuple-element.43.own_f.a_2_, ...), custom_call_target="tpu_custom_call" | custom-call | tf_op jit(solution)/shard_map/halo_pack/pallas_call | solution.py:655
  50.0 1.3 %collective-permute-start.4 = (f32[17,24,128]{2,1,0:T(8,128)S(1)}, f32[17,24,128]{2,1,0:T(8,128)S(1)}, u32[]{:S(2)}, u32[]{:S(2)}) collective-permute-start(f32[17,24,128]{2,1,0:T(8,128)S(1)} %get-tuple-element.59), channel_id=1, source_target_pairs={{0,4},{4,8},{8,12},{12,16},{16,20},{20,24},{24,28},{28,32},{32,36}... | collective-permute-start | bytes 626696 | tf_op jit(solution)/shard_map/ppermute | solution.py:662
  51.4 3.8 %collective-permute-start.5 = (f32[17,24,128]{2,1,0:T(8,128)S(1)}, f32[17,24,128]{2,1,0:T(8,128)S(1)}, u32[]{:S(2)}, u32[]{:S(2)}) collective-permute-start(f32[17,24,128]{2,1,0:T(8,128)S(1)} %get-tuple-element.60), channel_id=1, source_target_pairs={{4,0},{8,4},{12,8},{16,12},{20,16},{24,20},{28,24},{32,28},{36,32}... | collective-permute-start | bytes 626696 | tf_op jit(solution)/shard_map/ppermute | solution.py:663
  55.2 15.4 %edge.1 = (f32[16,16,2,8,128]{4,3,2,1,0:T(8,128)S(1)}, f32[3,16,2,8,128]{4,3,2,1,0:T(8,128)S(1)}) custom-call(s32[2]{0:T(128)S(1)} %pad_add_fusion.scal.a_0_, f32[16,16,2,8,128]{4,3,2,1,0:T(8,128)S(1)} %get-tuple-element.64.a_1_, f32[3,16,16,2,8,128]{5,4,3,2,1,0:T(8,128)S(1)} %get-tuple-element.65.a_2_, ...), custom_call_target="tpu_custom_call" | custom-call | tf_op jit(solution)/shard_map/edge/pallas_call | solution.py:664
  70.6 0.0 collective-permute-done.4.a_4_
  70.6 0.0 collective-permute-done.5.a_5_
  70.6 14.7 %strips.1 = (f32[16,16,16,256]{3,2,1,0:T(8,128)}, f32[8,16,256]{2,1,0:T(8,128)}, f32[2,8,16,256]{3,2,1,0:T(8,128)}) custom-call(s32[2]{0:T(128)S(1)} %pad_add_fusion.scal.a_0_, f32[16,4,16,128]{3,2,1,0:T(8,128)S(1)} %get-tuple-element.36.a_1_, f32[17,16,128]{2,1,0:T(8,128)S(1)} %get-tuple-element.43.own_f.a_2_, ...), custom_call_target="tpu_custom_call" | custom-call | tf_op jit(solution)/shard_map/strips/pallas_call | solution.py:678
Async XLA Ops:
  0.6 11.6 %collective-permute-start.1 = (f32[2,8,16,256]{3,2,1,0:T(8,128)}, f32[2,8,16,256]{3,2,1,0:T(8,128)S(1)}, u32[]{:S(2)}, u32[]{:S(2)}) collective-permute-start(f32[2,8,16,256]{3,2,1,0:T(8,128)} %vo.1), channel_id=1, source_target_pairs={{0,64},{64,0},{1,65},{65,1},{2,66},{66,2},{3,67},{67,3},{4,68},{68... | collective-permute-start | bytes 786440 | tf_op jit(solution)/shard_map/ppermute | solution.py:619
  3.2 9.0 %collective-permute-start = (f32[8,16,256]{2,1,0:T(8,128)}, f32[8,16,256]{2,1,0:T(8,128)S(1)}, u32[]{:S(2)}, u32[]{:S(2)}) collective-permute-start(f32[8,16,256]{2,1,0:T(8,128)} %ho.1), channel_id=1, source_target_pairs={{0,64},{64,0},{1,65},{65,1},{2,66},{66,2},{3,67},{67,3},{4,68},{68... | collective-permute-start | bytes 393224 | tf_op jit(solution)/shard_map/ppermute | solution.py:618
  3.3 2.2 %copy-start = (f32[16,16,16,256]{3,2,1,0:T(8,128)S(1)}, f32[16,16,16,256]{3,2,1,0:T(8,128)}, u32[]{:S(2)}) copy-start(f32[16,16,16,256]{3,2,1,0:T(8,128)} %tr.1) | copy-start | bytes 12582916
  5.5 0.7 copy-start.6
  6.2 6.1 %copy-start.1 = (f32[2,8,16,256]{3,2,1,0:T(8,128)S(1)}, f32[2,8,16,256]{3,2,1,0:T(8,128)}, u32[]{:S(2)}) copy-start(f32[2,8,16,256]{3,2,1,0:T(8,128)} %vo.1) | copy-start | bytes 786436
  6.2 6.1 %copy-start.2 = (f32[16,16,256]{2,1,0:T(8,128)S(1)}, f32[16,16,256]{2,1,0:T(8,128)}, u32[]{:S(2)}) copy-start(f32[16,16,256]{2,1,0:T(8,128)} %df.1) | copy-start | bytes 786436
  6.2 6.1 %copy-start.3 = (f32[8,16,256]{2,1,0:T(8,128)S(1)}, f32[8,16,256]{2,1,0:T(8,128)}, u32[]{:S(2)}) copy-start(f32[8,16,256]{2,1,0:T(8,128)} %ho.1) | copy-start | bytes 393220
  6.2 6.1 %copy-start.4 = (s32[16,256]{1,0:T(8,128)S(1)}, s32[16,256]{1,0:T(8,128)}, u32[]{:S(2)}) copy-start(s32[16,256]{1,0:T(8,128)} %land.1) | copy-start | bytes 49156
  6.2 6.1 %copy-start.5 = (s32[16,256]{1,0:T(8,128)S(1)}, s32[16,256]{1,0:T(8,128)}, u32[]{:S(2)}) copy-start(s32[16,256]{1,0:T(8,128)} %level.1) | copy-start | bytes 49156
  13.9 33.6 %collective-permute-start.2 = (f32[161,2,8,128]{3,2,1,0:T(8,128)S(1)}, f32[161,2,8,128]{3,2,1,0:T(8,128)S(1)}, u32[]{:S(2)}, u32[]{:S(2)}) collective-permute-start(f32[161,2,8,128]{3,2,1,0:T(8,128)S(1)} %get-tuple-element.44), channel_id=1, source_target_pairs={{0,1},{1,2},{2,3},{4,5},{5,6},{6,7},{8,9},{9,10},{10,11},{12,13},{... | collective-permute-start | bytes 3956744 | tf_op jit(solution)/shard_map/ppermute | solution.py:642
  20.4 27.1 %collective-permute-start.3 = (f32[161,2,8,128]{3,2,1,0:T(8,128)S(1)}, f32[161,2,8,128]{3,2,1,0:T(8,128)S(1)}, u32[]{:S(2)}, u32[]{:S(2)}) collective-permute-start(f32[161,2,8,128]{3,2,1,0:T(8,128)S(1)} %get-tuple-element.45), channel_id=1, source_target_pairs={{1,0},{2,1},{3,2},{5,4},{6,5},{7,6},{9,8},{10,9},{11,10},{13,12},{... | collective-permute-start | bytes 3956744 | tf_op jit(solution)/shard_map/ppermute | solution.py:643
  50.0 20.5 %collective-permute-start.4 = (f32[17,24,128]{2,1,0:T(8,128)S(1)}, f32[17,24,128]{2,1,0:T(8,128)S(1)}, u32[]{:S(2)}, u32[]{:S(2)}) collective-permute-start(f32[17,24,128]{2,1,0:T(8,128)S(1)} %get-tuple-element.59), channel_id=1, source_target_pairs={{0,4},{4,8},{8,12},{12,16},{16,20},{20,24},{24,28},{28,32},{32,36}... | collective-permute-start | bytes 626696 | tf_op jit(solution)/shard_map/ppermute | solution.py:662
  51.4 19.2 %collective-permute-start.5 = (f32[17,24,128]{2,1,0:T(8,128)S(1)}, f32[17,24,128]{2,1,0:T(8,128)S(1)}, u32[]{:S(2)}, u32[]{:S(2)}) collective-permute-start(f32[17,24,128]{2,1,0:T(8,128)S(1)} %get-tuple-element.60), channel_id=1, source_target_pairs={{4,0},{8,4},{12,8},{16,12},{20,16},{24,20},{28,24},{32,28},{36,32}... | collective-permute-start | bytes 626696 | tf_op jit(solution)/shard_map/ppermute | solution.py:663

commit v5 on v4

--- a/solution.py
+++ b/solution.py
@@ -13,6 +13,7 @@
 NT = 16
 PER = 8
 F32 = jnp.float32
+BF16 = jnp.bfloat16
 ANY = pl.BlockSpec(memory_space=pl.ANY)
 SMEM = pl.BlockSpec(memory_space=pltpu.SMEM)
 VMEM = pl.BlockSpec(memory_space=pltpu.VMEM)
@@ -92,16 +93,26 @@
     return result
 
 
-def react(table, s, m):
-    outs = []
-    for a in range(PER):
-        acc = None
-        for b in range(PER):
-            w = table[s * 64 + a * 8 + b]
-            term = [w * x for x in m[b]]
-            acc = term if acc is None else [p + q for p, q in zip(acc, term)]
-        outs.append(acc)
-    return outs
+def react(weights, m):
+    x = jnp.concatenate([jnp.concatenate([m[t][j] for t in range(PER)], axis=0) for j in range(2)], axis=1)
+    high = x.astype(BF16)
+    rest = (x - high.astype(F32)).astype(BF16)
+    parts = jnp.concatenate([high, rest, high], axis=0)
+    out = jnp.dot(weights[:, :192], parts, preferred_element_type=F32)
+    return [[out[8 * t:8 * t + 8, 128 * j:128 * j + 128] for j in range(2)] for t in range(PER)]
+
+
+def sweep(down, upward, unroll=8):
+    def step(i, carry):
+        before, m = carry
+        if down is not None:
+            before = down(i, before)
+        if upward is not None:
+            m = upward(LV - 1 - i, m)
+        return before, m
+
+    start = [zeros_like_tiles(8, 2) for _ in range(PER)]
+    lax.fori_loop(0, LV, step, (start if down is not None else 0, start if upward is not None else 0), unroll=unroll)
 
 
 def zeros_like_tiles(rows, count):
@@ -137,11 +148,20 @@
     low = sub_iota() < 4
     place = lane_iota() & 31
     slot = lane_iota() >> 5
+    same = (lane_iota() & 7) == sub_iota()
+    column = (lane_iota() >> 3) & 7
     for s in range(2):
+        blocks = []
         for a in range(PER):
+            v = jnp.zeros((8, 128), F32)
             for b in range(PER):
-                v = DT * reaction[s, a, b] + (1.0 if a == b else 0.0)
-                table[s * 64 + a * 8 + b] = jnp.full((8, 128), v, F32)
+                w = DT * reaction[s, a, b] + (1.0 if a == b else 0.0)
+                v = jnp.where(same & (column == b), jnp.full((8, 128), w, F32), v)
+            blocks.append(v)
+        v = jnp.concatenate(blocks, axis=0)
+        high = v.astype(BF16)
+        table[s, :, 0:128] = high
+        table[s, :, 128:256] = (v - high.astype(F32)).astype(BF16)
     for s in range(2):
         for go in range(2):
             for gi in range(2):
@@ -236,7 +256,7 @@
 
 
 def inner_kernel(rows_total, scal, c_first, h_first, u_first, v_first, d_buf, p_buf, table, saved, saved_f, mid, mid_f,
-                 h_buf, u_buf, v_buf, c_one, c_two, solved, coef):
+                 h_buf, u_buf, v_buf, one_a, one_b, two_a, two_b, solved_a, solved_b, coef, ratio):
     rows = lax.broadcasted_iota(jnp.int32, (16, 128), 0) + scal[1]
     cor_c = coriolis_of(rows, rows_total)
     cor_s = coriolis_of(rows - 1, rows_total)
@@ -244,7 +264,10 @@
     d_e = [jnp.minimum(a, b) for a, b in zip(d_c, from_east(d_c))]
     d_n = [jnp.minimum(d_c[j], p_buf[j, 9:25, :]) for j in range(2)]
     d_s = [jnp.minimum(d_c[j], p_buf[j, 7:23, :]) for j in range(2)]
-    buffers = (c_first, c_one, c_two, c_one, None)
+    c_one, c_two = (one_a, one_b), (two_a, two_b)
+    buffers = ((c_first.at[pl.ds(0, PER)], c_first.at[pl.ds(PER, PER)]), c_one, c_two, c_one, None)
+    solved = (solved_a, solved_b)
+    pending, keep, slot = None, None, 0
     for n in range(1, ITERS + 1):
         src, dst = buffers[n - 1], buffers[n]
         old = (h_first, u_first, v_first) if n == 1 else (h_buf, u_buf, v_buf)
@@ -259,8 +282,9 @@
                 h_buf[k, j, 8:24, :] = h_new[j]
                 u_buf[k, j, 8:24, :] = u_new[j]
                 v_buf[k, j, 8:24, :] = v_new[j]
-                for c in range(7):
+                for c in range(6):
                     coef[c, k, j] = co[j][c]
+                ratio[n % 2, k, j] = co[j][6]
             return links, ratios
 
         lax.fori_loop(0, LV, dynamics, (zeros_like_tiles(16, 2), zeros_like_tiles(16, 2)), unroll=4)
@@ -274,40 +298,44 @@
                     else:
                         mid_f[f, k, j] = buf[k, j, 12:20, :]
 
-        for r0 in ((8, 16) if n < ITERS else (12,)):
-            @pl.loop(0, 2)
-            def _(s):
-                def down(k, before):
+        for s in range(2):
+            for r0 in ((8, 16) if n < ITERS else (12,)):
+                def down(k, before, s=s, r0=r0, src=src, slot=slot):
                     co = [[coef[c, k, j, r0 - 8:r0, :] for j in range(2)] for c in range(6)]
-                    read = lambda t, r: [src[s * PER + t, k, j, r:r + 8, :] for j in range(2)]
+                    read = lambda t, r: [src[s][t, k, j, r:r + 8, :] for j in range(2)]
                     now = forward(co, [(read(t, r0), read(t, r0 - 1), read(t, r0 + 1)) for t in range(PER)], before)
                     for t in range(PER):
                         for j in range(2):
-                            solved[k, t, j] = now[t][j]
+                            solved[slot][k, t, j] = now[t][j]
                     return now
 
-                lax.fori_loop(0, LV, down, [zeros_like_tiles(8, 2) for _ in range(PER)], unroll=8)
-
-                def upward(i, m):
-                    k = LV - 1 - i
-                    r = [coef[6, k, j, r0 - 8:r0, :] for j in range(2)]
-                    m = [[solved[k, t, j] + r[j] * m[t][j] for j in range(2)] for t in range(PER)]
-                    outs = react(table, s, m)
+                def upward(k, m, s=s, r0=r0, dst=dst, slot=slot, n=n):
+                    r = [ratio[n % 2, k, j, r0 - 8:r0, :] for j in range(2)]
+                    m = [[solved[slot][k, t, j] + r[j] * m[t][j] for j in range(2)] for t in range(PER)]
+                    outs = react(table[s], m)
                     for t in range(PER):
                         for j in range(2):
                             if n < ITERS:
-                                dst[s * PER + t, k, j, r0:r0 + 8, :] = outs[t][j]
+                                dst[s][t, k, j, r0:r0 + 8, :] = outs[t][j]
                             else:
                                 mid[s * PER + t, k, j] = outs[t][j]
                     return m
 
-                lax.fori_loop(0, LV, upward, [zeros_like_tiles(8, 2) for _ in range(PER)], unroll=4)
-        if n < ITERS:
+                sweep(down, pending)
+                pending = upward
+                slot = 1 - slot
+                if keep is not None:
+                    keep()
+                    keep = None
+
+        def keep(n=n, dst=dst):
             @pl.loop(0, LV)
             def _(k):
                 for t in range(NT):
                     for j in range(2):
-                        saved[n - 1, t, k, j] = keep_rows(n, lambda r: dst[t, k, j, r:r + 8, :])
+                        saved[n - 1, t, k, j] = keep_rows(n, lambda r: dst[t // PER][t % PER, k, j, r:r + 8, :])
+
+    sweep(None, pending)
 
 
 def halo_pack_kernel(y_s, y_n, own_f, r_own, l_own, halo, x_r, x_l):
@@ -354,10 +382,14 @@
 
 
 def edge_kernel(rows_total, scal, kept, saved, saved_f, h_first, u_first, v_first, y_s, y_n, d_first, p_first, table,
-                out_c, out_f, c_buf, f_buf, d_buf, p_buf, solved, coef, sem):
-    tracer = [None] + [pltpu.make_async_copy(saved.at[n - 1], c_buf.at[n, :, :, :, pl.ds(0, 8), :], sem.at[n]) for n in range(1, ITERS)]
-    fields = [None] + [pltpu.make_async_copy(saved_f.at[n - 1], f_buf.at[n, :, :, :, pl.ds(0, 8), :], sem.at[3 + n]) for n in range(1, ITERS)]
-    for c in fields[1:] + tracer[1:]:
+                out_c, out_f, *scratch):
+    c_buf = [scratch[2 * n:2 * n + 2] for n in range(ITERS)]
+    f_buf, d_buf, p_buf, solved_a, solved_b, coef, ratio, sem = scratch[2 * ITERS:]
+    solved = (solved_a, solved_b)
+    tracer = [[pltpu.make_async_copy(saved.at[n - 1, pl.ds(PER * s, PER)], c_buf[n][s].at[:, :, :, pl.ds(0, 8), :], sem.at[2 * n + s])
+               for s in range(2)] for n in range(1, ITERS)]
+    fields = [None] + [pltpu.make_async_copy(saved_f.at[n - 1], f_buf.at[n, :, :, :, pl.ds(0, 8), :], sem.at[2 * ITERS + n]) for n in range(1, ITERS)]
+    for c in fields[1:] + tracer[0] + tracer[1] + tracer[2]:
         c.start()
     sub = sub_iota()
     low = sub < 4
@@ -375,7 +407,7 @@
             for t in range(PER):
                 ys, yn = y_s[t * LV + k, j], y_n[t * LV + k, j]
                 for half in range(2):
-                    put(c_buf.at[0, t + PER * half, k, j], kept[t + PER * half, k, j], ys, yn, half)
+                    put(c_buf[0][half].at[t, k, j], kept[t + PER * half, k, j], ys, yn, half)
             for f, (buf, index, half) in enumerate(((h_first, 128, 0), (u_first, 128, 1), (v_first, 144, 0))):
                 inside = keep_rows(0, lambda r: buf[k, j, r:r + 8, :])
                 put(f_buf.at[0, f, k, j], inside, y_s[index + k, j], y_n[index + k, j], half)
@@ -393,10 +425,12 @@
     def gather(read, shift):
         return jnp.where(low, read(shift), read(shift + 2))
 
+    pending, slot = None, 0
     for n in range(1, ITERS + 1):
         if n < ITERS:
             fields[n].wait()
-            tracer[n].wait()
+            for c in tracer[n - 1]:
+                c.wait()
 
         def at(buf, j, shift):
             return jnp.where(low, buf[j, 4 + n + shift:12 + n + shift, :], buf[j, 20 - n + shift:28 - n + shift, :])
@@ -423,43 +457,44 @@
                         pltpu.store(f_buf.at[n, f, k, j, pl.ds(4, 8), :], x, mask=jnp.logical_not(low))
                     else:
                         out_f[f, k, j] = x
-                for c in range(7):
+                for c in range(6):
                     coef[c, k, j] = co[j][c]
+                ratio[n % 2, k, j] = co[j][6]
             return links, ratios
 
         lax.fori_loop(0, LV, dynamics, (zeros_like_tiles(8, 2), zeros_like_tiles(8, 2)), unroll=8)
 
-        @pl.loop(0, 2)
-        def _(s):
-            def down(k, before):
+        for s in range(2):
+            def down(k, before, s=s, n=n, slot=slot):
                 co = [[coef[c, k, j] for j in range(2)] for c in range(6)]
 
                 def read(t, shift):
-                    return [gather(lambda r: c_buf[n - 1, s * PER + t, k, j, r:r + 8, :], shift) for j in range(2)]
+                    return [gather(lambda r: c_buf[n - 1][s][t, k, j, r:r + 8, :], shift) for j in range(2)]
 
                 now = forward(co, [(read(t, 1), read(t, 0), read(t, 2)) for t in range(PER)], before)
                 for t in range(PER):
                     for j in range(2):
-                        solved[k, t, j] = now[t][j]
+                        solved[slot][k, t, j] = now[t][j]
                 return now
 
-            lax.fori_loop(0, LV, down, [zeros_like_tiles(8, 2) for _ in range(PER)], unroll=8)
-
-            def upward(i, m):
-                k = LV - 1 - i
-                r = [coef[6, k, j] for j in range(2)]
-                m = [[solved[k, t, j] + r[j] * m[t][j] for j in range(2)] for t in range(PER)]
-                outs = react(table, s, m)
+            def upward(k, m, s=s, n=n, slot=slot):
+                r = [ratio[n % 2, k, j] for j in range(2)]
+                m = [[solved[slot][k, t, j] + r[j] * m[t][j] for j in range(2)] for t in range(PER)]
+                outs = react(table[s], m)
                 for t in range(PER):
                     for j in range(2):
                         if n < ITERS:
-                            pltpu.store(c_buf.at[n, s * PER + t, k, j, pl.ds(0, 8), :], outs[t][j], mask=low)
-                            pltpu.store(c_buf.at[n, s * PER + t, k, j, pl.ds(4, 8), :], outs[t][j], mask=jnp.logical_not(low))
+                            pltpu.store(c_buf[n][s].at[t, k, j, pl.ds(0, 8), :], outs[t][j], mask=low)
+                            pltpu.store(c_buf[n][s].at[t, k, j, pl.ds(4, 8), :], outs[t][j], mask=high)
                         else:
                             out_c[s * PER + t, k, j] = outs[t][j]
                 return m
 
-            lax.fori_loop(0, LV, upward, [zeros_like_tiles(8, 2) for _ in range(PER)], unroll=4)
+            sweep(down, pending)
+            pending = upward
+            slot = 1 - slot
+
+    sweep(None, pending)
 
 
 def strip_kernel(rows_total, scal, own, own_f, halo, x_w, x_e, table, mid, mid_f, edge, edge_f, out, out_h, out_v,
@@ -622,7 +657,7 @@
     up_part, dn_part, own, r_own, l_own, c_first, kept, table, s_table = pl.pallas_call(
         tracer_pack_kernel,
         out_shape=[y_shape, y_shape, sds(LV, 4, 16, 128), sds(LV, 16, 128), sds(LV, 16, 128), sds(NT, LV, 2, 32, 128),
-                   sds(NT, LV, 2, 8, 128), sds(128, 8, 128), sds(32, 8, 128)],
+                   sds(NT, LV, 2, 8, 128), jax.ShapeDtypeStruct((2, 64, 256), BF16), sds(32, 8, 128)],
         in_specs=[ANY, SMEM], out_specs=[VMEM] * 9,
         scratch_shapes=[pltpu.SemaphoreType.DMA((4,))],
         compiler_params=room(4), name="tracer_pack")(tracers, reaction)
@@ -646,11 +681,12 @@
         out_shape=[sds(ITERS - 1, NT, LV, 2, 8, 128), sds(ITERS - 1, 3, LV, 2, 8, 128), sds(NT, LV, 2, 8, 128), sds(3, LV, 2, 8, 128)],
         in_specs=[SMEM] + [VMEM] * 7, out_specs=[VMEM] * 4,
         scratch_shapes=[pltpu.VMEM((LV, 2, 32, 128), F32)] * 3 + [
-            pltpu.VMEM((NT, LV, 2, 32, 128), F32),
-            pltpu.VMEM((NT, LV, 2, 32, 128), F32),
+            pltpu.VMEM((PER, LV, 2, 32, 128), F32)] * 4 + [
             pltpu.VMEM((LV, PER, 2, 8, 128), F32),
-            pltpu.VMEM((7, LV, 2, 16, 128), F32)],
-        compiler_params=room(24), name="inner")(scal, c_first, h_first, u_first, v_first, d_first, p_first, table)
+            pltpu.VMEM((LV, PER, 2, 8, 128), F32),
+            pltpu.VMEM((6, LV, 2, 16, 128), F32),
+            pltpu.VMEM((2, LV, 2, 16, 128), F32)],
+        compiler_params=room(26), name="inner")(scal, c_first, h_first, u_first, v_first, d_first, p_first, table)
     y_s, y_n, mid_f = lax.optimization_barrier((y_s, y_n, mid_f))
     halo, x_r, x_l = pl.pallas_call(
         halo_pack_kernel, out_shape=[sds(LV + 1, 5, 8, 128), sds(LV + 1, 24, 128), sds(LV + 1, 24, 128)],
@@ -665,15 +701,16 @@
         lambda *a: edge_kernel(rows_total, *a),
         out_shape=[sds(NT, LV, 2, 8, 128), sds(3, LV, 2, 8, 128)],
         in_specs=[SMEM] + [VMEM] * 11, out_specs=[VMEM] * 2,
-        scratch_shapes=[
-            pltpu.VMEM((ITERS, NT, LV, 2, 16, 128), F32),
+        scratch_shapes=[pltpu.VMEM((PER, LV, 2, 16, 128), F32)] * (2 * ITERS) + [
             pltpu.VMEM((ITERS, 3, LV, 2, 16, 128), F32),
             pltpu.VMEM((LV, 2, 32, 128), F32),
             pltpu.VMEM((2, 32, 128), jnp.int32),
             pltpu.VMEM((LV, PER, 2, 8, 128), F32),
-            pltpu.VMEM((7, LV, 2, 8, 128), F32),
-            pltpu.SemaphoreType.DMA((2 * ITERS,))],
-        compiler_params=room(24), name="edge")(
+            pltpu.VMEM((LV, PER, 2, 8, 128), F32),
+            pltpu.VMEM((6, LV, 2, 8, 128), F32),
+            pltpu.VMEM((2, LV, 2, 8, 128), F32),
+            pltpu.SemaphoreType.DMA((3 * ITERS,))],
+        compiler_params=room(25), name="edge")(
             scal, kept, saved, saved_f, h_first, u_first, v_first, y_s, y_n, d_first, p_first, table)
     return pl.pallas_call(
         lambda *a: strip_kernel(rows_total, *a),

time: 85.7 us -> 75.1 us (0.88)
  Pallas kernels: 64.5 us -> 52.8 us
  waiting for transfers between devices: 0.83 us -> 2.05 us
    pallas_call x1, Pallas kernels: 25.2 us -> 17.4 us  [body(): pl.pallas_call(lambda *a: inner_kernel(rows_total, *a), out_shape=[sds(IT...]
    pallas_call x1, Pallas kernels: 15.4 us -> 11.5 us  [body(): pl.pallas_call(lambda *a: edge_kernel(rows_total, *a), out_shape=[sds(NT,...]
    ppermute x1, waiting for transfers between devices: 0.01 us -> 1.22 us  [body(): y_n = lax.ppermute(y_dn, 'ty', south)]
  transfers between devices with their start and end apart: 6 -> 6, of which waited for: 1 -> 2; matrix products, arithmetic and copies ran while one was open for 0% -> 0% of each run, Pallas kernels for 54% -> 45%
where the time goes in v5:
time: 75.1 us; the launch traced here: 74.9 us
  Pallas kernels  52.8 us (70%)
  starting transfers between devices  16.2 us (22%)
  local copies, waits for them, and re-layouts  2.9 us (4%)
  waiting for transfers between devices  2.05 us (3%)
  between operations  0.91 us (1%)
    pallas_call x1, Pallas kernels, body(): pl.pallas_call(lambda *a: inner_kernel(rows_total, *a), out_shape=[sds(IT...  17.4 us
    pallas_call x1, Pallas kernels, body(): pl.pallas_call(lambda *a: strip_kernel(rows_total, *a), out_shape=[sds(*t...  14.7 us
    pallas_call x1, Pallas kernels, body(): pl.pallas_call(lambda *a: edge_kernel(rows_total, *a), out_shape=[sds(NT,...  11.5 us
    ppermute x1, starting transfers between devices, body(): y_s = lax.ppermute(y_up, 'ty', north)  6.46 us
    pallas_call x1, Pallas kernels, body(): pl.pallas_call(tracer_pack_kernel, out_shape=[y_shape, y_shape, sds(LV, 4...  5.12 us
    ppermute x1, starting transfers between devices, body(): x_e = lax.ppermute(x_l, 'tx', west)  3.84 us
    unnamed x14, local copies, waits for them, and re-layouts  2.9 us
    ppermute x1, starting transfers between devices, body(): v_pair = lax.ppermute(velocity, 'set', swap)  2.55 us
  transfers between devices with their start and end apart: 6, of which 2 were waited for; matrix products, arithmetic and copies ran while one was open for 0% of the time, Pallas kernels for 45%

profile of v5, /device:TPU:1, one launch (start us, length us, event | category | flops | bytes accessed | tf_op | source)
XLA Modules:
  0.0 74.9 jit_solution(10736317064421070218)
XLA Ops:
  0.6 2.5 %collective-permute-start.1 = (f32[2,8,16,256]{3,2,1,0:T(8,128)}, f32[2,8,16,256]{3,2,1,0:T(8,128)S(1)}, u32[]{:S(2)}, u32[]{:S(2)}) collective-permute-start(f32[2,8,16,256]{3,2,1,0:T(8,128)} %vo.1), channel_id=1, source_target_pairs={{0,64},{64,0},{1,65},{65,1},{2,66},{66,2},{3,67},{67,3},{4,68},{68... | collective-permute-start | bytes 786440 | tf_op jit(solution)/shard_map/ppermute | solution.py:654
  3.2 0.1 collective-permute-start
  3.3 0.0 copy-start
  3.3 2.2 %copy-done = f32[16,16,16,256]{3,2,1,0:T(8,128)S(1)} copy-done((f32[16,16,16,256]{3,2,1,0:T(8,128)S(1)}, f32[16,16,16,256]{3,2,1,0:T(8,128)}, u32[]{:S(2)}) %copy-start) | copy-done | bytes 4194328
  5.5 0.0 copy-start.6
  5.5 0.7 copy-done.6
  6.2 0.0 copy-start.1
  6.2 0.0 copy-start.2
  6.2 0.0 copy-start.3
  6.2 0.0 copy-start.4
  6.2 0.0 copy-start.5
  6.2 5.1 %tracer_pack.1 = (f32[161,2,8,128]{3,2,1,0:T(8,128)S(1)}, f32[161,2,8,128]{3,2,1,0:T(8,128)S(1)}, f32[16,4,16,128]{3,2,1,0:T(8,128)S(1)}, f32[16,16,128]{2,1,0:T...) custom-call(f32[16,16,16,256]{3,2,1,0:T(8,128)S(1)} %copy-done, ...), custom_call_target="tpu_custom_call" | custom-call | tf_op jit(solution)/shard_map/tracer_pack/pallas_call | solution.py:657
  11.3 0.1 pad_add_fusion.scal.a_0_
  11.4 0.8 %collective-permute-done.hp = f32[8,16,256]{2,1,0:T(8,128)S(1)} collective-permute-done((f32[8,16,256]{2,1,0:T(8,128)}, f32[8,16,256]{2,1,0:T(8,128)S(1)}, u32[]{:S(2)}, u32[]{:S(2)}) %collective-permute-start) | collective-permute-done | bytes 131104 | tf_op jit(solution)/shard_map/ppermute | solution.py:653
  12.2 0.0 collective-permute-done.1.vp
  12.2 0.0 copy-done.1
  12.2 0.0 copy-done.2
  12.2 0.0 copy-done.3
  12.2 0.0 copy-done.4
  12.2 0.0 copy-done.5
  12.2 1.6 %field_pack.1 = (f32[161,2,8,128]{3,2,1,0:T(8,128)S(1)}, f32[161,2,8,128]{3,2,1,0:T(8,128)S(1)}, f32[17,16,128]{2,1,0:T(8,128)S(1)}, f32[16,2,32,128]{3,2,1,0:T(...) custom-call(s32[2]{0:T(128)S(1)} %pad_add_fusion.scal.a_0_, ...), custom_call_target="tpu_custom_call", output_to_operand_aliasing={{0}: (8, {}), {1}: (9, {})} | custom-call | tf_op jit(solution)/shard_map/field_pack/pallas_call | solution.py:665
  13.9 6.5 %collective-permute-start.2 = (f32[161,2,8,128]{3,2,1,0:T(8,128)S(1)}, f32[161,2,8,128]{3,2,1,0:T(8,128)S(1)}, u32[]{:S(2)}, u32[]{:S(2)}) collective-permute-start(f32[161,2,8,128]{3,2,1,0:T(8,128)S(1)} %get-tuple-element.44), channel_id=1, source_target_pairs={{0,1},{1,2},{2,3},{4,5},{5,6},{6,7},{8,9},{9,10},{10,11},{12,13},{... | collective-permute-start | bytes 3956744 | tf_op jit(solution)/shard_map/ppermute | solution.py:677
  20.4 1.9 %collective-permute-start.3 = (f32[161,2,8,128]{3,2,1,0:T(8,128)S(1)}, f32[161,2,8,128]{3,2,1,0:T(8,128)S(1)}, u32[]{:S(2)}, u32[]{:S(2)}) collective-permute-start(f32[161,2,8,128]{3,2,1,0:T(8,128)S(1)} %get-tuple-element.45), channel_id=1, source_target_pairs={{1,0},{2,1},{3,2},{5,4},{6,5},{7,6},{9,8},{10,9},{11,10},{13,12},{... | collective-permute-start | bytes 3956744 | tf_op jit(solution)/shard_map/ppermute | solution.py:678
  22.3 17.4 %inner.1 = (f32[3,16,16,2,8,128]{5,4,3,2,1,0:T(8,128)S(1)}, f32[3,3,16,2,8,128]{5,4,3,2,1,0:T(8,128)S(1)}, f32[16,16,2,8,128]{4,3,2,1,0:T(8,128)S(1)}, f32[3,16,2,8,128]{4,3,2,1,0:T(8,128)S(1)}) custom-call(s32[2]{0:T(128)S(1)} %pad_add_fusion.scal.a_0_, f32[16,16,2,32,128]{4,3,2,1,0:T(8,128)S(1)} %get-tuple-element.46.a_1_, ...), custom_call_target="tpu_custom_call" | custom-call | tf_op jit(solution)/shard_map/inner/pallas_call | solution.py:679
  39.7 0.0 collective-permute-done.2.y_s.a_7_
  39.7 1.2 %collective-permute-done.3.y_n.a_8_ = f32[161,2,8,128]{3,2,1,0:T(8,128)S(1)} collective-permute-done((f32[161,2,8,128]{3,2,1,0:T(8,128)S(1)}, f32[161,2,8,128]{3,2,1,0:T(8,128)S(1)}, u32[]{:S(2)}, u32[]{:S(2)}) %collective-permute-start.3) | collective-permute-done | bytes 1318944 | tf_op jit(solution)/shard_map/ppermute | solution.py:678
  40.9 2.5 %halo_pack.1 = (f32[17,5,8,128]{3,2,1,0:T(8,128)S(1)}, f32[17,24,128]{2,1,0:T(8,128)S(1)}, f32[17,24,128]{2,1,0:T(8,128)S(1)}) custom-call(f32[161,2,8,128]{3,2,1,0:T(8,128)S(1)} %collective-permute-done.2.y_s.a_7_, f32[161,2,8,128]{3,2,1,0:T(8,128)S(1)} %collective-permute-done.3.y_n.a_8_, f32[17,16,128]{2,1,0:T(8,128)S(1)} %get-tuple-element.43.own_f.a_2_, ...), custom_call_target="tpu_custom_call" | custom-call | tf_op jit(solution)/shard_map/halo_pack/pallas_call | solution.py:691
  43.4 1.3 %collective-permute-start.4 = (f32[17,24,128]{2,1,0:T(8,128)S(1)}, f32[17,24,128]{2,1,0:T(8,128)S(1)}, u32[]{:S(2)}, u32[]{:S(2)}) collective-permute-start(f32[17,24,128]{2,1,0:T(8,128)S(1)} %get-tuple-element.59), channel_id=1, source_target_pairs={{0,4},{4,8},{8,12},{12,16},{16,20},{20,24},{24,28},{28,32},{32,36}... | collective-permute-start | bytes 626696 | tf_op jit(solution)/shard_map/ppermute | solution.py:698
  44.7 3.8 %collective-permute-start.5 = (f32[17,24,128]{2,1,0:T(8,128)S(1)}, f32[17,24,128]{2,1,0:T(8,128)S(1)}, u32[]{:S(2)}, u32[]{:S(2)}) collective-permute-start(f32[17,24,128]{2,1,0:T(8,128)S(1)} %get-tuple-element.60), channel_id=1, source_target_pairs={{4,0},{8,4},{12,8},{16,12},{20,16},{24,20},{28,24},{32,28},{36,32}... | collective-permute-start | bytes 626696 | tf_op jit(solution)/shard_map/ppermute | solution.py:699
  48.5 11.5 %edge.1 = (f32[16,16,2,8,128]{4,3,2,1,0:T(8,128)S(1)}, f32[3,16,2,8,128]{4,3,2,1,0:T(8,128)S(1)}) custom-call(s32[2]{0:T(128)S(1)} %pad_add_fusion.scal.a_0_, f32[16,16,2,8,128]{4,3,2,1,0:T(8,128)S(1)} %get-tuple-element.64.a_1_, f32[3,16,16,2,8,128]{5,4,3,2,1,0:T(8,128)S(1)} %get-tuple-element.65.a_2_, ...), custom_call_target="tpu_custom_call" | custom-call | tf_op jit(solution)/shard_map/edge/pallas_call | solution.py:700
  60.0 0.0 collective-permute-done.4.a_4_
  60.0 0.0 collective-permute-done.5.a_5_
  60.1 14.7 %strips.1 = (f32[16,16,16,256]{3,2,1,0:T(8,128)}, f32[8,16,256]{2,1,0:T(8,128)}, f32[2,8,16,256]{3,2,1,0:T(8,128)}) custom-call(s32[2]{0:T(128)S(1)} %pad_add_fusion.scal.a_0_, f32[16,4,16,128]{3,2,1,0:T(8,128)S(1)} %get-tuple-element.36.a_1_, f32[17,16,128]{2,1,0:T(8,128)S(1)} %get-tuple-element.43.own_f.a_2_, ...), custom_call_target="tpu_custom_call" | custom-call | tf_op jit(solution)/shard_map/strips/pallas_call | solution.py:715
Async XLA Ops:
  0.6 11.6 %collective-permute-start.1 = (f32[2,8,16,256]{3,2,1,0:T(8,128)}, f32[2,8,16,256]{3,2,1,0:T(8,128)S(1)}, u32[]{:S(2)}, u32[]{:S(2)}) collective-permute-start(f32[2,8,16,256]{3,2,1,0:T(8,128)} %vo.1), channel_id=1, source_target_pairs={{0,64},{64,0},{1,65},{65,1},{2,66},{66,2},{3,67},{67,3},{4,68},{68... | collective-permute-start | bytes 786440 | tf_op jit(solution)/shard_map/ppermute | solution.py:654
  3.2 9.0 %collective-permute-start = (f32[8,16,256]{2,1,0:T(8,128)}, f32[8,16,256]{2,1,0:T(8,128)S(1)}, u32[]{:S(2)}, u32[]{:S(2)}) collective-permute-start(f32[8,16,256]{2,1,0:T(8,128)} %ho.1), channel_id=1, source_target_pairs={{0,64},{64,0},{1,65},{65,1},{2,66},{66,2},{3,67},{67,3},{4,68},{68... | collective-permute-start | bytes 393224 | tf_op jit(solution)/shard_map/ppermute | solution.py:653
  3.3 2.2 %copy-start = (f32[16,16,16,256]{3,2,1,0:T(8,128)S(1)}, f32[16,16,16,256]{3,2,1,0:T(8,128)}, u32[]{:S(2)}) copy-start(f32[16,16,16,256]{3,2,1,0:T(8,128)} %tr.1) | copy-start | bytes 12582916
  5.5 0.7 copy-start.6
  6.2 6.1 %copy-start.1 = (f32[2,8,16,256]{3,2,1,0:T(8,128)S(1)}, f32[2,8,16,256]{3,2,1,0:T(8,128)}, u32[]{:S(2)}) copy-start(f32[2,8,16,256]{3,2,1,0:T(8,128)} %vo.1) | copy-start | bytes 786436
  6.2 6.1 %copy-start.2 = (f32[16,16,256]{2,1,0:T(8,128)S(1)}, f32[16,16,256]{2,1,0:T(8,128)}, u32[]{:S(2)}) copy-start(f32[16,16,256]{2,1,0:T(8,128)} %df.1) | copy-start | bytes 786436
  6.2 6.1 %copy-start.3 = (f32[8,16,256]{2,1,0:T(8,128)S(1)}, f32[8,16,256]{2,1,0:T(8,128)}, u32[]{:S(2)}) copy-start(f32[8,16,256]{2,1,0:T(8,128)} %ho.1) | copy-start | bytes 393220
  6.2 6.1 %copy-start.4 = (s32[16,256]{1,0:T(8,128)S(1)}, s32[16,256]{1,0:T(8,128)}, u32[]{:S(2)}) copy-start(s32[16,256]{1,0:T(8,128)} %land.1) | copy-start | bytes 49156
  6.2 6.1 %copy-start.5 = (s32[16,256]{1,0:T(8,128)S(1)}, s32[16,256]{1,0:T(8,128)}, u32[]{:S(2)}) copy-start(s32[16,256]{1,0:T(8,128)} %level.1) | copy-start | bytes 49156
  13.9 25.8 %collective-permute-start.2 = (f32[161,2,8,128]{3,2,1,0:T(8,128)S(1)}, f32[161,2,8,128]{3,2,1,0:T(8,128)S(1)}, u32[]{:S(2)}, u32[]{:S(2)}) collective-permute-start(f32[161,2,8,128]{3,2,1,0:T(8,128)S(1)} %get-tuple-element.44), channel_id=1, source_target_pairs={{0,1},{1,2},{2,3},{4,5},{5,6},{6,7},{8,9},{9,10},{10,11},{12,13},{... | collective-permute-start | bytes 3956744 | tf_op jit(solution)/shard_map/ppermute | solution.py:677
  20.4 20.5 %collective-permute-start.3 = (f32[161,2,8,128]{3,2,1,0:T(8,128)S(1)}, f32[161,2,8,128]{3,2,1,0:T(8,128)S(1)}, u32[]{:S(2)}, u32[]{:S(2)}) collective-permute-start(f32[161,2,8,128]{3,2,1,0:T(8,128)S(1)} %get-tuple-element.45), channel_id=1, source_target_pairs={{1,0},{2,1},{3,2},{5,4},{6,5},{7,6},{9,8},{10,9},{11,10},{13,12},{... | collective-permute-start | bytes 3956744 | tf_op jit(solution)/shard_map/ppermute | solution.py:678
  43.4 16.6 %collective-permute-start.4 = (f32[17,24,128]{2,1,0:T(8,128)S(1)}, f32[17,24,128]{2,1,0:T(8,128)S(1)}, u32[]{:S(2)}, u32[]{:S(2)}) collective-permute-start(f32[17,24,128]{2,1,0:T(8,128)S(1)} %get-tuple-element.59), channel_id=1, source_target_pairs={{0,4},{4,8},{8,12},{12,16},{16,20},{20,24},{24,28},{28,32},{32,36}... | collective-permute-start | bytes 626696 | tf_op jit(solution)/shard_map/ppermute | solution.py:698
  44.7 15.3 %collective-permute-start.5 = (f32[17,24,128]{2,1,0:T(8,128)S(1)}, f32[17,24,128]{2,1,0:T(8,128)S(1)}, u32[]{:S(2)}, u32[]{:S(2)}) collective-permute-start(f32[17,24,128]{2,1,0:T(8,128)S(1)} %get-tuple-element.60), channel_id=1, source_target_pairs={{4,0},{8,4},{12,8},{16,12},{20,16},{24,20},{28,24},{32,28},{36,32}... | collective-permute-start | bytes 626696 | tf_op jit(solution)/shard_map/ppermute | solution.py:699

commit v6 on v5

--- a/solution.py
+++ b/solution.py
@@ -147,7 +147,6 @@
         c.start()
     low = sub_iota() < 4
     place = lane_iota() & 31
-    slot = lane_iota() >> 5
     same = (lane_iota() & 7) == sub_iota()
     column = (lane_iota() >> 3) & 7
     for s in range(2):
@@ -162,16 +161,25 @@
         high = v.astype(BF16)
         table[s, :, 0:128] = high
         table[s, :, 128:256] = (v - high.astype(F32)).astype(BF16)
+    slot = lane_iota() >> 5
     for s in range(2):
-        for go in range(2):
-            for gi in range(2):
-                for rho in range(4):
-                    v = jnp.zeros((8, 128), F32)
-                    for q in range(4):
-                        a, b = 4 * go + q, 4 * gi + (q - rho) % 4
-                        w = DT * reaction[s, a, b] + (1.0 if a == b else 0.0)
-                        v = jnp.where(slot == q, jnp.full((8, 128), w, F32), v)
-                    s_table[((s * 2 + go) * 2 + gi) * 4 + rho] = v
+        for b in range(PER):
+            spread = []
+            for go in range(2):
+                v = jnp.zeros((8, 128), F32)
+                for q in range(4):
+                    a = 4 * go + q
+                    w = DT * reaction[s, a, b] + (1.0 if a == b else 0.0)
+                    v = jnp.where(slot == q, jnp.full((8, 128), w, F32), v)
+                spread.append(v)
+            for go in range(2):
+                tiles = [jnp.where((lane_iota() & 31) == sub_iota() + 8 * r, spread[go], 0.0) for r in range(4)]
+                v = jnp.concatenate(tiles, axis=0)
+                high = v.astype(BF16)
+                lanes = slice(128 * go, 128 * go + 128)
+                s_table[s, 32 * b:32 * b + 32, lanes] = high
+                s_table[s, 256 + 32 * b:288 + 32 * b, lanes] = high
+                s_table[s, 512 + 32 * b:544 + 32 * b, lanes] = (v - high.astype(F32)).astype(BF16)
     for c in copies:
         c.wait()
 
@@ -318,7 +326,7 @@
                             if n < ITERS:
                                 dst[s][t, k, j, r0:r0 + 8, :] = outs[t][j]
                             else:
-                                mid[s * PER + t, k, j] = outs[t][j]
+                                mid[s * PER + t, k, j, 4:12, :] = outs[t][j]
                     return m
 
                 sweep(down, pending)
@@ -381,7 +389,7 @@
     x_l[LV, 16:24, :] = to_west(packed, 4)
 
 
-def edge_kernel(rows_total, scal, kept, saved, saved_f, h_first, u_first, v_first, y_s, y_n, d_first, p_first, table,
+def edge_kernel(rows_total, scal, kept, saved, saved_f, h_first, u_first, v_first, y_s, y_n, d_first, p_first, table, mid,
                 out_c, out_f, *scratch):
     c_buf = [scratch[2 * n:2 * n + 2] for n in range(ITERS)]
     f_buf, d_buf, p_buf, solved_a, solved_b, coef, ratio, sem = scratch[2 * ITERS:]
@@ -487,7 +495,9 @@
                             pltpu.store(c_buf[n][s].at[t, k, j, pl.ds(0, 8), :], outs[t][j], mask=low)
                             pltpu.store(c_buf[n][s].at[t, k, j, pl.ds(4, 8), :], outs[t][j], mask=high)
                         else:
-                            out_c[s * PER + t, k, j] = outs[t][j]
+                            inside = mid.at[s * PER + t, k, j]
+                            out_c[s * PER + t, k, j, 0:8, :] = jnp.where(low, outs[t][j], inside[0:8, :])
+                            out_c[s * PER + t, k, j, 8:16, :] = jnp.where(low, inside[8:16, :], outs[t][j])
                 return m
 
             sweep(down, pending)
@@ -497,10 +507,11 @@
     sweep(None, pending)
 
 
-def strip_kernel(rows_total, scal, own, own_f, halo, x_w, x_e, table, mid, mid_f, edge, edge_f, out, out_h, out_v,
-                 c_buf, c_alt, h_buf, u_buf, v_buf, d_buf, p_buf, solved, coef, out_c, sem):
+def strip_kernel(rows_total, scal, own, own_f, halo, x_w, x_e, table, mid_f, edge, edge_f, out, out_h, out_v,
+                 c_buf, c_alt, h_buf, u_buf, v_buf, d_buf, p_buf, solved, coef, mixed, out_c, o_h, o_v, sem):
     lane = lane_iota()
     place = lane & 31
+    slot = lane >> 5
     low = sub_iota() < 4
 
     def whole(k, g, i, xg):
@@ -528,10 +539,11 @@
             for g in range(4):
                 put(c_buf.at[g, k], i, whole(k, g, i, g))
             x = whole(k, 4, i, 4)
+            turned = [x] + [pltpu.roll(x, 32 * rho, 1) for rho in range(1, 4)]
             for f, buf in enumerate((h_buf, u_buf, v_buf, d_buf)):
-                y = jnp.where(lane < 32, pltpu.roll(x, (-32 * f) % 128, 1), 0.0)
-                y = y + pltpu.roll(y, 32, 1)
-                y = y + pltpu.roll(y, 64, 1)
+                y = turned[(3 - f) % 4]
+                for q in range(3):
+                    y = jnp.where(slot == q, turned[(q - f) % 4], y)
                 put(buf.at[k], i, y)
 
     for i in range(3):
@@ -545,92 +557,106 @@
     d_n = [jnp.minimum(d_c[0], p_buf[9:33, :])]
     d_s = [jnp.minimum(d_c[0], p_buf[7:31, :])]
 
+    def merge(body, strip, q, j):
+        if j == 0:
+            return jnp.where(lane < 4, pltpu.roll(strip, (-(32 * q + 4)) % 128, 1), body)
+        return jnp.where(lane >= 124, pltpu.roll(strip, (100 - 32 * q) % 128, 1), body)
+
+    def dynamics(k, carry, side):
+        up, prev = carry
+        read = lambda buf, r: [buf[k, r:r + 24, :]]
+        h_new, u_new, v_new, co, links, ratios = level_step(
+            k, read(h_buf, 7), read(h_buf, 8), read(h_buf, 9), read(u_buf, 7), read(u_buf, 8),
+            read(v_buf, 7), read(v_buf, 8), (d_c, d_e, d_n, d_s), cor_c, cor_s, read(d_buf, 8), up, prev)
+        h_buf[k, 8:32, :] = h_new[0]
+        u_buf[k, 8:32, :] = u_new[0]
+        v_buf[k, 8:32, :] = v_new[0]
+        for c in range(7):
+            coef[side, c, k] = co[0][c]
+        return links, ratios
+
+    fresh = (zeros_like_tiles(24, 1), zeros_like_tiles(24, 1))
+    lax.fori_loop(0, LV, lambda k, carry: dynamics(k, carry, 1), fresh, unroll=8)
+    leaving = []
     for n in range(1, ITERS + 1):
         src, dst = (c_buf, c_alt) if n % 2 else (c_alt, c_buf)
-
-        def dynamics(k, carry):
-            up, prev = carry
-            read = lambda buf, r: [buf[k, r:r + 24, :]]
-            h_new, u_new, v_new, co, links, ratios = level_step(
-                k, read(h_buf, 7), read(h_buf, 8), read(h_buf, 9), read(u_buf, 7), read(u_buf, 8),
-                read(v_buf, 7), read(v_buf, 8), (d_c, d_e, d_n, d_s), cor_c, cor_s, read(d_buf, 8), up, prev)
-            h_buf[k, 8:32, :] = h_new[0]
-            u_buf[k, 8:32, :] = u_new[0]
-            v_buf[k, 8:32, :] = v_new[0]
-            for c in range(7):
-                coef[c, k] = co[0][c]
-            return links, ratios
-
-        lax.fori_loop(0, LV, dynamics, (zeros_like_tiles(24, 1), zeros_like_tiles(24, 1)), unroll=8)
-
         starts = (8, 16, 24) if n < ITERS else (12, 20)
         tiles = len(starts)
 
-        def down(k, before):
-            co = [[coef[c, k, r0 - 8:r0, :] for r0 in starts] for c in range(6)]
+        def down(k, carry):
+            before, after = carry
+            co = [[coef[n % 2, c, k, r0 - 8:r0, :] for r0 in starts] for c in range(6)]
             read = lambda t, shift: [src[t, k, r0 + shift:r0 + shift + 8, :] for r0 in starts]
             now = forward(co, [(read(t, 0), read(t, -1), read(t, 1)) for t in range(4)], before, joined=False)
             for t in range(4):
                 for i in range(tiles):
                     solved[k, t, i] = now[t][i]
-            return now
-
-        lax.fori_loop(0, LV, down, [zeros_like_tiles(8, tiles) for _ in range(4)], unroll=4)
+            if n < ITERS:
+                after = dynamics(k, after, (n + 1) % 2)
+            return now, after
+
+        lax.fori_loop(0, LV, down, ([zeros_like_tiles(8, tiles) for _ in range(4)], fresh if n < ITERS else 0), unroll=4)
+
+        if n == ITERS - 1:
+            off = scal[0] * (LV // 2)
+
+            @pl.loop(0, LV // 2, unroll=4)
+            def _(k):
+                for f, buf in enumerate((h_buf, u_buf, v_buf)):
+                    for i in range(2):
+                        strip = buf[k + off, 12 + 8 * i:20 + 8 * i, :]
+                        for j in range(2):
+                            turned = pltpu.roll(mid_f[f, k + off, j], 4, 0)
+                            outer = edge_f[f, k + off, j]
+                            body = jnp.where(low, outer, turned) if i == 0 else jnp.where(low, turned, outer)
+                            place_at = (k, slice(8 * i, 8 * i + 8), slice(128 * j, 128 * j + 128))
+                            if f == 0:
+                                o_h[place_at] = merge(body, strip, 0, j)
+                            else:
+                                o_v[(f - 1,) + place_at] = merge(body, strip, 0, j)
+
+            leaving += [pltpu.make_async_copy(o_h, out_h, sem.at[8]), pltpu.make_async_copy(o_v, out_v, sem.at[9])]
+            for c in leaving:
+                c.start()
 
         def upward(i, m):
             k = LV - 1 - i
-            r = [coef[6, k, r0 - 8:r0, :] for r0 in starts]
+            r = [coef[n % 2, 6, k, r0 - 8:r0, :] for r0 in starts]
             m = [[solved[k, t, i] + r[i] * m[t][i] for i in range(tiles)] for t in range(4)]
-            for i, r0 in enumerate(starts):
-                turned = [[m[t][i]] + [pltpu.roll(m[t][i], 32 * rho, 1) for rho in range(1, 4)] for t in range(4)]
-                for s in range(2):
-                    for go in range(2):
-                        acc = None
-                        for gi in range(2):
-                            for rho in range(4):
-                                term = table[((s * 2 + go) * 2 + gi) * 4 + rho] * turned[2 * s + gi][rho]
-                                acc = term if acc is None else acc + term
-                        dst[2 * s + go, k, r0:r0 + 8, :] = acc
+            for t in range(4):
+                for i in range(tiles):
+                    mixed[t // 2, pl.ds(pl.multiple_of(8 * tiles * k + 8 * i, 8), 8), 128 * (t % 2):128 * (t % 2) + 128] = m[t][i]
             return m
 
         lax.fori_loop(0, LV, upward, [zeros_like_tiles(8, tiles) for _ in range(4)], unroll=4)
 
+        size = 8 * tiles * LV // 2
+        for s in range(2):
+            for half in range(2):
+                x = mixed[s, size * half:size * half + size, :]
+                high = x.astype(BF16)
+                rest = (x - high.astype(F32)).astype(BF16)
+                made = jnp.dot(jnp.concatenate([high, rest, high], axis=1), table[s], preferred_element_type=F32)
+                for k in range(LV // 2):
+                    for i, r0 in enumerate(starts):
+                        at = 8 * (tiles * k + i)
+                        for go in range(2):
+                            dst[2 * s + go, LV // 2 * half + k, r0:r0 + 8, :] = made[at:at + 8, 128 * go:128 * go + 128]
+
     final = c_buf if ITERS % 2 == 0 else c_alt
-
-    def merge(inner, outer, strip, q, j, i):
-        turned = pltpu.roll(inner, 4, 0)
-        body = jnp.where(low, outer, turned) if i == 0 else jnp.where(low, turned, outer)
-        if j == 0:
-            return jnp.where(lane < 4, pltpu.roll(strip, (-(32 * q + 4)) % 128, 1), body)
-        return jnp.where(lane >= 124, pltpu.roll(strip, (100 - 32 * q) % 128, 1), body)
-
-    leaving = []
-    for part in range(4):
-        @pl.loop(4 * part, 4 * part + 4, unroll=2)
+    for part in range(8):
+        @pl.loop(2 * part, 2 * part + 2, unroll=2)
         def _(k):
             for t in range(NT):
                 for i in range(2):
                     strip = final[t // 4, k, 12 + 8 * i:20 + 8 * i, :]
                     for j in range(2):
                         out_c[t, k, 8 * i:8 * i + 8, 128 * j:128 * j + 128] = merge(
-                            mid[t, k, j], edge[t, k, j], strip, t % 4, j, i)
-        levels = pl.ds(4 * part, 4)
+                            edge[t, k, j, 8 * i:8 * i + 8, :], strip, t % 4, j)
+        levels = pl.ds(2 * part, 2)
         leaving.append(pltpu.make_async_copy(out_c.at[:, levels], out.at[:, levels], sem.at[part]))
-        leaving[part].start()
-
-    off = scal[0] * (LV // 2)
-
-    @pl.loop(0, LV // 2, unroll=4)
-    def _(k):
-        for f, buf in enumerate((h_buf, u_buf, v_buf)):
-            for i in range(2):
-                strip = buf[k + off, 12 + 8 * i:20 + 8 * i, :]
-                for j in range(2):
-                    x = merge(mid_f[f, k + off, j], edge_f[f, k + off, j], strip, 0, j, i)
-                    if f == 0:
-                        out_h[k, 8 * i:8 * i + 8, 128 * j:128 * j + 128] = x
-                    else:
-                        out_v[f - 1, k, 8 * i:8 * i + 8, 128 * j:128 * j + 128] = x
+        leaving[-1].start()
+
     for c in leaving:
         c.wait()
 
@@ -657,7 +683,7 @@
     up_part, dn_part, own, r_own, l_own, c_first, kept, table, s_table = pl.pallas_call(
         tracer_pack_kernel,
         out_shape=[y_shape, y_shape, sds(LV, 4, 16, 128), sds(LV, 16, 128), sds(LV, 16, 128), sds(NT, LV, 2, 32, 128),
-                   sds(NT, LV, 2, 8, 128), jax.ShapeDtypeStruct((2, 64, 256), BF16), sds(32, 8, 128)],
+                   sds(NT, LV, 2, 8, 128), jax.ShapeDtypeStruct((2, 64, 256), BF16), jax.ShapeDtypeStruct((2, 768, 256), BF16)],
         in_specs=[ANY, SMEM], out_specs=[VMEM] * 9,
         scratch_shapes=[pltpu.SemaphoreType.DMA((4,))],
         compiler_params=room(4), name="tracer_pack")(tracers, reaction)
@@ -678,7 +704,7 @@
     y_n = lax.ppermute(y_dn, "ty", south)
     saved, saved_f, mid, mid_f = pl.pallas_call(
         lambda *a: inner_kernel(rows_total, *a),
-        out_shape=[sds(ITERS - 1, NT, LV, 2, 8, 128), sds(ITERS - 1, 3, LV, 2, 8, 128), sds(NT, LV, 2, 8, 128), sds(3, LV, 2, 8, 128)],
+        out_shape=[sds(ITERS - 1, NT, LV, 2, 8, 128), sds(ITERS - 1, 3, LV, 2, 8, 128), sds(NT, LV, 2, 16, 128), sds(3, LV, 2, 8, 128)],
         in_specs=[SMEM] + [VMEM] * 7, out_specs=[VMEM] * 4,
         scratch_shapes=[pltpu.VMEM((LV, 2, 32, 128), F32)] * 3 + [
             pltpu.VMEM((PER, LV, 2, 32, 128), F32)] * 4 + [
@@ -699,8 +725,8 @@
     x_e = lax.ppermute(x_l, "tx", west)
     edge, edge_f = pl.pallas_call(
         lambda *a: edge_kernel(rows_total, *a),
-        out_shape=[sds(NT, LV, 2, 8, 128), sds(3, LV, 2, 8, 128)],
-        in_specs=[SMEM] + [VMEM] * 11, out_specs=[VMEM] * 2,
+        out_shape=[sds(NT, LV, 2, 16, 128), sds(3, LV, 2, 8, 128)],
+        in_specs=[SMEM] + [VMEM] * 12, out_specs=[VMEM] * 2,
         scratch_shapes=[pltpu.VMEM((PER, LV, 2, 16, 128), F32)] * (2 * ITERS) + [
             pltpu.VMEM((ITERS, 3, LV, 2, 16, 128), F32),
             pltpu.VMEM((LV, 2, 32, 128), F32),
@@ -711,11 +737,11 @@
             pltpu.VMEM((2, LV, 2, 8, 128), F32),
             pltpu.SemaphoreType.DMA((3 * ITERS,))],
         compiler_params=room(25), name="edge")(
-            scal, kept, saved, saved_f, h_first, u_first, v_first, y_s, y_n, d_first, p_first, table)
+            scal, kept, saved, saved_f, h_first, u_first, v_first, y_s, y_n, d_first, p_first, table, mid)
     return pl.pallas_call(
         lambda *a: strip_kernel(rows_total, *a),
         out_shape=[sds(*tracers.shape), sds(*thickness.shape), sds(*velocity.shape)],
-        in_specs=[SMEM] + [VMEM] * 10, out_specs=[ANY, VMEM, VMEM],
+        in_specs=[SMEM] + [VMEM] * 9, out_specs=[ANY] * 3,
         scratch_shapes=[
             pltpu.VMEM((4, LV, 40, 128), F32),
             pltpu.VMEM((4, LV, 40, 128), F32),
@@ -725,10 +751,13 @@
             pltpu.VMEM((LV, 40, 128), F32),
             pltpu.VMEM((40, 128), jnp.int32),
             pltpu.VMEM((LV, 4, 3, 8, 128), F32),
-            pltpu.VMEM((7, LV, 24, 128), F32),
+            pltpu.VMEM((2, 7, LV, 24, 128), F32),
+            pltpu.VMEM((2, 24 * LV, 256), F32),
             pltpu.VMEM((NT, LV, 16, 256), F32),
-            pltpu.SemaphoreType.DMA((4,))],
-        compiler_params=room(14), name="strips")(scal, own, own_f, halo, x_w, x_e, s_table, mid, mid_f, edge, edge_f)
+            pltpu.VMEM(thickness.shape, F32),
+            pltpu.VMEM(velocity.shape, F32),
+            pltpu.SemaphoreType.DMA((10,))],
+        compiler_params=room(17), name="strips")(scal, own, own_f, halo, x_w, x_e, s_table, mid_f, edge, edge_f)
 
 
 def solution(mesh):

time: 75.1 us -> 71.7 us (0.955)
  Pallas kernels: 52.8 us -> 49.5 us
    pallas_call x1, Pallas kernels: 14.7 us -> 11.1 us  [body(): pl.pallas_call(lambda *a: strip_kernel(rows_total, *a), out_shape=[sds(*t...]
  transfers between devices with their start and end apart: 6 -> 6, of which waited for: 2 -> 2; matrix products, arithmetic and copies ran while one was open for 0% -> 0% of each run, Pallas kernels for 45% -> 48%
where the time goes in v6:
time: 71.7 us; the launch traced here: 71.5 us
  Pallas kernels  49.5 us (69%)
  starting transfers between devices  16.2 us (23%)
  local copies, waits for them, and re-layouts  2.9 us (4%)
  waiting for transfers between devices  1.95 us (3%)
  between operations  0.91 us (1%)
    pallas_call x1, Pallas kernels, body(): pl.pallas_call(lambda *a: inner_kernel(rows_total, *a), out_shape=[sds(IT...  17.4 us
    pallas_call x1, Pallas kernels, body(): pl.pallas_call(lambda *a: edge_kernel(rows_total, *a), out_shape=[sds(NT,...  11.7 us
    pallas_call x1, Pallas kernels, body(): pl.pallas_call(lambda *a: strip_kernel(rows_total, *a), out_shape=[sds(*t...  11.1 us
    ppermute x1, starting transfers between devices, body(): y_s = lax.ppermute(y_up, 'ty', north)  6.46 us
    pallas_call x1, Pallas kernels, body(): pl.pallas_call(tracer_pack_kernel, out_shape=[y_shape, y_shape, sds(LV, 4...  5.21 us
    ppermute x1, starting transfers between devices, body(): x_e = lax.ppermute(x_l, 'tx', west)  3.84 us
    unnamed x14, local copies, waits for them, and re-layouts  2.9 us
    ppermute x1, starting transfers between devices, body(): v_pair = lax.ppermute(velocity, 'set', swap)  2.55 us
  transfers between devices with their start and end apart: 6, of which 2 were waited for; matrix products, arithmetic and copies ran while one was open for 0% of the time, Pallas kernels for 48%

profile of v6, /device:TPU:1, one launch (start us, length us, event | category | flops | bytes accessed | tf_op | source)
XLA Modules:
  0.0 71.5 jit_solution(13486962464183302915)
XLA Ops:
  0.6 2.5 %collective-permute-start.1 = (f32[2,8,16,256]{3,2,1,0:T(8,128)}, f32[2,8,16,256]{3,2,1,0:T(8,128)S(1)}, u32[]{:S(2)}, u32[]{:S(2)}) collective-permute-start(f32[2,8,16,256]{3,2,1,0:T(8,128)} %vo.1), channel_id=1, source_target_pairs={{0,64},{64,0},{1,65},{65,1},{2,66},{66,2},{3,67},{67,3},{4,68},{68... | collective-permute-start | bytes 786440 | tf_op jit(solution)/shard_map/ppermute | solution.py:680
  3.2 0.1 collective-permute-start
  3.3 0.0 copy-start
  3.3 2.2 %copy-done = f32[16,16,16,256]{3,2,1,0:T(8,128)S(1)} copy-done((f32[16,16,16,256]{3,2,1,0:T(8,128)S(1)}, f32[16,16,16,256]{3,2,1,0:T(8,128)}, u32[]{:S(2)}) %copy-start) | copy-done | bytes 4194328
  5.5 0.0 copy-start.6
  5.5 0.7 copy-done.6
  6.2 0.0 copy-start.1
  6.2 0.0 copy-start.2
  6.2 0.0 copy-start.3
  6.2 0.0 copy-start.4
  6.2 0.0 copy-start.5
  6.2 5.2 %tracer_pack.1 = (f32[161,2,8,128]{3,2,1,0:T(8,128)S(1)}, f32[161,2,8,128]{3,2,1,0:T(8,128)S(1)}, f32[16,4,16,128]{3,2,1,0:T(8,128)S(1)}, f32[16,16,128]{2,1,0:T...) custom-call(f32[16,16,16,256]{3,2,1,0:T(8,128)S(1)} %copy-done, ...), custom_call_target="tpu_custom_call" | custom-call | tf_op jit(solution)/shard_map/tracer_pack/pallas_call | solution.py:683
  11.4 0.1 pad_add_fusion.scal.a_0_
  11.5 0.7 %collective-permute-done.hp = f32[8,16,256]{2,1,0:T(8,128)S(1)} collective-permute-done((f32[8,16,256]{2,1,0:T(8,128)}, f32[8,16,256]{2,1,0:T(8,128)S(1)}, u32[]{:S(2)}, u32[]{:S(2)}) %collective-permute-start) | collective-permute-done | bytes 131104 | tf_op jit(solution)/shard_map/ppermute | solution.py:679
  12.2 0.0 collective-permute-done.1.vp
  12.2 0.0 copy-done.1
  12.2 0.0 copy-done.2
  12.2 0.0 copy-done.3
  12.2 0.0 copy-done.4
  12.2 0.0 copy-done.5
  12.2 1.6 %field_pack.1 = (f32[161,2,8,128]{3,2,1,0:T(8,128)S(1)}, f32[161,2,8,128]{3,2,1,0:T(8,128)S(1)}, f32[17,16,128]{2,1,0:T(8,128)S(1)}, f32[16,2,32,128]{3,2,1,0:T(...) custom-call(s32[2]{0:T(128)S(1)} %pad_add_fusion.scal.a_0_, ...), custom_call_target="tpu_custom_call", output_to_operand_aliasing={{0}: (8, {}), {1}: (9, {})} | custom-call | tf_op jit(solution)/shard_map/field_pack/pallas_call | solution.py:691
  13.9 6.5 %collective-permute-start.2 = (f32[161,2,8,128]{3,2,1,0:T(8,128)S(1)}, f32[161,2,8,128]{3,2,1,0:T(8,128)S(1)}, u32[]{:S(2)}, u32[]{:S(2)}) collective-permute-start(f32[161,2,8,128]{3,2,1,0:T(8,128)S(1)} %get-tuple-element.44), channel_id=1, source_target_pairs={{0,1},{1,2},{2,3},{4,5},{5,6},{6,7},{8,9},{9,10},{10,11},{12,13},{... | collective-permute-start | bytes 3956744 | tf_op jit(solution)/shard_map/ppermute | solution.py:703
  20.4 1.9 %collective-permute-start.3 = (f32[161,2,8,128]{3,2,1,0:T(8,128)S(1)}, f32[161,2,8,128]{3,2,1,0:T(8,128)S(1)}, u32[]{:S(2)}, u32[]{:S(2)}) collective-permute-start(f32[161,2,8,128]{3,2,1,0:T(8,128)S(1)} %get-tuple-element.45), channel_id=1, source_target_pairs={{1,0},{2,1},{3,2},{5,4},{6,5},{7,6},{9,8},{10,9},{11,10},{13,12},{... | collective-permute-start | bytes 3956744 | tf_op jit(solution)/shard_map/ppermute | solution.py:704
  22.3 17.4 %inner.1 = (f32[3,16,16,2,8,128]{5,4,3,2,1,0:T(8,128)S(1)}, f32[3,3,16,2,8,128]{5,4,3,2,1,0:T(8,128)S(1)}, f32[16,16,2,16,128]{4,3,2,1,0:T(8,128)S(1)}, f32[3,16,2,8,128]{4,3,2,1,0:T(8,128)S(1)}) custom-call(s32[2]{0:T(128)S(1)} %pad_add_fusion.scal.a_0_, f32[16,16,2,32,128]{4,3,2,1,0:T(8,128)S(1)} %get-tuple-element.46.a_1_, ...), custom_call_target="tpu_custom_call" | custom-call | tf_op jit(solution)/shard_map/inner/pallas_call | solution.py:705
  39.7 0.0 collective-permute-done.2.y_s.a_7_
  39.7 1.2 %collective-permute-done.3.y_n.a_8_ = f32[161,2,8,128]{3,2,1,0:T(8,128)S(1)} collective-permute-done((f32[161,2,8,128]{3,2,1,0:T(8,128)S(1)}, f32[161,2,8,128]{3,2,1,0:T(8,128)S(1)}, u32[]{:S(2)}, u32[]{:S(2)}) %collective-permute-start.3) | collective-permute-done | bytes 1318944 | tf_op jit(solution)/shard_map/ppermute | solution.py:704
  40.9 2.5 %halo_pack.1 = (f32[17,5,8,128]{3,2,1,0:T(8,128)S(1)}, f32[17,24,128]{2,1,0:T(8,128)S(1)}, f32[17,24,128]{2,1,0:T(8,128)S(1)}) custom-call(f32[161,2,8,128]{3,2,1,0:T(8,128)S(1)} %collective-permute-done.2.y_s.a_7_, f32[161,2,8,128]{3,2,1,0:T(8,128)S(1)} %collective-permute-done.3.y_n.a_8_, f32[17,16,128]{2,1,0:T(8,128)S(1)} %get-tuple-element.43.own_f.a_2_, ...), custom_call_target="tpu_custom_call" | custom-call | tf_op jit(solution)/shard_map/halo_pack/pallas_call | solution.py:717
  43.4 1.3 %collective-permute-start.4 = (f32[17,24,128]{2,1,0:T(8,128)S(1)}, f32[17,24,128]{2,1,0:T(8,128)S(1)}, u32[]{:S(2)}, u32[]{:S(2)}) collective-permute-start(f32[17,24,128]{2,1,0:T(8,128)S(1)} %get-tuple-element.59), channel_id=1, source_target_pairs={{0,4},{4,8},{8,12},{12,16},{16,20},{20,24},{24,28},{28,32},{32,36}... | collective-permute-start | bytes 626696 | tf_op jit(solution)/shard_map/ppermute | solution.py:724
  44.7 3.8 %collective-permute-start.5 = (f32[17,24,128]{2,1,0:T(8,128)S(1)}, f32[17,24,128]{2,1,0:T(8,128)S(1)}, u32[]{:S(2)}, u32[]{:S(2)}) collective-permute-start(f32[17,24,128]{2,1,0:T(8,128)S(1)} %get-tuple-element.60), channel_id=1, source_target_pairs={{4,0},{8,4},{12,8},{16,12},{20,16},{24,20},{28,24},{32,28},{36,32}... | collective-permute-start | bytes 626696 | tf_op jit(solution)/shard_map/ppermute | solution.py:725
  48.5 11.7 %edge.1 = (f32[16,16,2,16,128]{4,3,2,1,0:T(8,128)S(1)}, f32[3,16,2,8,128]{4,3,2,1,0:T(8,128)S(1)}) custom-call(s32[2]{0:T(128)S(1)} %pad_add_fusion.scal.a_0_, f32[16,16,2,8,128]{4,3,2,1,0:T(8,128)S(1)} %get-tuple-element.63.a_1_, f32[3,16,16,2,8,128]{5,4,3,2,1,0:T(8,128)S(1)} %get-tuple-element.64.a_2_, ...), custom_call_target="tpu_custom_call" | custom-call | tf_op jit(solution)/shard_map/edge/pallas_call | solution.py:726
  60.2 0.0 collective-permute-done.4.a_4_
  60.2 0.0 collective-permute-done.5.a_5_
  60.2 11.1 %strips.1 = (f32[16,16,16,256]{3,2,1,0:T(8,128)}, f32[8,16,256]{2,1,0:T(8,128)}, f32[2,8,16,256]{3,2,1,0:T(8,128)}) custom-call(s32[2]{0:T(128)S(1)} %pad_add_fusion.scal.a_0_, f32[16,4,16,128]{3,2,1,0:T(8,128)S(1)} %get-tuple-element.36.a_1_, f32[17,16,128]{2,1,0:T(8,128)S(1)} %get-tuple-element.43.own_f.a_2_, ...), custom_call_target="tpu_custom_call" | custom-call | tf_op jit(solution)/shard_map/strips/pallas_call | solution.py:741
Async XLA Ops:
  0.6 11.6 %collective-permute-start.1 = (f32[2,8,16,256]{3,2,1,0:T(8,128)}, f32[2,8,16,256]{3,2,1,0:T(8,128)S(1)}, u32[]{:S(2)}, u32[]{:S(2)}) collective-permute-start(f32[2,8,16,256]{3,2,1,0:T(8,128)} %vo.1), channel_id=1, source_target_pairs={{0,64},{64,0},{1,65},{65,1},{2,66},{66,2},{3,67},{67,3},{4,68},{68... | collective-permute-start | bytes 786440 | tf_op jit(solution)/shard_map/ppermute | solution.py:680
  3.2 9.0 %collective-permute-start = (f32[8,16,256]{2,1,0:T(8,128)}, f32[8,16,256]{2,1,0:T(8,128)S(1)}, u32[]{:S(2)}, u32[]{:S(2)}) collective-permute-start(f32[8,16,256]{2,1,0:T(8,128)} %ho.1), channel_id=1, source_target_pairs={{0,64},{64,0},{1,65},{65,1},{2,66},{66,2},{3,67},{67,3},{4,68},{68... | collective-permute-start | bytes 393224 | tf_op jit(solution)/shard_map/ppermute | solution.py:679
  3.3 2.2 %copy-start = (f32[16,16,16,256]{3,2,1,0:T(8,128)S(1)}, f32[16,16,16,256]{3,2,1,0:T(8,128)}, u32[]{:S(2)}) copy-start(f32[16,16,16,256]{3,2,1,0:T(8,128)} %tr.1) | copy-start | bytes 12582916
  5.5 0.7 copy-start.6
  6.2 6.1 %copy-start.1 = (f32[2,8,16,256]{3,2,1,0:T(8,128)S(1)}, f32[2,8,16,256]{3,2,1,0:T(8,128)}, u32[]{:S(2)}) copy-start(f32[2,8,16,256]{3,2,1,0:T(8,128)} %vo.1) | copy-start | bytes 786436
  6.2 6.1 %copy-start.2 = (f32[16,16,256]{2,1,0:T(8,128)S(1)}, f32[16,16,256]{2,1,0:T(8,128)}, u32[]{:S(2)}) copy-start(f32[16,16,256]{2,1,0:T(8,128)} %df.1) | copy-start | bytes 786436
  6.2 6.1 %copy-start.3 = (f32[8,16,256]{2,1,0:T(8,128)S(1)}, f32[8,16,256]{2,1,0:T(8,128)}, u32[]{:S(2)}) copy-start(f32[8,16,256]{2,1,0:T(8,128)} %ho.1) | copy-start | bytes 393220
  6.2 6.1 %copy-start.4 = (s32[16,256]{1,0:T(8,128)S(1)}, s32[16,256]{1,0:T(8,128)}, u32[]{:S(2)}) copy-start(s32[16,256]{1,0:T(8,128)} %land.1) | copy-start | bytes 49156
  6.2 6.1 %copy-start.5 = (s32[16,256]{1,0:T(8,128)S(1)}, s32[16,256]{1,0:T(8,128)}, u32[]{:S(2)}) copy-start(s32[16,256]{1,0:T(8,128)} %level.1) | copy-start | bytes 49156
  13.9 25.8 %collective-permute-start.2 = (f32[161,2,8,128]{3,2,1,0:T(8,128)S(1)}, f32[161,2,8,128]{3,2,1,0:T(8,128)S(1)}, u32[]{:S(2)}, u32[]{:S(2)}) collective-permute-start(f32[161,2,8,128]{3,2,1,0:T(8,128)S(1)} %get-tuple-element.44), channel_id=1, source_target_pairs={{0,1},{1,2},{2,3},{4,5},{5,6},{6,7},{8,9},{9,10},{10,11},{12,13},{... | collective-permute-start | bytes 3956744 | tf_op jit(solution)/shard_map/ppermute | solution.py:703
  20.4 20.5 %collective-permute-start.3 = (f32[161,2,8,128]{3,2,1,0:T(8,128)S(1)}, f32[161,2,8,128]{3,2,1,0:T(8,128)S(1)}, u32[]{:S(2)}, u32[]{:S(2)}) collective-permute-start(f32[161,2,8,128]{3,2,1,0:T(8,128)S(1)} %get-tuple-element.45), channel_id=1, source_target_pairs={{1,0},{2,1},{3,2},{5,4},{6,5},{7,6},{9,8},{10,9},{11,10},{13,12},{... | collective-permute-start | bytes 3956744 | tf_op jit(solution)/shard_map/ppermute | solution.py:704
  43.4 16.8 %collective-permute-start.4 = (f32[17,24,128]{2,1,0:T(8,128)S(1)}, f32[17,24,128]{2,1,0:T(8,128)S(1)}, u32[]{:S(2)}, u32[]{:S(2)}) collective-permute-start(f32[17,24,128]{2,1,0:T(8,128)S(1)} %get-tuple-element.59), channel_id=1, source_target_pairs={{0,4},{4,8},{8,12},{12,16},{16,20},{20,24},{24,28},{28,32},{32,36}... | collective-permute-start | bytes 626696 | tf_op jit(solution)/shard_map/ppermute | solution.py:724
  44.7 15.5 %collective-permute-start.5 = (f32[17,24,128]{2,1,0:T(8,128)S(1)}, f32[17,24,128]{2,1,0:T(8,128)S(1)}, u32[]{:S(2)}, u32[]{:S(2)}) collective-permute-start(f32[17,24,128]{2,1,0:T(8,128)S(1)} %get-tuple-element.60), channel_id=1, source_target_pairs={{4,0},{8,4},{12,8},{16,12},{20,16},{24,20},{28,24},{32,28},{36,32}... | collective-permute-start | bytes 626696 | tf_op jit(solution)/shard_map/ppermute | solution.py:725

commit v7 on v6

--- a/solution.py
+++ b/solution.py
@@ -44,28 +44,26 @@
     return ROTATION * (2.0 * (row.astype(F32) + 0.5) / rows_total - 1.0)
 
 
-def level_step(k, h_s, h_c, h_n, u_s, u_c, v_s, v_c, deep, cor_c, cor_s, diff, up, prev):
-    d_c, d_e, d_n, d_s = deep
+def level_step(k, h_c, h_n, u_c, v_c, deep, cor_c, link, up, prev, south):
+    d_c, d_e, d_n = deep
     h_e = from_east(h_c)
     count = len(h_c)
-    u_new, v_new, u_flux, v_flux, s_flux = [], [], [], [], []
+    u_new, v_new, u_flux, v_flux = [], [], [], []
     for j in range(count):
         un = jnp.where(k < d_e[j], u_c[j] + DT * (cor_c * v_c[j] - G * (h_e[j] - h_c[j])), 0.0)
         vn = jnp.where(k < d_n[j], v_c[j] - DT * (cor_c * u_c[j] + G * (h_n[j] - h_c[j])), 0.0)
-        vs = jnp.where(k < d_s[j], v_s[j] - DT * (cor_s * u_s[j] + G * (h_c[j] - h_s[j])), 0.0)
         u_new.append(un)
         v_new.append(vn)
         u_flux.append(un * 0.5 * (h_c[j] + h_e[j]))
         v_flux.append(vn * 0.5 * (h_c[j] + h_n[j]))
-        s_flux.append(vs * 0.5 * (h_s[j] + h_c[j]))
     w_flux = from_west(u_flux)
-    h_new, coefs, links, ratios = [], [], [], []
+    s_flux = south(v_flux)
+    h_new, coefs, ratios = [], [], []
     for j in range(count):
         fe, fw, fn, fs = u_flux[j], w_flux[j], v_flux[j], s_flux[j]
         hn = h_c[j] - DT * ((fe - fw) + (fn - fs))
-        link = jnp.where(k + 1 < d_c[j], DT * diff[j], 0.0)
-        q = jnp.where(k < d_c[j], 1.0 / (hn + up[j] + link - up[j] * prev[j]), 0.0)
-        r = link * q
+        q = jnp.where(k < d_c[j], 1.0 / (hn + up[j] + link[j] - up[j] * prev[j]), 0.0)
+        r = link[j] * q
         dq = DT * q
         ce = dq * jnp.maximum(-fe, 0.0)
         cw = dq * jnp.maximum(fw, 0.0)
@@ -74,10 +72,9 @@
         out = (jnp.maximum(fe, 0.0) - jnp.minimum(fw, 0.0)) + (jnp.maximum(fn, 0.0) - jnp.minimum(fs, 0.0))
         ca = q * h_c[j] - dq * out
         h_new.append(hn)
-        links.append(link)
         ratios.append(r)
         coefs.append((ca, ce, cw, cn, cs, up[j] * q, r))
-    return h_new, u_new, v_new, coefs, links, ratios
+    return h_new, u_new, v_new, coefs, ratios
 
 
 def forward(coefs, cells, before, joined=True):
@@ -234,6 +231,11 @@
     for j in range(2):
         p_buf[j, 8:24, :] = jnp.where(l_buf[0, j] == 1, l_buf[1, j], 0)
 
+    @pl.loop(0, LV, unroll=4)
+    def _(k):
+        for j in range(2):
+            d_buf[k, j, 8:24, :] = jnp.where(k + 1 < p_buf[j, 8:24, :], DT * d_buf[k, j, 8:24, :], 0.0)
+
     def put(index, j, first, second):
         f_up[index, j] = jnp.where(low, first(20), second(16))
         f_dn[index, j] = jnp.where(low, first(8), second(4))
@@ -264,14 +266,12 @@
 
 
 def inner_kernel(rows_total, scal, c_first, h_first, u_first, v_first, d_buf, p_buf, table, saved, saved_f, mid, mid_f,
-                 h_buf, u_buf, v_buf, one_a, one_b, two_a, two_b, solved_a, solved_b, coef, ratio):
+                 h_buf, u_buf, v_buf, flux, one_a, one_b, two_a, two_b, solved_a, solved_b, coef, ratio):
     rows = lax.broadcasted_iota(jnp.int32, (16, 128), 0) + scal[1]
     cor_c = coriolis_of(rows, rows_total)
-    cor_s = coriolis_of(rows - 1, rows_total)
     d_c = [p_buf[j, 8:24, :] for j in range(2)]
     d_e = [jnp.minimum(a, b) for a, b in zip(d_c, from_east(d_c))]
     d_n = [jnp.minimum(d_c[j], p_buf[j, 9:25, :]) for j in range(2)]
-    d_s = [jnp.minimum(d_c[j], p_buf[j, 7:23, :]) for j in range(2)]
     c_one, c_two = (one_a, one_b), (two_a, two_b)
     buffers = ((c_first.at[pl.ds(0, PER)], c_first.at[pl.ds(PER, PER)]), c_one, c_two, c_one, None)
     solved = (solved_a, solved_b)
@@ -283,9 +283,15 @@
         def dynamics(k, carry):
             up, prev = carry
             read = lambda buf, r: [buf[k, j, r:r + 16, :] for j in range(2)]
-            h_new, u_new, v_new, co, links, ratios = level_step(
-                k, read(old[0], 7), read(old[0], 8), read(old[0], 9), read(old[1], 7), read(old[1], 8),
-                read(old[2], 7), read(old[2], 8), (d_c, d_e, d_n, d_s), cor_c, cor_s, read(d_buf, 8), up, prev)
+            link = read(d_buf, 8)
+
+            def south(fluxes):
+                for j in range(2):
+                    flux[k, j, 8:24, :] = fluxes[j]
+                return read(flux, 7)
+
+            h_new, u_new, v_new, co, ratios = level_step(
+                k, read(old[0], 8), read(old[0], 9), read(old[1], 8), read(old[2], 8), (d_c, d_e, d_n), cor_c, link, up, prev, south)
             for j in range(2):
                 h_buf[k, j, 8:24, :] = h_new[j]
                 u_buf[k, j, 8:24, :] = u_new[j]
@@ -293,11 +299,11 @@
                 for c in range(6):
                     coef[c, k, j] = co[j][c]
                 ratio[n % 2, k, j] = co[j][6]
-            return links, ratios
+            return link, ratios
 
         lax.fori_loop(0, LV, dynamics, (zeros_like_tiles(16, 2), zeros_like_tiles(16, 2)), unroll=4)
 
-        @pl.loop(0, LV)
+        @pl.loop(0, LV, unroll=4)
         def _(k):
             for f, buf in enumerate((h_buf, u_buf, v_buf)):
                 for j in range(2):
@@ -337,7 +343,7 @@
                     keep = None
 
         def keep(n=n, dst=dst):
-            @pl.loop(0, LV)
+            @pl.loop(0, LV, unroll=2)
             def _(k):
                 for t in range(NT):
                     for j in range(2):
@@ -392,13 +398,8 @@
 def edge_kernel(rows_total, scal, kept, saved, saved_f, h_first, u_first, v_first, y_s, y_n, d_first, p_first, table, mid,
                 out_c, out_f, *scratch):
     c_buf = [scratch[2 * n:2 * n + 2] for n in range(ITERS)]
-    f_buf, d_buf, p_buf, solved_a, solved_b, coef, ratio, sem = scratch[2 * ITERS:]
+    f_buf, d_buf, p_buf, solved_a, solved_b, coef, ratio = scratch[2 * ITERS:]
     solved = (solved_a, solved_b)
-    tracer = [[pltpu.make_async_copy(saved.at[n - 1, pl.ds(PER * s, PER)], c_buf[n][s].at[:, :, :, pl.ds(0, 8), :], sem.at[2 * n + s])
-               for s in range(2)] for n in range(1, ITERS)]
-    fields = [None] + [pltpu.make_async_copy(saved_f.at[n - 1], f_buf.at[n, :, :, :, pl.ds(0, 8), :], sem.at[2 * ITERS + n]) for n in range(1, ITERS)]
-    for c in fields[1:] + tracer[0] + tracer[1] + tracer[2]:
-        c.start()
     sub = sub_iota()
     low = sub < 4
     high = jnp.logical_not(low)
@@ -435,11 +436,6 @@
 
     pending, slot = None, 0
     for n in range(1, ITERS + 1):
-        if n < ITERS:
-            fields[n].wait()
-            for c in tracer[n - 1]:
-                c.wait()
-
         def at(buf, j, shift):
             return jnp.where(low, buf[j, 4 + n + shift:12 + n + shift, :], buf[j, 20 - n + shift:28 - n + shift, :])
 
@@ -454,21 +450,27 @@
         def dynamics(k, carry):
             up, prev = carry
             read = lambda f, shift: [gather(lambda r: f_buf[n - 1, f, k, j, r:r + 8, :], shift) for j in range(2)]
-            diff = [at(d_buf.at[k], j, 0) for j in range(2)]
-            h_new, u_new, v_new, co, links, ratios = level_step(
-                k, read(0, 0), read(0, 1), read(0, 2), read(1, 0), read(1, 1), read(2, 0), read(2, 1),
-                (d_c, d_e, d_n, d_s), cor_c, cor_s, diff, up, prev)
+            link = [at(d_buf.at[k], j, 0) for j in range(2)]
+            h_c = read(0, 1)
+
+            def south(_):
+                h_s, u_s, v_s = read(0, 0), read(1, 0), read(2, 0)
+                return [jnp.where(k < d_s[j], v_s[j] - DT * (cor_s * u_s[j] + G * (h_c[j] - h_s[j])), 0.0)
+                        * 0.5 * (h_s[j] + h_c[j]) for j in range(2)]
+
+            h_new, u_new, v_new, co, ratios = level_step(
+                k, h_c, read(0, 2), read(1, 1), read(2, 1), (d_c, d_e, d_n), cor_c, link, up, prev, south)
             for j in range(2):
                 for f, x in enumerate((h_new[j], u_new[j], v_new[j])):
                     if n < ITERS:
-                        pltpu.store(f_buf.at[n, f, k, j, pl.ds(0, 8), :], x, mask=low)
+                        f_buf[n, f, k, j, 0:8, :] = jnp.where(low, x, saved_f[n - 1, f, k, j])
                         pltpu.store(f_buf.at[n, f, k, j, pl.ds(4, 8), :], x, mask=jnp.logical_not(low))
                     else:
                         out_f[f, k, j] = x
                 for c in range(6):
                     coef[c, k, j] = co[j][c]
                 ratio[n % 2, k, j] = co[j][6]
-            return links, ratios
+            return link, ratios
 
         lax.fori_loop(0, LV, dynamics, (zeros_like_tiles(8, 2), zeros_like_tiles(8, 2)), unroll=8)
 
@@ -492,7 +494,7 @@
                 for t in range(PER):
                     for j in range(2):
                         if n < ITERS:
-                            pltpu.store(c_buf[n][s].at[t, k, j, pl.ds(0, 8), :], outs[t][j], mask=low)
+                            c_buf[n][s][t, k, j, 0:8, :] = jnp.where(low, outs[t][j], saved[n - 1, s * PER + t, k, j])
                             pltpu.store(c_buf[n][s].at[t, k, j, pl.ds(4, 8), :], outs[t][j], mask=high)
                         else:
                             inside = mid.at[s * PER + t, k, j]
@@ -508,7 +510,7 @@
 
 
 def strip_kernel(rows_total, scal, own, own_f, halo, x_w, x_e, table, mid_f, edge, edge_f, out, out_h, out_v,
-                 c_buf, c_alt, h_buf, u_buf, v_buf, d_buf, p_buf, solved, coef, mixed, out_c, o_h, o_v, sem):
+                 c_buf, c_alt, h_buf, u_buf, v_buf, flux, d_buf, p_buf, solved, coef, mixed, out_c, o_h, o_v, sem):
     lane = lane_iota()
     place = lane & 31
     slot = lane >> 5
@@ -551,11 +553,9 @@
 
     rows = lax.broadcasted_iota(jnp.int32, (24, 128), 0) - 4 + scal[1]
     cor_c = coriolis_of(rows, rows_total)
-    cor_s = coriolis_of(rows - 1, rows_total)
     d_c = [p_buf[8:32, :]]
     d_e = [jnp.minimum(d_c[0], from_east(d_c)[0])]
     d_n = [jnp.minimum(d_c[0], p_buf[9:33, :])]
-    d_s = [jnp.minimum(d_c[0], p_buf[7:31, :])]
 
     def merge(body, strip, q, j):
         if j == 0:
@@ -565,15 +565,20 @@
     def dynamics(k, carry, side):
         up, prev = carry
         read = lambda buf, r: [buf[k, r:r + 24, :]]
-        h_new, u_new, v_new, co, links, ratios = level_step(
-            k, read(h_buf, 7), read(h_buf, 8), read(h_buf, 9), read(u_buf, 7), read(u_buf, 8),
-            read(v_buf, 7), read(v_buf, 8), (d_c, d_e, d_n, d_s), cor_c, cor_s, read(d_buf, 8), up, prev)
+        link = read(d_buf, 8)
+
+        def south(fluxes):
+            flux[k, 8:32, :] = fluxes[0]
+            return read(flux, 7)
+
+        h_new, u_new, v_new, co, ratios = level_step(
+            k, read(h_buf, 8), read(h_buf, 9), read(u_buf, 8), read(v_buf, 8), (d_c, d_e, d_n), cor_c, link, up, prev, south)
         h_buf[k, 8:32, :] = h_new[0]
         u_buf[k, 8:32, :] = u_new[0]
         v_buf[k, 8:32, :] = v_new[0]
         for c in range(7):
             coef[side, c, k] = co[0][c]
-        return links, ratios
+        return link, ratios
 
     fresh = (zeros_like_tiles(24, 1), zeros_like_tiles(24, 1))
     lax.fori_loop(0, LV, lambda k, carry: dynamics(k, carry, 1), fresh, unroll=8)
@@ -706,7 +711,7 @@
         lambda *a: inner_kernel(rows_total, *a),
         out_shape=[sds(ITERS - 1, NT, LV, 2, 8, 128), sds(ITERS - 1, 3, LV, 2, 8, 128), sds(NT, LV, 2, 16, 128), sds(3, LV, 2, 8, 128)],
         in_specs=[SMEM] + [VMEM] * 7, out_specs=[VMEM] * 4,
-        scratch_shapes=[pltpu.VMEM((LV, 2, 32, 128), F32)] * 3 + [
+        scratch_shapes=[pltpu.VMEM((LV, 2, 32, 128), F32)] * 4 + [
             pltpu.VMEM((PER, LV, 2, 32, 128), F32)] * 4 + [
             pltpu.VMEM((LV, PER, 2, 8, 128), F32),
             pltpu.VMEM((LV, PER, 2, 8, 128), F32),
@@ -734,8 +739,7 @@
             pltpu.VMEM((LV, PER, 2, 8, 128), F32),
             pltpu.VMEM((LV, PER, 2, 8, 128), F32),
             pltpu.VMEM((6, LV, 2, 8, 128), F32),
-            pltpu.VMEM((2, LV, 2, 8, 128), F32),
-            pltpu.SemaphoreType.DMA((3 * ITERS,))],
+            pltpu.VMEM((2, LV, 2, 8, 128), F32)],
         compiler_params=room(25), name="edge")(
             scal, kept, saved, saved_f, h_first, u_first, v_first, y_s, y_n, d_first, p_first, table, mid)
     return pl.pallas_call(
@@ -749,6 +753,7 @@
             pltpu.VMEM((LV, 40, 128), F32),
             pltpu.VMEM((LV, 40, 128), F32),
             pltpu.VMEM((LV, 40, 128), F32),
+            pltpu.VMEM((LV, 40, 128), F32),
             pltpu.VMEM((40, 128), jnp.int32),
             pltpu.VMEM((LV, 4, 3, 8, 128), F32),
             pltpu.VMEM((2, 7, LV, 24, 128), F32),

time: 71.7 us -> 71.5 us (level)
  transfers between devices with their start and end apart: 6 -> 6, of which waited for: 2 -> 2; matrix products, arithmetic and copies ran while one was open for 0% -> 0% of each run, Pallas kernels for 48% -> 47%
where the time goes in v7:
time: 71.5 us; the launch traced here: 71.3 us
  Pallas kernels  49 us (69%)
  starting transfers between devices  16.2 us (23%)
  local copies, waits for them, and re-layouts  2.9 us (4%)
  waiting for transfers between devices  2.26 us (3%)
  between operations  0.91 us (1%)
    pallas_call x1, Pallas kernels, body(): pl.pallas_call(lambda *a: inner_kernel(rows_total, *a), out_shape=[sds(IT...  17.1 us
    pallas_call x1, Pallas kernels, body(): pl.pallas_call(lambda *a: edge_kernel(rows_total, *a), out_shape=[sds(NT,...  11.5 us
    pallas_call x1, Pallas kernels, body(): pl.pallas_call(lambda *a: strip_kernel(rows_total, *a), out_shape=[sds(*t...  11 us
    ppermute x1, starting transfers between devices, body(): y_s = lax.ppermute(y_up, 'ty', north)  6.46 us
    pallas_call x1, Pallas kernels, body(): pl.pallas_call(tracer_pack_kernel, out_shape=[y_shape, y_shape, sds(LV, 4...  5.21 us
    ppermute x1, starting transfers between devices, body(): x_e = lax.ppermute(x_l, 'tx', west)  3.84 us
    unnamed x14, local copies, waits for them, and re-layouts  2.9 us
    ppermute x1, starting transfers between devices, body(): v_pair = lax.ppermute(velocity, 'set', swap)  2.55 us
  transfers between devices with their start and end apart: 6, of which 2 were waited for; matrix products, arithmetic and copies ran while one was open for 0% of the time, Pallas kernels for 47%

profile of v7, /device:TPU:1, one launch (start us, length us, event | category | flops | bytes accessed | tf_op | source)
XLA Modules:
  0.0 71.3 jit_solution(16966776048056205950)
XLA Ops:
  0.6 2.5 %collective-permute-start.1 = (f32[2,8,16,256]{3,2,1,0:T(8,128)}, f32[2,8,16,256]{3,2,1,0:T(8,128)S(1)}, u32[]{:S(2)}, u32[]{:S(2)}) collective-permute-start(f32[2,8,16,256]{3,2,1,0:T(8,128)} %vo.1), channel_id=1, source_target_pairs={{0,64},{64,0},{1,65},{65,1},{2,66},{66,2},{3,67},{67,3},{4,68},{68... | collective-permute-start | bytes 786440 | tf_op jit(solution)/shard_map/ppermute | solution.py:685
  3.2 0.1 collective-permute-start
  3.3 0.0 copy-start
  3.3 2.2 %copy-done = f32[16,16,16,256]{3,2,1,0:T(8,128)S(1)} copy-done((f32[16,16,16,256]{3,2,1,0:T(8,128)S(1)}, f32[16,16,16,256]{3,2,1,0:T(8,128)}, u32[]{:S(2)}) %copy-start) | copy-done | bytes 4194328
  5.5 0.0 copy-start.6
  5.5 0.7 copy-done.6
  6.2 0.0 copy-start.1
  6.2 0.0 copy-start.2
  6.2 0.0 copy-start.3
  6.2 0.0 copy-start.4
  6.2 0.0 copy-start.5
  6.2 5.2 %tracer_pack.1 = (f32[161,2,8,128]{3,2,1,0:T(8,128)S(1)}, f32[161,2,8,128]{3,2,1,0:T(8,128)S(1)}, f32[16,4,16,128]{3,2,1,0:T(8,128)S(1)}, f32[16,16,128]{2,1,0:T...) custom-call(f32[16,16,16,256]{3,2,1,0:T(8,128)S(1)} %copy-done, ...), custom_call_target="tpu_custom_call" | custom-call | tf_op jit(solution)/shard_map/tracer_pack/pallas_call | solution.py:688
  11.4 0.1 pad_add_fusion.scal.a_0_
  11.5 0.7 %collective-permute-done.hp = f32[8,16,256]{2,1,0:T(8,128)S(1)} collective-permute-done((f32[8,16,256]{2,1,0:T(8,128)}, f32[8,16,256]{2,1,0:T(8,128)S(1)}, u32[]{:S(2)}, u32[]{:S(2)}) %collective-permute-start) | collective-permute-done | bytes 131104 | tf_op jit(solution)/shard_map/ppermute | solution.py:684
  12.2 0.0 collective-permute-done.1.vp
  12.2 0.0 copy-done.1
  12.2 0.0 copy-done.2
  12.2 0.0 copy-done.3
  12.2 0.0 copy-done.4
  12.2 0.0 copy-done.5
  12.2 1.7 %field_pack.1 = (f32[161,2,8,128]{3,2,1,0:T(8,128)S(1)}, f32[161,2,8,128]{3,2,1,0:T(8,128)S(1)}, f32[17,16,128]{2,1,0:T(8,128)S(1)}, f32[16,2,32,128]{3,2,1,0:T(...) custom-call(s32[2]{0:T(128)S(1)} %pad_add_fusion.scal.a_0_, ...), custom_call_target="tpu_custom_call", output_to_operand_aliasing={{0}: (8, {}), {1}: (9, {})} | custom-call | tf_op jit(solution)/shard_map/field_pack/pallas_call | solution.py:696
  13.9 6.5 %collective-permute-start.2 = (f32[161,2,8,128]{3,2,1,0:T(8,128)S(1)}, f32[161,2,8,128]{3,2,1,0:T(8,128)S(1)}, u32[]{:S(2)}, u32[]{:S(2)}) collective-permute-start(f32[161,2,8,128]{3,2,1,0:T(8,128)S(1)} %get-tuple-element.44), channel_id=1, source_target_pairs={{0,1},{1,2},{2,3},{4,5},{5,6},{6,7},{8,9},{9,10},{10,11},{12,13},{... | collective-permute-start | bytes 3956744 | tf_op jit(solution)/shard_map/ppermute | solution.py:708
  20.4 1.9 %collective-permute-start.3 = (f32[161,2,8,128]{3,2,1,0:T(8,128)S(1)}, f32[161,2,8,128]{3,2,1,0:T(8,128)S(1)}, u32[]{:S(2)}, u32[]{:S(2)}) collective-permute-start(f32[161,2,8,128]{3,2,1,0:T(8,128)S(1)} %get-tuple-element.45), channel_id=1, source_target_pairs={{1,0},{2,1},{3,2},{5,4},{6,5},{7,6},{9,8},{10,9},{11,10},{13,12},{... | collective-permute-start | bytes 3956744 | tf_op jit(solution)/shard_map/ppermute | solution.py:709
  22.3 17.1 %inner.1 = (f32[3,16,16,2,8,128]{5,4,3,2,1,0:T(8,128)S(1)}, f32[3,3,16,2,8,128]{5,4,3,2,1,0:T(8,128)S(1)}, f32[16,16,2,16,128]{4,3,2,1,0:T(8,128)S(1)}, f32[3,16,2,8,128]{4,3,2,1,0:T(8,128)S(1)}) custom-call(s32[2]{0:T(128)S(1)} %pad_add_fusion.scal.a_0_, f32[16,16,2,32,128]{4,3,2,1,0:T(8,128)S(1)} %get-tuple-element.46.a_1_, ...), custom_call_target="tpu_custom_call" | custom-call | tf_op jit(solution)/shard_map/inner/pallas_call | solution.py:710
  39.4 0.0 collective-permute-done.2.y_s.a_7_
  39.4 1.5 %collective-permute-done.3.y_n.a_8_ = f32[161,2,8,128]{3,2,1,0:T(8,128)S(1)} collective-permute-done((f32[161,2,8,128]{3,2,1,0:T(8,128)S(1)}, f32[161,2,8,128]{3,2,1,0:T(8,128)S(1)}, u32[]{:S(2)}, u32[]{:S(2)}) %collective-permute-start.3) | collective-permute-done | bytes 1318944 | tf_op jit(solution)/shard_map/ppermute | solution.py:709
  40.9 2.5 %halo_pack.1 = (f32[17,5,8,128]{3,2,1,0:T(8,128)S(1)}, f32[17,24,128]{2,1,0:T(8,128)S(1)}, f32[17,24,128]{2,1,0:T(8,128)S(1)}) custom-call(f32[161,2,8,128]{3,2,1,0:T(8,128)S(1)} %collective-permute-done.2.y_s.a_7_, f32[161,2,8,128]{3,2,1,0:T(8,128)S(1)} %collective-permute-done.3.y_n.a_8_, f32[17,16,128]{2,1,0:T(8,128)S(1)} %get-tuple-element.43.own_f.a_2_, ...), custom_call_target="tpu_custom_call" | custom-call | tf_op jit(solution)/shard_map/halo_pack/pallas_call | solution.py:722
  43.4 1.3 %collective-permute-start.4 = (f32[17,24,128]{2,1,0:T(8,128)S(1)}, f32[17,24,128]{2,1,0:T(8,128)S(1)}, u32[]{:S(2)}, u32[]{:S(2)}) collective-permute-start(f32[17,24,128]{2,1,0:T(8,128)S(1)} %get-tuple-element.59), channel_id=1, source_target_pairs={{0,4},{4,8},{8,12},{12,16},{16,20},{20,24},{24,28},{28,32},{32,36}... | collective-permute-start | bytes 626696 | tf_op jit(solution)/shard_map/ppermute | solution.py:729
  44.7 3.8 %collective-permute-start.5 = (f32[17,24,128]{2,1,0:T(8,128)S(1)}, f32[17,24,128]{2,1,0:T(8,128)S(1)}, u32[]{:S(2)}, u32[]{:S(2)}) collective-permute-start(f32[17,24,128]{2,1,0:T(8,128)S(1)} %get-tuple-element.60), channel_id=1, source_target_pairs={{4,0},{8,4},{12,8},{16,12},{20,16},{24,20},{28,24},{32,28},{36,32}... | collective-permute-start | bytes 626696 | tf_op jit(solution)/shard_map/ppermute | solution.py:730
  48.6 11.5 %edge.1 = (f32[16,16,2,16,128]{4,3,2,1,0:T(8,128)S(1)}, f32[3,16,2,8,128]{4,3,2,1,0:T(8,128)S(1)}) custom-call(s32[2]{0:T(128)S(1)} %pad_add_fusion.scal.a_0_, f32[16,16,2,8,128]{4,3,2,1,0:T(8,128)S(1)} %get-tuple-element.63.a_1_, f32[3,16,16,2,8,128]{5,4,3,2,1,0:T(8,128)S(1)} %get-tuple-element.64.a_2_, ...), custom_call_target="tpu_custom_call" | custom-call | tf_op jit(solution)/shard_map/edge/pallas_call | solution.py:731
  60.1 0.0 collective-permute-done.4.a_4_
  60.1 0.0 collective-permute-done.5.a_5_
  60.1 11.0 %strips.1 = (f32[16,16,16,256]{3,2,1,0:T(8,128)}, f32[8,16,256]{2,1,0:T(8,128)}, f32[2,8,16,256]{3,2,1,0:T(8,128)}) custom-call(s32[2]{0:T(128)S(1)} %pad_add_fusion.scal.a_0_, f32[16,4,16,128]{3,2,1,0:T(8,128)S(1)} %get-tuple-element.36.a_1_, f32[17,16,128]{2,1,0:T(8,128)S(1)} %get-tuple-element.43.own_f.a_2_, ...), custom_call_target="tpu_custom_call" | custom-call | tf_op jit(solution)/shard_map/strips/pallas_call | solution.py:745
Async XLA Ops:
  0.6 11.6 %collective-permute-start.1 = (f32[2,8,16,256]{3,2,1,0:T(8,128)}, f32[2,8,16,256]{3,2,1,0:T(8,128)S(1)}, u32[]{:S(2)}, u32[]{:S(2)}) collective-permute-start(f32[2,8,16,256]{3,2,1,0:T(8,128)} %vo.1), channel_id=1, source_target_pairs={{0,64},{64,0},{1,65},{65,1},{2,66},{66,2},{3,67},{67,3},{4,68},{68... | collective-permute-start | bytes 786440 | tf_op jit(solution)/shard_map/ppermute | solution.py:685
  3.2 9.0 %collective-permute-start = (f32[8,16,256]{2,1,0:T(8,128)}, f32[8,16,256]{2,1,0:T(8,128)S(1)}, u32[]{:S(2)}, u32[]{:S(2)}) collective-permute-start(f32[8,16,256]{2,1,0:T(8,128)} %ho.1), channel_id=1, source_target_pairs={{0,64},{64,0},{1,65},{65,1},{2,66},{66,2},{3,67},{67,3},{4,68},{68... | collective-permute-start | bytes 393224 | tf_op jit(solution)/shard_map/ppermute | solution.py:684
  3.3 2.2 %copy-start = (f32[16,16,16,256]{3,2,1,0:T(8,128)S(1)}, f32[16,16,16,256]{3,2,1,0:T(8,128)}, u32[]{:S(2)}) copy-start(f32[16,16,16,256]{3,2,1,0:T(8,128)} %tr.1) | copy-start | bytes 12582916
  5.5 0.7 copy-start.6
  6.2 6.1 %copy-start.1 = (f32[2,8,16,256]{3,2,1,0:T(8,128)S(1)}, f32[2,8,16,256]{3,2,1,0:T(8,128)}, u32[]{:S(2)}) copy-start(f32[2,8,16,256]{3,2,1,0:T(8,128)} %vo.1) | copy-start | bytes 786436
  6.2 6.1 %copy-start.2 = (f32[16,16,256]{2,1,0:T(8,128)S(1)}, f32[16,16,256]{2,1,0:T(8,128)}, u32[]{:S(2)}) copy-start(f32[16,16,256]{2,1,0:T(8,128)} %df.1) | copy-start | bytes 786436
  6.2 6.1 %copy-start.3 = (f32[8,16,256]{2,1,0:T(8,128)S(1)}, f32[8,16,256]{2,1,0:T(8,128)}, u32[]{:S(2)}) copy-start(f32[8,16,256]{2,1,0:T(8,128)} %ho.1) | copy-start | bytes 393220
  6.2 6.1 %copy-start.4 = (s32[16,256]{1,0:T(8,128)S(1)}, s32[16,256]{1,0:T(8,128)}, u32[]{:S(2)}) copy-start(s32[16,256]{1,0:T(8,128)} %land.1) | copy-start | bytes 49156
  6.2 6.1 %copy-start.5 = (s32[16,256]{1,0:T(8,128)S(1)}, s32[16,256]{1,0:T(8,128)}, u32[]{:S(2)}) copy-start(s32[16,256]{1,0:T(8,128)} %level.1) | copy-start | bytes 49156
  13.9 25.5 %collective-permute-start.2 = (f32[161,2,8,128]{3,2,1,0:T(8,128)S(1)}, f32[161,2,8,128]{3,2,1,0:T(8,128)S(1)}, u32[]{:S(2)}, u32[]{:S(2)}) collective-permute-start(f32[161,2,8,128]{3,2,1,0:T(8,128)S(1)} %get-tuple-element.44), channel_id=1, source_target_pairs={{0,1},{1,2},{2,3},{4,5},{5,6},{6,7},{8,9},{9,10},{10,11},{12,13},{... | collective-permute-start | bytes 3956744 | tf_op jit(solution)/shard_map/ppermute | solution.py:708
  20.4 20.5 %collective-permute-start.3 = (f32[161,2,8,128]{3,2,1,0:T(8,128)S(1)}, f32[161,2,8,128]{3,2,1,0:T(8,128)S(1)}, u32[]{:S(2)}, u32[]{:S(2)}) collective-permute-start(f32[161,2,8,128]{3,2,1,0:T(8,128)S(1)} %get-tuple-element.45), channel_id=1, source_target_pairs={{1,0},{2,1},{3,2},{5,4},{6,5},{7,6},{9,8},{10,9},{11,10},{13,12},{... | collective-permute-start | bytes 3956744 | tf_op jit(solution)/shard_map/ppermute | solution.py:709
  43.4 16.6 %collective-permute-start.4 = (f32[17,24,128]{2,1,0:T(8,128)S(1)}, f32[17,24,128]{2,1,0:T(8,128)S(1)}, u32[]{:S(2)}, u32[]{:S(2)}) collective-permute-start(f32[17,24,128]{2,1,0:T(8,128)S(1)} %get-tuple-element.59), channel_id=1, source_target_pairs={{0,4},{4,8},{8,12},{12,16},{16,20},{20,24},{24,28},{28,32},{32,36}... | collective-permute-start | bytes 626696 | tf_op jit(solution)/shard_map/ppermute | solution.py:729
  44.7 15.4 %collective-permute-start.5 = (f32[17,24,128]{2,1,0:T(8,128)S(1)}, f32[17,24,128]{2,1,0:T(8,128)S(1)}, u32[]{:S(2)}, u32[]{:S(2)}) collective-permute-start(f32[17,24,128]{2,1,0:T(8,128)S(1)} %get-tuple-element.60), channel_id=1, source_target_pairs={{4,0},{8,4},{12,8},{16,12},{20,16},{24,20},{28,24},{32,28},{36,32}... | collective-permute-start | bytes 626696 | tf_op jit(solution)/shard_map/ppermute | solution.py:730

commit v8 on v7

--- a/solution.py
+++ b/solution.py
@@ -265,17 +265,16 @@
         c.wait()
 
 
-def inner_kernel(rows_total, scal, c_first, h_first, u_first, v_first, d_buf, p_buf, table, saved, saved_f, mid, mid_f,
-                 h_buf, u_buf, v_buf, flux, one_a, one_b, two_a, two_b, solved_a, solved_b, coef, ratio):
+def inner_kernel(rows_total, scal, c_first, h_first, u_first, v_first, d_buf, p_buf, table, one_a, one_b, two_a, two_b, three_a, three_b, saved_f, mid, mid_f,
+                 h_buf, u_buf, v_buf, flux, solved_a, solved_b, coef, ratio):
     rows = lax.broadcasted_iota(jnp.int32, (16, 128), 0) + scal[1]
     cor_c = coriolis_of(rows, rows_total)
     d_c = [p_buf[j, 8:24, :] for j in range(2)]
     d_e = [jnp.minimum(a, b) for a, b in zip(d_c, from_east(d_c))]
     d_n = [jnp.minimum(d_c[j], p_buf[j, 9:25, :]) for j in range(2)]
-    c_one, c_two = (one_a, one_b), (two_a, two_b)
-    buffers = ((c_first.at[pl.ds(0, PER)], c_first.at[pl.ds(PER, PER)]), c_one, c_two, c_one, None)
+    buffers = ((c_first.at[pl.ds(0, PER)], c_first.at[pl.ds(PER, PER)]), (one_a, one_b), (two_a, two_b), (three_a, three_b), None)
     solved = (solved_a, solved_b)
-    pending, keep, slot = None, None, 0
+    pending, slot = None, 0
     for n in range(1, ITERS + 1):
         src, dst = buffers[n - 1], buffers[n]
         old = (h_first, u_first, v_first) if n == 1 else (h_buf, u_buf, v_buf)
@@ -314,10 +313,10 @@
 
         for s in range(2):
             for r0 in ((8, 16) if n < ITERS else (12,)):
-                def down(k, before, s=s, r0=r0, src=src, slot=slot):
+                def down(k, before, s=s, r0=r0, src=src, slot=slot, base=r0 if n == 1 else r0 - 4):
                     co = [[coef[c, k, j, r0 - 8:r0, :] for j in range(2)] for c in range(6)]
                     read = lambda t, r: [src[s][t, k, j, r:r + 8, :] for j in range(2)]
-                    now = forward(co, [(read(t, r0), read(t, r0 - 1), read(t, r0 + 1)) for t in range(PER)], before)
+                    now = forward(co, [(read(t, base), read(t, base - 1), read(t, base + 1)) for t in range(PER)], before)
                     for t in range(PER):
                         for j in range(2):
                             solved[slot][k, t, j] = now[t][j]
@@ -330,7 +329,7 @@
                     for t in range(PER):
                         for j in range(2):
                             if n < ITERS:
-                                dst[s][t, k, j, r0:r0 + 8, :] = outs[t][j]
+                                dst[s][t, k, j, r0 - 4:r0 + 4, :] = outs[t][j]
                             else:
                                 mid[s * PER + t, k, j, 4:12, :] = outs[t][j]
                     return m
@@ -338,16 +337,6 @@
                 sweep(down, pending)
                 pending = upward
                 slot = 1 - slot
-                if keep is not None:
-                    keep()
-                    keep = None
-
-        def keep(n=n, dst=dst):
-            @pl.loop(0, LV, unroll=2)
-            def _(k):
-                for t in range(NT):
-                    for j in range(2):
-                        saved[n - 1, t, k, j] = keep_rows(n, lambda r: dst[t // PER][t % PER, k, j, r:r + 8, :])
 
     sweep(None, pending)
 
@@ -395,13 +384,14 @@
     x_l[LV, 16:24, :] = to_west(packed, 4)
 
 
-def edge_kernel(rows_total, scal, kept, saved, saved_f, h_first, u_first, v_first, y_s, y_n, d_first, p_first, table, mid,
+def edge_kernel(rows_total, scal, kept, one_a, one_b, two_a, two_b, three_a, three_b, saved_f, h_first, u_first, v_first, y_s, y_n, d_first, p_first, table, mid,
                 out_c, out_f, *scratch):
-    c_buf = [scratch[2 * n:2 * n + 2] for n in range(ITERS)]
-    f_buf, d_buf, p_buf, solved_a, solved_b, coef, ratio = scratch[2 * ITERS:]
+    c_buf = [scratch[2 * (n % 2):2 * (n % 2) + 2] for n in range(ITERS)]
+    f_buf, d_buf, p_buf, solved_a, solved_b, coef, ratio = scratch[4:]
     solved = (solved_a, solved_b)
+    stages = (None, (one_a, one_b), (two_a, two_b), (three_a, three_b))
     sub = sub_iota()
-    low = sub < 4
+    low, six = sub < 4, sub < 6
     high = jnp.logical_not(low)
 
     def put(ref, inside, ys, yn, half):
@@ -494,7 +484,11 @@
                 for t in range(PER):
                     for j in range(2):
                         if n < ITERS:
-                            c_buf[n][s][t, k, j, 0:8, :] = jnp.where(low, outs[t][j], saved[n - 1, s * PER + t, k, j])
+                            inside = stages[n][s].at[t, k, j]
+                            first = c_buf[n][s].at[t, k, j, pl.ds(0, 8), :]
+                            pltpu.store(first, outs[t][j], mask=low)
+                            pltpu.store(first, inside[n:n + 8, :], mask=high & six)
+                            pltpu.store(first, inside[12 - n:20 - n, :], mask=jnp.logical_not(six))
                             pltpu.store(c_buf[n][s].at[t, k, j, pl.ds(4, 8), :], outs[t][j], mask=high)
                         else:
                             inside = mid.at[s * PER + t, k, j]
@@ -707,17 +701,16 @@
     south = [(j, i) for i, j in north]
     y_s = lax.ppermute(y_up, "ty", north)
     y_n = lax.ppermute(y_dn, "ty", south)
-    saved, saved_f, mid, mid_f = pl.pallas_call(
+    *stages, saved_f, mid, mid_f = pl.pallas_call(
         lambda *a: inner_kernel(rows_total, *a),
-        out_shape=[sds(ITERS - 1, NT, LV, 2, 8, 128), sds(ITERS - 1, 3, LV, 2, 8, 128), sds(NT, LV, 2, 16, 128), sds(3, LV, 2, 8, 128)],
-        in_specs=[SMEM] + [VMEM] * 7, out_specs=[VMEM] * 4,
+        out_shape=[sds(PER, LV, 2, 24, 128)] * (2 * ITERS - 2) + [sds(ITERS - 1, 3, LV, 2, 8, 128), sds(NT, LV, 2, 16, 128), sds(3, LV, 2, 8, 128)],
+        in_specs=[SMEM] + [VMEM] * 7, out_specs=[VMEM] * (2 * ITERS + 1),
         scratch_shapes=[pltpu.VMEM((LV, 2, 32, 128), F32)] * 4 + [
-            pltpu.VMEM((PER, LV, 2, 32, 128), F32)] * 4 + [
             pltpu.VMEM((LV, PER, 2, 8, 128), F32),
             pltpu.VMEM((LV, PER, 2, 8, 128), F32),
             pltpu.VMEM((6, LV, 2, 16, 128), F32),
             pltpu.VMEM((2, LV, 2, 16, 128), F32)],
-        compiler_params=room(26), name="inner")(scal, c_first, h_first, u_first, v_first, d_first, p_first, table)
+        compiler_params=room(8), name="inner")(scal, c_first, h_first, u_first, v_first, d_first, p_first, table)
     y_s, y_n, mid_f = lax.optimization_barrier((y_s, y_n, mid_f))
     halo, x_r, x_l = pl.pallas_call(
         halo_pack_kernel, out_shape=[sds(LV + 1, 5, 8, 128), sds(LV + 1, 24, 128), sds(LV + 1, 24, 128)],
@@ -731,8 +724,8 @@
     edge, edge_f = pl.pallas_call(
         lambda *a: edge_kernel(rows_total, *a),
         out_shape=[sds(NT, LV, 2, 16, 128), sds(3, LV, 2, 8, 128)],
-        in_specs=[SMEM] + [VMEM] * 12, out_specs=[VMEM] * 2,
-        scratch_shapes=[pltpu.VMEM((PER, LV, 2, 16, 128), F32)] * (2 * ITERS) + [
+        in_specs=[SMEM] + [VMEM] * 17, out_specs=[VMEM] * 2,
+        scratch_shapes=[pltpu.VMEM((PER, LV, 2, 16, 128), F32)] * 4 + [
             pltpu.VMEM((ITERS, 3, LV, 2, 16, 128), F32),
             pltpu.VMEM((LV, 2, 32, 128), F32),
             pltpu.VMEM((2, 32, 128), jnp.int32),
@@ -740,8 +733,8 @@
             pltpu.VMEM((LV, PER, 2, 8, 128), F32),
             pltpu.VMEM((6, LV, 2, 8, 128), F32),
             pltpu.VMEM((2, LV, 2, 8, 128), F32)],
-        compiler_params=room(25), name="edge")(
-            scal, kept, saved, saved_f, h_first, u_first, v_first, y_s, y_n, d_first, p_first, table, mid)
+        compiler_params=room(17), name="edge")(
+            scal, kept, *stages, saved_f, h_first, u_first, v_first, y_s, y_n, d_first, p_first, table, mid)
     return pl.pallas_call(
         lambda *a: strip_kernel(rows_total, *a),
         out_shape=[sds(*tracers.shape), sds(*thickness.shape), sds(*velocity.shape)],

time: 71.5 us -> 72.2 us (level)
  no operation moved by 1% of the time
where the time goes in v8:
time: 72.2 us; the launch traced here: 72 us
  Pallas kernels  49.3 us (68%)
  starting transfers between devices  16.2 us (22%)
  local copies, waits for them, and re-layouts  2.9 us (4%)
  waiting for transfers between devices  2.67 us (4%)
  between operations  0.91 us (1%)
    pallas_call x1, Pallas kernels, body(): pl.pallas_call(lambda *a: inner_kernel(rows_total, *a), out_shape=[sds(PE...  16.6 us
    pallas_call x1, Pallas kernels, body(): pl.pallas_call(lambda *a: edge_kernel(rows_total, *a), out_shape=[sds(NT,...  12.2 us
    pallas_call x1, Pallas kernels, body(): pl.pallas_call(lambda *a: strip_kernel(rows_total, *a), out_shape=[sds(*t...  11 us
    ppermute x1, starting transfers between devices, body(): y_s = lax.ppermute(y_up, 'ty', north)  6.46 us
    pallas_call x1, Pallas kernels, body(): pl.pallas_call(tracer_pack_kernel, out_shape=[y_shape, y_shape, sds(LV, 4...  5.26 us
    ppermute x1, starting transfers between devices, body(): x_e = lax.ppermute(x_l, 'tx', west)  3.84 us
    unnamed x14, local copies, waits for them, and re-layouts  2.9 us
    ppermute x1, starting transfers between devices, body(): v_pair = lax.ppermute(velocity, 'set', swap)  2.55 us
  transfers between devices with their start and end apart: 6, of which 2 were waited for; matrix products, arithmetic and copies ran while one was open for 0% of the time, Pallas kernels for 47%

profile of v8, /device:TPU:1, one launch (start us, length us, event | category | flops | bytes accessed | tf_op | source)
XLA Modules:
  0.0 72.0 jit_solution(8742308672129447680)
XLA Ops:
  0.6 2.5 %collective-permute-start.1 = (f32[2,8,16,256]{3,2,1,0:T(8,128)}, f32[2,8,16,256]{3,2,1,0:T(8,128)S(1)}, u32[]{:S(2)}, u32[]{:S(2)}) collective-permute-start(f32[2,8,16,256]{3,2,1,0:T(8,128)} %vo.1), channel_id=1, source_target_pairs={{0,64},{64,0},{1,65},{65,1},{2,66},{66,2},{3,67},{67,3},{4,68},{68... | collective-permute-start | bytes 786440 | tf_op jit(solution)/shard_map/ppermute | solution.py:679
  3.2 0.1 collective-permute-start
  3.3 0.0 copy-start
  3.3 2.2 %copy-done = f32[16,16,16,256]{3,2,1,0:T(8,128)S(1)} copy-done((f32[16,16,16,256]{3,2,1,0:T(8,128)S(1)}, f32[16,16,16,256]{3,2,1,0:T(8,128)}, u32[]{:S(2)}) %copy-start) | copy-done | bytes 4194328
  5.5 0.0 copy-start.6
  5.5 0.7 copy-done.6
  6.2 0.0 copy-start.1
  6.2 0.0 copy-start.2
  6.2 0.0 copy-start.3
  6.2 0.0 copy-start.4
  6.2 0.0 copy-start.5
  6.2 5.3 %tracer_pack.1 = (f32[161,2,8,128]{3,2,1,0:T(8,128)S(1)}, f32[161,2,8,128]{3,2,1,0:T(8,128)S(1)}, f32[16,4,16,128]{3,2,1,0:T(8,128)S(1)}, f32[16,16,128]{2,1,0:T...) custom-call(f32[16,16,16,256]{3,2,1,0:T(8,128)S(1)} %copy-done, ...), custom_call_target="tpu_custom_call" | custom-call | tf_op jit(solution)/shard_map/tracer_pack/pallas_call | solution.py:682
  11.5 0.1 pad_add_fusion.scal.a_0_
  11.5 0.7 collective-permute-done.hp
  12.2 0.0 collective-permute-done.1.vp
  12.2 0.0 copy-done.1
  12.2 0.0 copy-done.2
  12.2 0.0 copy-done.3
  12.2 0.0 copy-done.4
  12.2 0.0 copy-done.5
  12.2 1.7 %field_pack.1 = (f32[161,2,8,128]{3,2,1,0:T(8,128)S(1)}, f32[161,2,8,128]{3,2,1,0:T(8,128)S(1)}, f32[17,16,128]{2,1,0:T(8,128)S(1)}, f32[16,2,32,128]{3,2,1,0:T(...) custom-call(s32[2]{0:T(128)S(1)} %pad_add_fusion.scal.a_0_, ...), custom_call_target="tpu_custom_call", output_to_operand_aliasing={{0}: (8, {}), {1}: (9, {})} | custom-call | tf_op jit(solution)/shard_map/field_pack/pallas_call | solution.py:690
  13.9 6.5 %collective-permute-start.2 = (f32[161,2,8,128]{3,2,1,0:T(8,128)S(1)}, f32[161,2,8,128]{3,2,1,0:T(8,128)S(1)}, u32[]{:S(2)}, u32[]{:S(2)}) collective-permute-start(f32[161,2,8,128]{3,2,1,0:T(8,128)S(1)} %get-tuple-element.49), channel_id=1, source_target_pairs={{0,1},{1,2},{2,3},{4,5},{5,6},{6,7},{8,9},{9,10},{10,11},{12,13},{... | collective-permute-start | bytes 3956744 | tf_op jit(solution)/shard_map/ppermute | solution.py:702
  20.4 1.9 %collective-permute-start.3 = (f32[161,2,8,128]{3,2,1,0:T(8,128)S(1)}, f32[161,2,8,128]{3,2,1,0:T(8,128)S(1)}, u32[]{:S(2)}, u32[]{:S(2)}) collective-permute-start(f32[161,2,8,128]{3,2,1,0:T(8,128)S(1)} %get-tuple-element.50), channel_id=1, source_target_pairs={{1,0},{2,1},{3,2},{5,4},{6,5},{7,6},{9,8},{10,9},{11,10},{13,12},{... | collective-permute-start | bytes 3956744 | tf_op jit(solution)/shard_map/ppermute | solution.py:703
  22.3 16.6 %inner.1 = (f32[8,16,2,24,128]{4,3,2,1,0:T(8,128)S(1)}, f32[8,16,2,24,128]{4,3,2,1,0:T(8,128)S(1)}, f32[8,16,2,24,128]{4,3,2,1,0:T(8,128)S(1)}, f32[8,16,2,24,12...) custom-call(s32[2]{0:T(128)S(1)} %pad_add_fusion.scal.a_0_, ...), custom_call_target="tpu_custom_call" | custom-call | tf_op jit(solution)/shard_map/inner/pallas_call | solution.py:704
  38.9 0.0 collective-permute-done.2.y_s.a_12_
  39.0 2.0 %collective-permute-done.3.y_n.a_13_ = f32[161,2,8,128]{3,2,1,0:T(8,128)S(1)} collective-permute-done((f32[161,2,8,128]{3,2,1,0:T(8,128)S(1)}, f32[161,2,8,128]{3,2,1,0:T(8,128)S(1)}, u32[]{:S(2)}, u32[]{:S(2)}) %collective-permute-start.3) | collective-permute-done | bytes 1318944 | tf_op jit(solution)/shard_map/ppermute | solution.py:703
  40.9 2.5 %halo_pack.1 = (f32[17,5,8,128]{3,2,1,0:T(8,128)S(1)}, f32[17,24,128]{2,1,0:T(8,128)S(1)}, f32[17,24,128]{2,1,0:T(8,128)S(1)}) custom-call(f32[161,2,8,128]{3,2,1,0:T(8,128)S(1)} %collective-permute-done.2.y_s.a_12_, f32[161,2,8,128]{3,2,1,0:T(8,128)S(1)} %collective-permute-done.3.y_n.a_13_, f32[17,16,128]{2,1,0:T(8,128)S(1)} %get-tuple-element.48.own_f.a_2_, ...), custom_call_target="tpu_custom_call" | custom-call | tf_op jit(solution)/shard_map/halo_pack/pallas_call | solution.py:715
  43.5 1.3 %collective-permute-start.4 = (f32[17,24,128]{2,1,0:T(8,128)S(1)}, f32[17,24,128]{2,1,0:T(8,128)S(1)}, u32[]{:S(2)}, u32[]{:S(2)}) collective-permute-start(f32[17,24,128]{2,1,0:T(8,128)S(1)} %get-tuple-element.64), channel_id=1, source_target_pairs={{0,4},{4,8},{8,12},{12,16},{16,20},{20,24},{24,28},{28,32},{32,36}... | collective-permute-start | bytes 626696 | tf_op jit(solution)/shard_map/ppermute | solution.py:722
  44.8 3.8 %collective-permute-start.5 = (f32[17,24,128]{2,1,0:T(8,128)S(1)}, f32[17,24,128]{2,1,0:T(8,128)S(1)}, u32[]{:S(2)}, u32[]{:S(2)}) collective-permute-start(f32[17,24,128]{2,1,0:T(8,128)S(1)} %get-tuple-element.65), channel_id=1, source_target_pairs={{4,0},{8,4},{12,8},{16,12},{20,16},{24,20},{28,24},{32,28},{36,32}... | collective-permute-start | bytes 626696 | tf_op jit(solution)/shard_map/ppermute | solution.py:723
  48.6 12.2 %edge.1 = (f32[16,16,2,16,128]{4,3,2,1,0:T(8,128)S(1)}, f32[3,16,2,8,128]{4,3,2,1,0:T(8,128)S(1)}) custom-call(s32[2]{0:T(128)S(1)} %pad_add_fusion.scal.a_0_, f32[16,16,2,8,128]{4,3,2,1,0:T(8,128)S(1)} %get-tuple-element.68.a_1_, f32[8,16,2,24,128]{4,3,2,1,0:T(8,128)S(1)} %get-tuple-element.69.a_2_, f32[8,16,2,24,128]{4,3,2,1,0:T(8,128)S(1)} %get-tuple-element.70.a_3_, ...), custom_call_target="tpu_custom_call" | custom-call | tf_op jit(solution)/shard_map/edge/pallas_call | solution.py:724
  60.8 0.0 collective-permute-done.4.a_4_
  60.8 0.0 collective-permute-done.5.a_5_
  60.8 11.0 %strips.1 = (f32[16,16,16,256]{3,2,1,0:T(8,128)}, f32[8,16,256]{2,1,0:T(8,128)}, f32[2,8,16,256]{3,2,1,0:T(8,128)}) custom-call(s32[2]{0:T(128)S(1)} %pad_add_fusion.scal.a_0_, f32[16,4,16,128]{3,2,1,0:T(8,128)S(1)} %get-tuple-element.41.a_1_, f32[17,16,128]{2,1,0:T(8,128)S(1)} %get-tuple-element.48.own_f.a_2_, ...), custom_call_target="tpu_custom_call" | custom-call | tf_op jit(solution)/shard_map/strips/pallas_call | solution.py:738
Async XLA Ops:
  0.6 11.6 %collective-permute-start.1 = (f32[2,8,16,256]{3,2,1,0:T(8,128)}, f32[2,8,16,256]{3,2,1,0:T(8,128)S(1)}, u32[]{:S(2)}, u32[]{:S(2)}) collective-permute-start(f32[2,8,16,256]{3,2,1,0:T(8,128)} %vo.1), channel_id=1, source_target_pairs={{0,64},{64,0},{1,65},{65,1},{2,66},{66,2},{3,67},{67,3},{4,68},{68... | collective-permute-start | bytes 786440 | tf_op jit(solution)/shard_map/ppermute | solution.py:679
  3.2 9.0 %collective-permute-start = (f32[8,16,256]{2,1,0:T(8,128)}, f32[8,16,256]{2,1,0:T(8,128)S(1)}, u32[]{:S(2)}, u32[]{:S(2)}) collective-permute-start(f32[8,16,256]{2,1,0:T(8,128)} %ho.1), channel_id=1, source_target_pairs={{0,64},{64,0},{1,65},{65,1},{2,66},{66,2},{3,67},{67,3},{4,68},{68... | collective-permute-start | bytes 393224 | tf_op jit(solution)/shard_map/ppermute | solution.py:678
  3.3 2.2 %copy-start = (f32[16,16,16,256]{3,2,1,0:T(8,128)S(1)}, f32[16,16,16,256]{3,2,1,0:T(8,128)}, u32[]{:S(2)}) copy-start(f32[16,16,16,256]{3,2,1,0:T(8,128)} %tr.1) | copy-start | bytes 12582916
  5.5 0.7 copy-start.6
  6.2 6.1 %copy-start.1 = (f32[2,8,16,256]{3,2,1,0:T(8,128)S(1)}, f32[2,8,16,256]{3,2,1,0:T(8,128)}, u32[]{:S(2)}) copy-start(f32[2,8,16,256]{3,2,1,0:T(8,128)} %vo.1) | copy-start | bytes 786436
  6.2 6.1 %copy-start.2 = (f32[16,16,256]{2,1,0:T(8,128)S(1)}, f32[16,16,256]{2,1,0:T(8,128)}, u32[]{:S(2)}) copy-start(f32[16,16,256]{2,1,0:T(8,128)} %df.1) | copy-start | bytes 786436
  6.2 6.1 %copy-start.3 = (f32[8,16,256]{2,1,0:T(8,128)S(1)}, f32[8,16,256]{2,1,0:T(8,128)}, u32[]{:S(2)}) copy-start(f32[8,16,256]{2,1,0:T(8,128)} %ho.1) | copy-start | bytes 393220
  6.2 6.1 %copy-start.4 = (s32[16,256]{1,0:T(8,128)S(1)}, s32[16,256]{1,0:T(8,128)}, u32[]{:S(2)}) copy-start(s32[16,256]{1,0:T(8,128)} %land.1) | copy-start | bytes 49156
  6.2 6.1 %copy-start.5 = (s32[16,256]{1,0:T(8,128)S(1)}, s32[16,256]{1,0:T(8,128)}, u32[]{:S(2)}) copy-start(s32[16,256]{1,0:T(8,128)} %level.1) | copy-start | bytes 49156
  13.9 25.0 %collective-permute-start.2 = (f32[161,2,8,128]{3,2,1,0:T(8,128)S(1)}, f32[161,2,8,128]{3,2,1,0:T(8,128)S(1)}, u32[]{:S(2)}, u32[]{:S(2)}) collective-permute-start(f32[161,2,8,128]{3,2,1,0:T(8,128)S(1)} %get-tuple-element.49), channel_id=1, source_target_pairs={{0,1},{1,2},{2,3},{4,5},{5,6},{6,7},{8,9},{9,10},{10,11},{12,13},{... | collective-permute-start | bytes 3956744 | tf_op jit(solution)/shard_map/ppermute | solution.py:702
  20.4 20.5 %collective-permute-start.3 = (f32[161,2,8,128]{3,2,1,0:T(8,128)S(1)}, f32[161,2,8,128]{3,2,1,0:T(8,128)S(1)}, u32[]{:S(2)}, u32[]{:S(2)}) collective-permute-start(f32[161,2,8,128]{3,2,1,0:T(8,128)S(1)} %get-tuple-element.50), channel_id=1, source_target_pairs={{1,0},{2,1},{3,2},{5,4},{6,5},{7,6},{9,8},{10,9},{11,10},{13,12},{... | collective-permute-start | bytes 3956744 | tf_op jit(solution)/shard_map/ppermute | solution.py:703
  43.5 17.4 %collective-permute-start.4 = (f32[17,24,128]{2,1,0:T(8,128)S(1)}, f32[17,24,128]{2,1,0:T(8,128)S(1)}, u32[]{:S(2)}, u32[]{:S(2)}) collective-permute-start(f32[17,24,128]{2,1,0:T(8,128)S(1)} %get-tuple-element.64), channel_id=1, source_target_pairs={{0,4},{4,8},{8,12},{12,16},{16,20},{20,24},{24,28},{28,32},{32,36}... | collective-permute-start | bytes 626696 | tf_op jit(solution)/shard_map/ppermute | solution.py:722
  44.8 16.1 %collective-permute-start.5 = (f32[17,24,128]{2,1,0:T(8,128)S(1)}, f32[17,24,128]{2,1,0:T(8,128)S(1)}, u32[]{:S(2)}, u32[]{:S(2)}) collective-permute-start(f32[17,24,128]{2,1,0:T(8,128)S(1)} %get-tuple-element.65), channel_id=1, source_target_pairs={{4,0},{8,4},{12,8},{16,12},{20,16},{24,20},{28,24},{32,28},{36,32}... | collective-permute-start | bytes 626696 | tf_op jit(solution)/shard_map/ppermute | solution.py:723

commit v9 on v7

--- a/solution.py
+++ b/solution.py
@@ -188,6 +188,8 @@
                 y_up[t * LV + k, j] = jnp.where(low, read(0, 20), read(PER, 16))
                 y_dn[t * LV + k, j] = jnp.where(low, read(0, 8), read(PER, 4))
             for t in range(NT):
+                c_buf[t, k, j, 0:8, :] = jnp.zeros((8, 128), F32)
+                c_buf[t, k, j, 24:32, :] = jnp.zeros((8, 128), F32)
                 kept[t, k, j] = keep_rows(0, lambda r: c_buf[t, k, j, r:r + 8, :])
         for i in range(2):
             rows = slice(8 * i, 8 * i + 8)
@@ -229,11 +231,14 @@
         c.wait()
 
     for j in range(2):
+        p_buf[j, 0:8, :] = jnp.zeros((8, 128), jnp.int32)
         p_buf[j, 8:24, :] = jnp.where(l_buf[0, j] == 1, l_buf[1, j], 0)
+        p_buf[j, 24:32, :] = jnp.zeros((8, 128), jnp.int32)
 
     @pl.loop(0, LV, unroll=4)
     def _(k):
         for j in range(2):
+            h_buf[k, j, 24:32, :] = jnp.zeros((8, 128), F32)
             d_buf[k, j, 8:24, :] = jnp.where(k + 1 < p_buf[j, 8:24, :], DT * d_buf[k, j, 8:24, :], 0.0)
 
     def put(index, j, first, second):
@@ -287,6 +292,9 @@
 
             def south(fluxes):
                 for j in range(2):
+                    if n == 1:
+                        flux[k, j, 0:8, :] = jnp.zeros((8, 128), F32)
+                        h_buf[k, j, 24:32, :] = jnp.zeros((8, 128), F32)
                     flux[k, j, 8:24, :] = fluxes[j]
                 return read(flux, 7)
 
@@ -331,6 +339,9 @@
                         for j in range(2):
                             if n < ITERS:
                                 dst[s][t, k, j, r0:r0 + 8, :] = outs[t][j]
+                                if n < 3:
+                                    beyond = 0 if r0 == 8 else 24
+                                    dst[s][t, k, j, beyond:beyond + 8, :] = jnp.zeros((8, 128), F32)
                             else:
                                 mid[s * PER + t, k, j, 4:12, :] = outs[t][j]
                     return m
@@ -548,8 +559,13 @@
                     y = jnp.where(slot == q, turned[(q - f) % 4], y)
                 put(buf.at[k], i, y)
 
+        for buf in [c_buf.at[g] for g in range(4)] + [c_alt.at[g] for g in range(4)] + [h_buf, flux]:
+            buf[k, 0:8, :] = jnp.zeros((8, 128), F32)
+            buf[k, 32:40, :] = jnp.zeros((8, 128), F32)
+
     for i in range(3):
         put(p_buf, i, whole(LV, 4, i, 4).astype(jnp.int32))
+    p_buf[32:40, :] = jnp.zeros((8, 128), jnp.int32)
 
     rows = lax.broadcasted_iota(jnp.int32, (24, 128), 0) - 4 + scal[1]
     cor_c = coriolis_of(rows, rows_total)

time: 71.5 us -> 71.5 us (level)
  transfers between devices with their start and end apart: 6 -> 6, of which waited for: 2 -> 2; matrix products, arithmetic and copies ran while one was open for 0% -> 0% of each run, Pallas kernels for 47% -> 48%
where the time goes in v9:
time: 71.5 us; the launch traced here: 71.3 us
  Pallas kernels  49.5 us (69%)
  starting transfers between devices  16.2 us (23%)
  local copies, waits for them, and re-layouts  2.9 us (4%)
  waiting for transfers between devices  1.69 us (2%)
  between operations  0.91 us (1%)
    pallas_call x1, Pallas kernels, body(): pl.pallas_call(lambda *a: inner_kernel(rows_total, *a), out_shape=[sds(IT...  17.5 us
    pallas_call x1, Pallas kernels, body(): pl.pallas_call(lambda *a: edge_kernel(rows_total, *a), out_shape=[sds(NT,...  11.5 us
    pallas_call x1, Pallas kernels, body(): pl.pallas_call(lambda *a: strip_kernel(rows_total, *a), out_shape=[sds(*t...  11 us
    ppermute x1, starting transfers between devices, body(): y_s = lax.ppermute(y_up, 'ty', north)  6.46 us
    pallas_call x1, Pallas kernels, body(): pl.pallas_call(tracer_pack_kernel, out_shape=[y_shape, y_shape, sds(LV, 4...  5.37 us
    ppermute x1, starting transfers between devices, body(): x_e = lax.ppermute(x_l, 'tx', west)  3.84 us
    unnamed x14, local copies, waits for them, and re-layouts  2.9 us
    ppermute x1, starting transfers between devices, body(): v_pair = lax.ppermute(velocity, 'set', swap)  2.55 us
  transfers between devices with their start and end apart: 6, of which 2 were waited for; matrix products, arithmetic and copies ran while one was open for 0% of the time, Pallas kernels for 48%

profile of v9, /device:TPU:1, one launch (start us, length us, event | category | flops | bytes accessed | tf_op | source)
XLA Modules:
  0.0 71.3 jit_solution(17711186714125395604)
XLA Ops:
  0.6 2.5 %collective-permute-start.1 = (f32[2,8,16,256]{3,2,1,0:T(8,128)}, f32[2,8,16,256]{3,2,1,0:T(8,128)S(1)}, u32[]{:S(2)}, u32[]{:S(2)}) collective-permute-start(f32[2,8,16,256]{3,2,1,0:T(8,128)} %vo.1), channel_id=1, source_target_pairs={{0,64},{64,0},{1,65},{65,1},{2,66},{66,2},{3,67},{67,3},{4,68},{68... | collective-permute-start | bytes 786440 | tf_op jit(solution)/shard_map/ppermute | solution.py:701
  3.2 0.1 collective-permute-start
  3.3 0.0 copy-start
  3.3 2.2 %copy-done = f32[16,16,16,256]{3,2,1,0:T(8,128)S(1)} copy-done((f32[16,16,16,256]{3,2,1,0:T(8,128)S(1)}, f32[16,16,16,256]{3,2,1,0:T(8,128)}, u32[]{:S(2)}) %copy-start) | copy-done | bytes 4194328
  5.5 0.0 copy-start.6
  5.5 0.7 copy-done.6
  6.2 0.0 copy-start.1
  6.2 0.0 copy-start.2
  6.2 0.0 copy-start.3
  6.2 0.0 copy-start.4
  6.2 0.0 copy-start.5
  6.2 5.4 %tracer_pack.1 = (f32[161,2,8,128]{3,2,1,0:T(8,128)S(1)}, f32[161,2,8,128]{3,2,1,0:T(8,128)S(1)}, f32[16,4,16,128]{3,2,1,0:T(8,128)S(1)}, f32[16,16,128]{2,1,0:T...) custom-call(f32[16,16,16,256]{3,2,1,0:T(8,128)S(1)} %copy-done, ...), custom_call_target="tpu_custom_call" | custom-call | tf_op jit(solution)/shard_map/tracer_pack/pallas_call | solution.py:704
  11.6 0.1 pad_add_fusion.scal.a_0_
  11.6 0.6 collective-permute-done.hp
  12.2 0.0 collective-permute-done.1.vp
  12.2 0.0 copy-done.1
  12.2 0.0 copy-done.2
  12.2 0.0 copy-done.3
  12.2 0.0 copy-done.4
  12.2 0.0 copy-done.5
  12.2 1.7 %field_pack.1 = (f32[161,2,8,128]{3,2,1,0:T(8,128)S(1)}, f32[161,2,8,128]{3,2,1,0:T(8,128)S(1)}, f32[17,16,128]{2,1,0:T(8,128)S(1)}, f32[16,2,32,128]{3,2,1,0:T(...) custom-call(s32[2]{0:T(128)S(1)} %pad_add_fusion.scal.a_0_, ...), custom_call_target="tpu_custom_call", output_to_operand_aliasing={{0}: (8, {}), {1}: (9, {})} | custom-call | tf_op jit(solution)/shard_map/field_pack/pallas_call | solution.py:712
  13.9 6.5 %collective-permute-start.2 = (f32[161,2,8,128]{3,2,1,0:T(8,128)S(1)}, f32[161,2,8,128]{3,2,1,0:T(8,128)S(1)}, u32[]{:S(2)}, u32[]{:S(2)}) collective-permute-start(f32[161,2,8,128]{3,2,1,0:T(8,128)S(1)} %get-tuple-element.44), channel_id=1, source_target_pairs={{0,1},{1,2},{2,3},{4,5},{5,6},{6,7},{8,9},{9,10},{10,11},{12,13},{... | collective-permute-start | bytes 3956744 | tf_op jit(solution)/shard_map/ppermute | solution.py:724
  20.4 1.9 %collective-permute-start.3 = (f32[161,2,8,128]{3,2,1,0:T(8,128)S(1)}, f32[161,2,8,128]{3,2,1,0:T(8,128)S(1)}, u32[]{:S(2)}, u32[]{:S(2)}) collective-permute-start(f32[161,2,8,128]{3,2,1,0:T(8,128)S(1)} %get-tuple-element.45), channel_id=1, source_target_pairs={{1,0},{2,1},{3,2},{5,4},{6,5},{7,6},{9,8},{10,9},{11,10},{13,12},{... | collective-permute-start | bytes 3956744 | tf_op jit(solution)/shard_map/ppermute | solution.py:725
  22.3 17.5 %inner.1 = (f32[3,16,16,2,8,128]{5,4,3,2,1,0:T(8,128)S(1)}, f32[3,3,16,2,8,128]{5,4,3,2,1,0:T(8,128)S(1)}, f32[16,16,2,16,128]{4,3,2,1,0:T(8,128)S(1)}, f32[3,16,2,8,128]{4,3,2,1,0:T(8,128)S(1)}) custom-call(s32[2]{0:T(128)S(1)} %pad_add_fusion.scal.a_0_, f32[16,16,2,32,128]{4,3,2,1,0:T(8,128)S(1)} %get-tuple-element.46.a_1_, ...), custom_call_target="tpu_custom_call" | custom-call | tf_op jit(solution)/shard_map/inner/pallas_call | solution.py:726
  39.8 0.0 collective-permute-done.2.y_s.a_7_
  39.8 1.1 %collective-permute-done.3.y_n.a_8_ = f32[161,2,8,128]{3,2,1,0:T(8,128)S(1)} collective-permute-done((f32[161,2,8,128]{3,2,1,0:T(8,128)S(1)}, f32[161,2,8,128]{3,2,1,0:T(8,128)S(1)}, u32[]{:S(2)}, u32[]{:S(2)}) %collective-permute-start.3) | collective-permute-done | bytes 1318944 | tf_op jit(solution)/shard_map/ppermute | solution.py:725
  40.9 2.5 %halo_pack.1 = (f32[17,5,8,128]{3,2,1,0:T(8,128)S(1)}, f32[17,24,128]{2,1,0:T(8,128)S(1)}, f32[17,24,128]{2,1,0:T(8,128)S(1)}) custom-call(f32[161,2,8,128]{3,2,1,0:T(8,128)S(1)} %collective-permute-done.2.y_s.a_7_, f32[161,2,8,128]{3,2,1,0:T(8,128)S(1)} %collective-permute-done.3.y_n.a_8_, f32[17,16,128]{2,1,0:T(8,128)S(1)} %get-tuple-element.43.own_f.a_2_, ...), custom_call_target="tpu_custom_call" | custom-call | tf_op jit(solution)/shard_map/halo_pack/pallas_call | solution.py:738
  43.4 1.3 %collective-permute-start.4 = (f32[17,24,128]{2,1,0:T(8,128)S(1)}, f32[17,24,128]{2,1,0:T(8,128)S(1)}, u32[]{:S(2)}, u32[]{:S(2)}) collective-permute-start(f32[17,24,128]{2,1,0:T(8,128)S(1)} %get-tuple-element.59), channel_id=1, source_target_pairs={{0,4},{4,8},{8,12},{12,16},{16,20},{20,24},{24,28},{28,32},{32,36}... | collective-permute-start | bytes 626696 | tf_op jit(solution)/shard_map/ppermute | solution.py:745
  44.8 3.8 %collective-permute-start.5 = (f32[17,24,128]{2,1,0:T(8,128)S(1)}, f32[17,24,128]{2,1,0:T(8,128)S(1)}, u32[]{:S(2)}, u32[]{:S(2)}) collective-permute-start(f32[17,24,128]{2,1,0:T(8,128)S(1)} %get-tuple-element.60), channel_id=1, source_target_pairs={{4,0},{8,4},{12,8},{16,12},{20,16},{24,20},{28,24},{32,28},{36,32}... | collective-permute-start | bytes 626696 | tf_op jit(solution)/shard_map/ppermute | solution.py:746
  48.6 11.5 %edge.1 = (f32[16,16,2,16,128]{4,3,2,1,0:T(8,128)S(1)}, f32[3,16,2,8,128]{4,3,2,1,0:T(8,128)S(1)}) custom-call(s32[2]{0:T(128)S(1)} %pad_add_fusion.scal.a_0_, f32[16,16,2,8,128]{4,3,2,1,0:T(8,128)S(1)} %get-tuple-element.63.a_1_, f32[3,16,16,2,8,128]{5,4,3,2,1,0:T(8,128)S(1)} %get-tuple-element.64.a_2_, ...), custom_call_target="tpu_custom_call" | custom-call | tf_op jit(solution)/shard_map/edge/pallas_call | solution.py:747
  60.1 0.0 collective-permute-done.4.a_4_
  60.1 0.0 collective-permute-done.5.a_5_
  60.1 11.0 %strips.1 = (f32[16,16,16,256]{3,2,1,0:T(8,128)}, f32[8,16,256]{2,1,0:T(8,128)}, f32[2,8,16,256]{3,2,1,0:T(8,128)}) custom-call(s32[2]{0:T(128)S(1)} %pad_add_fusion.scal.a_0_, f32[16,4,16,128]{3,2,1,0:T(8,128)S(1)} %get-tuple-element.36.a_1_, f32[17,16,128]{2,1,0:T(8,128)S(1)} %get-tuple-element.43.own_f.a_2_, ...), custom_call_target="tpu_custom_call" | custom-call | tf_op jit(solution)/shard_map/strips/pallas_call | solution.py:761
Async XLA Ops:
  0.6 11.6 %collective-permute-start.1 = (f32[2,8,16,256]{3,2,1,0:T(8,128)}, f32[2,8,16,256]{3,2,1,0:T(8,128)S(1)}, u32[]{:S(2)}, u32[]{:S(2)}) collective-permute-start(f32[2,8,16,256]{3,2,1,0:T(8,128)} %vo.1), channel_id=1, source_target_pairs={{0,64},{64,0},{1,65},{65,1},{2,66},{66,2},{3,67},{67,3},{4,68},{68... | collective-permute-start | bytes 786440 | tf_op jit(solution)/shard_map/ppermute | solution.py:701
  3.2 9.0 %collective-permute-start = (f32[8,16,256]{2,1,0:T(8,128)}, f32[8,16,256]{2,1,0:T(8,128)S(1)}, u32[]{:S(2)}, u32[]{:S(2)}) collective-permute-start(f32[8,16,256]{2,1,0:T(8,128)} %ho.1), channel_id=1, source_target_pairs={{0,64},{64,0},{1,65},{65,1},{2,66},{66,2},{3,67},{67,3},{4,68},{68... | collective-permute-start | bytes 393224 | tf_op jit(solution)/shard_map/ppermute | solution.py:700
  3.3 2.2 %copy-start = (f32[16,16,16,256]{3,2,1,0:T(8,128)S(1)}, f32[16,16,16,256]{3,2,1,0:T(8,128)}, u32[]{:S(2)}) copy-start(f32[16,16,16,256]{3,2,1,0:T(8,128)} %tr.1) | copy-start | bytes 12582916
  5.5 0.7 copy-start.6
  6.2 6.1 %copy-start.1 = (f32[2,8,16,256]{3,2,1,0:T(8,128)S(1)}, f32[2,8,16,256]{3,2,1,0:T(8,128)}, u32[]{:S(2)}) copy-start(f32[2,8,16,256]{3,2,1,0:T(8,128)} %vo.1) | copy-start | bytes 786436
  6.2 6.1 %copy-start.2 = (f32[16,16,256]{2,1,0:T(8,128)S(1)}, f32[16,16,256]{2,1,0:T(8,128)}, u32[]{:S(2)}) copy-start(f32[16,16,256]{2,1,0:T(8,128)} %df.1) | copy-start | bytes 786436
  6.2 6.1 %copy-start.3 = (f32[8,16,256]{2,1,0:T(8,128)S(1)}, f32[8,16,256]{2,1,0:T(8,128)}, u32[]{:S(2)}) copy-start(f32[8,16,256]{2,1,0:T(8,128)} %ho.1) | copy-start | bytes 393220
  6.2 6.1 %copy-start.4 = (s32[16,256]{1,0:T(8,128)S(1)}, s32[16,256]{1,0:T(8,128)}, u32[]{:S(2)}) copy-start(s32[16,256]{1,0:T(8,128)} %land.1) | copy-start | bytes 49156
  6.2 6.1 %copy-start.5 = (s32[16,256]{1,0:T(8,128)S(1)}, s32[16,256]{1,0:T(8,128)}, u32[]{:S(2)}) copy-start(s32[16,256]{1,0:T(8,128)} %level.1) | copy-start | bytes 49156
  13.9 25.9 %collective-permute-start.2 = (f32[161,2,8,128]{3,2,1,0:T(8,128)S(1)}, f32[161,2,8,128]{3,2,1,0:T(8,128)S(1)}, u32[]{:S(2)}, u32[]{:S(2)}) collective-permute-start(f32[161,2,8,128]{3,2,1,0:T(8,128)S(1)} %get-tuple-element.44), channel_id=1, source_target_pairs={{0,1},{1,2},{2,3},{4,5},{5,6},{6,7},{8,9},{9,10},{10,11},{12,13},{... | collective-permute-start | bytes 3956744 | tf_op jit(solution)/shard_map/ppermute | solution.py:724
  20.4 20.5 %collective-permute-start.3 = (f32[161,2,8,128]{3,2,1,0:T(8,128)S(1)}, f32[161,2,8,128]{3,2,1,0:T(8,128)S(1)}, u32[]{:S(2)}, u32[]{:S(2)}) collective-permute-start(f32[161,2,8,128]{3,2,1,0:T(8,128)S(1)} %get-tuple-element.45), channel_id=1, source_target_pairs={{1,0},{2,1},{3,2},{5,4},{6,5},{7,6},{9,8},{10,9},{11,10},{13,12},{... | collective-permute-start | bytes 3956744 | tf_op jit(solution)/shard_map/ppermute | solution.py:725
  43.4 16.6 %collective-permute-start.4 = (f32[17,24,128]{2,1,0:T(8,128)S(1)}, f32[17,24,128]{2,1,0:T(8,128)S(1)}, u32[]{:S(2)}, u32[]{:S(2)}) collective-permute-start(f32[17,24,128]{2,1,0:T(8,128)S(1)} %get-tuple-element.59), channel_id=1, source_target_pairs={{0,4},{4,8},{8,12},{12,16},{16,20},{20,24},{24,28},{28,32},{32,36}... | collective-permute-start | bytes 626696 | tf_op jit(solution)/shard_map/ppermute | solution.py:745
  44.8 15.3 %collective-permute-start.5 = (f32[17,24,128]{2,1,0:T(8,128)S(1)}, f32[17,24,128]{2,1,0:T(8,128)S(1)}, u32[]{:S(2)}, u32[]{:S(2)}) collective-permute-start(f32[17,24,128]{2,1,0:T(8,128)S(1)} %get-tuple-element.60), channel_id=1, source_target_pairs={{4,0},{8,4},{12,8},{16,12},{20,16},{24,20},{28,24},{32,28},{36,32}... | collective-permute-start | bytes 626696 | tf_op jit(solution)/shard_map/ppermute | solution.py:746
